TPU v7x, 256 devices: a whole 4x4x8 slice. The times are simulated.
256 devices in a mesh: row: 16 (over z, core), col: 16 (over x, y).
Axes of the slice: x: 4, y: 4, z: 8, core: 2. Of those that a mesh axis runs over, the one named last changes fastest.
Arguments:
- queries: bfloat16 [32768, 1024], P(('row', 'col')), may hold values from -45 to 45
- keys: bfloat16 [32768, 1024], P(('row', 'col')), may hold values from -4 to 4
- values: bfloat16 [32768, 1024], P(('row', 'col')), may hold values from -6 to 6
- mid_offsets: int32 [16], replicated, may hold values from 0 to 3
- long_offsets: int32 [16], replicated, may hold values from 0 to 15
- out_weight: bfloat16 [1024, 2048], replicated, may hold values from -0.1875 to 0.1875
Outputs:
- layer_out: bfloat16 [32768, 2048], P(('row', 'col'))
All inputs are finite; a program needn't handle non-finite values.
Results may differ from a plain program's by a relative error of at most 0.01.
Values may be sent and summed in bfloat16 or wider, within the bound.
No kernel may reach another device: no remote copies, remote signals or barrier semaphores. Data moves between devices by JAX's collectives and lax.ppermute only.
A program may use at most 128 MiB of HBM per device.

v0:
```python
import jax
import jax.numpy as jnp
from jax import lax
from jax.sharding import PartitionSpec as P

R_MID = 4
R_LONG = 16


NEGATIVE = -1e30


def swapped(shard, axis, stride):
    return lax.ppermute(shard, axis, [(i, i ^ 1 << stride) for i in range(lax.axis_size(axis))])


def select_rows(source_data, dilation, offsets, head_count):
    row_count = source_data.shape[0] // dilation
    feature_width = source_data.shape[1]
    shaped = source_data.reshape(row_count, dilation, head_count, feature_width // head_count)
    picked = jnp.take_along_axis(shaped, offsets.reshape(1, 1, head_count, 1), axis=1)
    return picked.reshape(row_count, feature_width)


def attend(state_now, query_rows, query_index, key_rows, value_rows, key_index, head_count):
    running_max, running_sum, summed = state_now
    piece_rows = key_rows.shape[0]
    head_dim = key_rows.shape[1] // head_count
    key_heads = key_rows.reshape(piece_rows, head_count, head_dim)
    value_heads = value_rows.reshape(piece_rows, head_count, head_dim)
    scores = jnp.einsum(
        "qhd,khd->hqk", query_rows, key_heads, preferred_element_type=jnp.float32
    ) * head_dim ** (-0.5)
    visible = (key_index[None, :] <= query_index[:, None])[None]
    new_max = jnp.maximum(running_max, jnp.max(jnp.where(visible, scores, NEGATIVE), axis=-1))
    weights = jnp.where(visible, jnp.exp(scores - new_max[..., None]), 0.0)
    factor = jnp.exp(running_max - new_max)
    running_sum = running_sum * factor + jnp.sum(weights, axis=-1)
    summed = summed * factor[..., None] + jnp.einsum(
        "hqk,khd->hqd",
        weights.astype(jnp.bfloat16),
        value_heads,
        preferred_element_type=jnp.float32,
    )
    return (new_max, running_sum, summed)


def finalize(state_now):
    running_max, running_sum, summed = state_now
    attended = (summed / running_sum[..., None]).transpose(1, 0, 2)
    log_total = (running_max + jnp.log(running_sum)).transpose(1, 0)
    return (attended, log_total)


def spread(result_pair, dilation, offsets):
    attended, log_total = result_pair
    row_count, head_count, head_dim = attended.shape
    selected = jnp.arange(dilation)[None, :, None] == offsets[None, None, :]
    full_log = jnp.where(selected, log_total[:, None, :], NEGATIVE).reshape(
        row_count * dilation, head_count
    )
    full_out = jnp.where(selected[..., None], attended[:, None], 0.0).reshape(
        row_count * dilation, head_count, head_dim
    )
    return (full_out, full_log)


def shards(queries, keys, values, mid_offsets, long_offsets, out_weight):
    rows_here, feature_width = queries.shape
    head_count = mid_offsets.shape[0]
    head_dim = feature_width // head_count
    col_count = lax.axis_size("col")
    row_id = lax.axis_index("row")
    col_id = lax.axis_index("col")
    block_id = row_id * col_count + col_id

    def start_state(row_count):
        return (
            jnp.full((head_count, row_count), NEGATIVE, jnp.float32),
            jnp.zeros((head_count, row_count), jnp.float32),
            jnp.zeros((head_count, row_count, head_dim), jnp.float32),
        )

    short_queries = queries.reshape(rows_here, head_count, head_dim)
    short_index = block_id * rows_here + jnp.arange(rows_here, dtype=jnp.int32)
    row_total = col_count * rows_here
    key_piece = (
        lax.all_gather(keys, "col", axis=0, tiled=True),
        lax.all_gather(values, "col", axis=0, tiled=True),
    )
    state_now = start_state(rows_here)
    short_piece_rows = key_piece[0].shape[0]
    key_index = row_id * row_total + jnp.arange(short_piece_rows, dtype=jnp.int32)
    state_now = attend(
        state_now, short_queries, short_index, key_piece[0], key_piece[1], key_index, head_count
    )
    key_buffer = key_piece[0]
    value_buffer = key_piece[1]
    mid_count = rows_here // R_MID
    mid_queries = select_rows(queries, R_MID, mid_offsets, head_count).reshape(
        mid_count, head_count, head_dim
    )
    mid_index = block_id * mid_count + jnp.arange(mid_count, dtype=jnp.int32)
    held_rows = (
        select_rows(key_buffer, R_MID, mid_offsets, head_count),
        select_rows(value_buffer, R_MID, mid_offsets, head_count),
    )
    row_span = col_count * mid_count
    own_index = row_id * row_span + jnp.arange(row_span, dtype=jnp.int32)
    mid_state = attend(
        start_state(mid_count),
        mid_queries,
        mid_index,
        held_rows[0],
        held_rows[1],
        own_index,
        head_count,
    )
    for bit_number in range(2):
        partner_rows = swapped((held_rows[0], held_rows[1]), "row", bit_number)
        piece_rows = held_rows[0].shape[0]
        partner_row = jnp.left_shift(
            jnp.bitwise_xor(jnp.right_shift(row_id, bit_number), 1), bit_number
        )
        partner_index = partner_row * row_span + jnp.arange(piece_rows, dtype=jnp.int32)
        mid_state = attend(
            mid_state,
            mid_queries,
            mid_index,
            partner_rows[0],
            partner_rows[1],
            partner_index,
            head_count,
        )
        if bit_number == 0:
            lower_half = jnp.bitwise_and(jnp.right_shift(row_id, bit_number), 1) == 0
            held_rows = tuple(
                (
                    jnp.where(
                        lower_half,
                        jnp.concatenate([mine, theirs], axis=0),
                        jnp.concatenate([theirs, mine], axis=0),
                    )
                    for mine, theirs in zip(held_rows, partner_rows)
                )
            )
    long_count = rows_here // R_LONG
    long_queries = select_rows(queries, R_LONG, long_offsets, head_count).reshape(
        long_count, head_count, head_dim
    )
    long_index = block_id * long_count + jnp.arange(long_count, dtype=jnp.int32)
    long_keys = select_rows(keys, R_LONG, long_offsets, head_count)
    long_values = select_rows(values, R_LONG, long_offsets, head_count)
    key_piece = (
        lax.all_gather(long_keys, ("row", "col"), axis=0, tiled=True),
        lax.all_gather(long_values, ("row", "col"), axis=0, tiled=True),
    )
    piece_rows = key_piece[0].shape[0]
    key_index = jnp.arange(piece_rows, dtype=jnp.int32)
    long_state = attend(
        start_state(long_count),
        long_queries,
        long_index,
        key_piece[0],
        key_piece[1],
        key_index,
        head_count,
    )
    level_results = [
        finalize(state_now),
        spread(finalize(mid_state), R_MID, mid_offsets),
        spread(finalize(long_state), R_LONG, long_offsets),
    ]
    level_max = jnp.maximum(
        jnp.maximum(level_results[0][1], level_results[1][1]), level_results[2][1]
    )
    numerator = jnp.zeros((rows_here, head_count, head_dim), jnp.float32)
    denominator = jnp.zeros((rows_here, head_count), jnp.float32)
    for attended, log_total in level_results:
        weight = jnp.exp(log_total - level_max)
        numerator = numerator + weight[..., None] * attended
        denominator = denominator + weight
    combined = (
        (numerator / denominator[..., None]).astype(jnp.bfloat16).reshape(rows_here, feature_width)
    )
    return jnp.dot(combined, out_weight, preferred_element_type=jnp.float32).astype(jnp.bfloat16)


def solution(mesh):
    in_specs = (
        P(("row", "col"), None),
        P(("row", "col"), None),
        P(("row", "col"), None),
        P(),
        P(),
        P(),
    )
    out_specs = P(("row", "col"), None)
    return jax.shard_map(shards, mesh=mesh, in_specs=in_specs, out_specs=out_specs, check_vma=False)
```

profile of v0, /device:TPU:1, one launch (start us, length us, event | category | flops | bytes accessed | tf_op | source)
XLA Modules:
  0.0 412.7 jit_solution(6117466711674249232)
XLA Ops:
  8.1 1.3 reshape.499
  9.4 1.3 reshape.507
  23.4 46.8 %all-gather.9.cloned.1.call-done = bf16[2048,1024]{1,0:T(8,128)(2,1)} async-done(((bf16[128,1024]{1,0:T(8,128)(2,1)}), bf16[2048,1024]{1,0:T(8,128)(2,1)}) %all-gather.9.cloned.1.call-update) | async-done | bytes 4194320 | tf_op jit(solution)/shard_map/all_gather | solution.py:89
  70.2 11.7 %reshape.503 = bf16[512,4,16,64]{3,2,1,0:T(8,128)(2,1)} reshape(bf16[2048,1024]{1,0:T(8,128)(2,1)} %all-gather.9.cloned.1.call-done) | data formatting | bytes 8388608 | tf_op jit(solution)/shard_map/reshape | solution.py:20
  81.8 9.9 %copy.75 = bf16[512,4,16,64]{0,3,2,1:T(8,128)(2,1)} copy(bf16[512,4,16,64]{3,2,1,0:T(8,128)(2,1)} %reshape.503) | data formatting | bytes 8388608 | tf_op jit(solution)/shard_map/reshape | solution.py:20
  91.7 37.2 %all-gather.5.cloned.1.call-done = bf16[2048,1024]{1,0:T(8,128)(2,1)} async-done(((bf16[128,1024]{1,0:T(8,128)(2,1)}), bf16[2048,1024]{1,0:T(8,128)(2,1)}) %all-gather.5.cloned.1.call-update) | async-done | bytes 4194320 | tf_op jit(solution)/shard_map/all_gather | solution.py:88
  128.9 11.6 %reshape.492 = bf16[512,4,16,64]{3,2,1,0:T(8,128)(2,1)} reshape(bf16[2048,1024]{1,0:T(8,128)(2,1)} %all-gather.5.cloned.1.call-done) | data formatting | bytes 8388608 | tf_op jit(solution)/shard_map/reshape | solution.py:20
  140.5 9.8 %copy.65 = bf16[512,4,16,64]{0,3,2,1:T(8,128)(2,1)} copy(bf16[512,4,16,64]{3,2,1,0:T(8,128)(2,1)} %reshape.492) | data formatting | bytes 8388608 | tf_op jit(solution)/shard_map/reshape | solution.py:20
  150.3 2.8 gather_fusion.4
  153.2 3.8 gather_fusion.1
  157.0 1.5 bitcast_select_fusion.1
  159.5 6.6 %copy.63 = bf16[2048,1024]{0,1:T(8,128)(2,1)} copy(bf16[2048,1024]{1,0:T(8,128)(2,1)} %all-gather.5.cloned.1.call-done) | data formatting | bytes 8388608 | tf_op jit(solution)/shard_map/all_gather | solution.py:88
  166.1 4.9 %select_reduce_fusion = (f32[16,128]{1,0:T(8,128)S(1)}, f32[16,128,2048]{2,1,0:T(8,128)S(1)}) fusion(pred[128,2048]{1,0:T(8,128)(4,1)S(1)} %broadcast_compare_fusion, bf16[128,16,64]{0,2,1:T(8,128)(2,1)} %bitcast.301, bf16[2048,16,64]{0,2,1:T(8,128)(2,1)} %bitcast.290), kind=kOutput, calls=%fused_computation.7 | convolution fusion | flops 549451776 | bytes 21504000 | tf_op jit(solution)/shard_map/qhd,khd->hqk/dot_general | solution.py:31
  171.6 5.2 %copy-done = f32[16,128,2048]{2,1,0:T(8,128)} copy-done((f32[16,128,2048]{2,1,0:T(8,128)}, f32[16,128,2048]{2,1,0:T(8,128)S(1)}, u32[]{:S(2)}) %copy-start) | copy-done | bytes 16777240
  176.8 5.2 %fusion.1 = f32[16,128]{1,0:T(8,128)} fusion(f32[16,128,2048]{2,1,0:T(8,128)S(1)} %get-tuple-element.34, f32[16,128]{1,0:T(8,128)S(1)} %broadcast_maximum_fusion.2, pred[128,2048]{1,0:T(8,128)(4,1)S(1)} %broadcast_compare_fusion), kind=kLoop, calls=%fused_computation.9 | loop fusion | flops 16775168 | bytes 17055744 | tf_op jit(solution)/shard_map/reduce_sum | solution.py:38
  182.0 6.5 %copy.73 = bf16[2048,1024]{0,1:T(8,128)(2,1)} copy(bf16[2048,1024]{1,0:T(8,128)(2,1)} %all-gather.9.cloned.1.call-done) | data formatting | bytes 8388608 | tf_op jit(solution)/shard_map/all_gather | solution.py:89
  188.5 2.0 maximum_select_fusion
  190.5 1.3 collective-permute-start.1
  192.8 55.6 %all-gather.7.cloned.1.call-done = bf16[2048,1024]{1,0:T(8,128)(2,1)} async-done(((bf16[8,1024]{1,0:T(8,128)(2,1)}), bf16[2048,1024]{1,0:T(8,128)(2,1)}) %all-gather.7.cloned.1.call-update) | async-done | bytes 4194320 | tf_op jit(solution)/shard_map/all_gather | solution.py:155
  248.3 6.5 %copy.72 = bf16[2048,1024]{0,1:T(8,128)(2,1)} copy(bf16[2048,1024]{1,0:T(8,128)(2,1)} %all-gather.7.cloned.1.call-done) | data formatting | bytes 8388608 | tf_op jit(solution)/shard_map/all_gather | solution.py:155
  254.8 3.8 maximum_select_fusion.1
  258.6 2.2 select_reduce_fusion.2
  260.8 103.6 %all-gather.11.cloned.1.call-done = bf16[2048,1024]{1,0:T(8,128)(2,1)} async-done(((bf16[8,1024]{1,0:T(8,128)(2,1)}), bf16[2048,1024]{1,0:T(8,128)(2,1)}) %all-gather.11.cloned.1.call-update) | async-done | bytes 4194320 | tf_op jit(solution)/shard_map/all_gather | solution.py:156
  364.4 6.5 %copy.80 = bf16[2048,1024]{0,1:T(8,128)(2,1)} copy(bf16[2048,1024]{1,0:T(8,128)(2,1)} %all-gather.11.cloned.1.call-done) | data formatting | bytes 8388608 | tf_op jit(solution)/shard_map/all_gather | solution.py:156
  373.4 3.4 fusion.20
  379.2 1.2 copy.82
  380.4 1.7 select_reduce_fusion.3
  382.1 2.3 select_reduce_fusion.1
  385.1 2.4 convolution_bitcast_fusion
  388.7 1.8 fusion.16
  391.4 11.0 %fusion.43 = bf16[128,16,64]{0,2,1:T(8,128)(2,1)S(1)} fusion(bf16[2048,16,64]{0,2,1:T(8,128)(2,1)} %bitcast.299, f32[16,128,2048]{2,1,0:T(8,128)} %copy-done, f32[16,128]{1,0:T(8,128)S(1)} %copy-done.11, pred[128,2048]{1,0:T(8,128)(4,1)S(1)} %broadcast_compare_fusion, f32[128,16,64]{0,2,1:T(8,128)S(1)} %copy-done.4, f32[128,16,64]{0,2,1:T(8,128)S(1)} %copy.77, ...), kind=kOutput, calls=%fused_computation.55 | convolution fusion | flops 555089920 | bytes 22605824 | tf_op jit(solution)/shard_map/hqk,khd->hqd/dot_general | solution.py:39
  402.4 3.7 convolution_convert_fusion
  (120 shorter events, 24.0 us)
Async XLA Ops:
  6.5 4.9 %copy-start.20 = (s32[16]{0:T(128)S(1)}, s32[16]{0:T(128)}, u32[]{:S(2)}) copy-start(s32[16]{0:T(128)} %param.13) | copy-start | bytes 196
  6.5 4.9 %copy-start.19 = (s32[16]{0:T(128)S(1)}, s32[16]{0:T(128)}, u32[]{:S(2)}) copy-start(s32[16]{0:T(128)} %param.14) | copy-start | bytes 196
  6.5 7.8 %copy-start.3 = (bf16[128,1024]{1,0:T(8,128)(2,1)S(1)}, bf16[128,1024]{1,0:T(8,128)(2,1)}, u32[]{:S(2)}) copy-start(bf16[128,1024]{1,0:T(8,128)(2,1)} %param.10) | copy-start | bytes 786436
  6.5 63.6 %all-gather.9.cloned.1.call-start = ((), (), s32[]{:S(2)}) async-start(), calls=%async_computation.2 | async-start | bytes 4456448 | tf_op jit(solution)/shard_map/all_gather | solution.py:89
  7.3 121.7 %all-gather.5.cloned.1.call-start = ((), (), s32[]{:S(2)}) async-start(), calls=%async_computation | async-start | bytes 4456448 | tf_op jit(solution)/shard_map/all_gather | solution.py:88
  8.0 240.3 %all-gather.7.cloned.1.call-start = ((), (), s32[]{:S(2)}) async-start(), calls=%async_computation.1 | async-start | bytes 4210688 | tf_op jit(solution)/shard_map/all_gather | solution.py:155
  12.7 2.5 copy-start.17
  13.6 350.9 %all-gather.11.cloned.1.call-start = ((), (), s32[]{:S(2)}) async-start(), calls=%async_computation.3 | async-start | bytes 4210688 | tf_op jit(solution)/shard_map/all_gather | solution.py:156
  158.4 96.4 %collective-permute-start.2 = (bf16[512,1024]{0,1:T(8,128)(2,1)S(1)}, bf16[512,1024]{0,1:T(8,128)(2,1)}, u32[]{:S(2)}, u32[]{:S(2)}) collective-permute-start(bf16[512,1024]{0,1:T(8,128)(2,1)S(1)} %bitcast.293), channel_id=1, source_target_pairs={{0,16},{16,0},{32,48},{48,32},{64,80},{80,64},{96,112},{112,96},{1... | collective-permute-start | bytes 3145736 | tf_op jit(solution)/shard_map/ppermute | solution.py:14
  159.2 29.3 %collective-permute-start = (bf16[512,1024]{0,1:T(8,128)(2,1)S(1)}, bf16[512,1024]{0,1:T(8,128)(2,1)S(1)}, u32[]{:S(2)}, u32[]{:S(2)}) collective-permute-start(bf16[512,1024]{0,1:T(8,128)(2,1)S(1)} %bitcast.295), channel_id=1, source_target_pairs={{0,16},{16,0},{32,48},{48,32},{64,80},{80,64},{96,112},{112,96},{1... | collective-permute-start | bytes 3145736 | tf_op jit(solution)/shard_map/ppermute | solution.py:14
  171.0 0.6 copy-start.7
  171.0 5.8 %copy-start = (f32[16,128,2048]{2,1,0:T(8,128)}, f32[16,128,2048]{2,1,0:T(8,128)S(1)}, u32[]{:S(2)}) copy-start(f32[16,128,2048]{2,1,0:T(8,128)S(1)} %get-tuple-element.34) | copy-start | bytes 50331652
  171.6 5.2 %copy-start.10 = (f32[16,128]{1,0:T(8,128)}, f32[16,128]{1,0:T(8,128)S(1)}, u32[]{:S(2)}) copy-start(f32[16,128]{1,0:T(8,128)S(1)} %broadcast_maximum_fusion.2) | copy-start | bytes 24580
  188.5 3.2 copy-start.16
  188.5 3.2 copy-start.2
  190.5 191.6 %collective-permute-start.1 = (bf16[1024,1024]{0,1:T(8,128)(2,1)}, bf16[1024,1024]{0,1:T(8,128)(2,1)}, u32[]{:S(2)}, u32[]{:S(2)}) collective-permute-start(bf16[1024,1024]{0,1:T(8,128)(2,1)} %maximum_select_fusion), channel_id=1, source_target_pairs={{0,32},{16,48},{32,0},{48,16},{64,96},{80,112},{96,64},{112,80},{1... | collective-permute-start | bytes 6291464 | tf_op jit(solution)/shard_map/ppermute | solution.py:14
  254.8 3.8 copy-start.1
  254.8 3.8 copy-start.18
  258.6 126.4 %collective-permute-start.3 = (bf16[1024,1024]{0,1:T(8,128)(2,1)}, bf16[1024,1024]{0,1:T(8,128)(2,1)}, u32[]{:S(2)}, u32[]{:S(2)}) collective-permute-start(bf16[1024,1024]{0,1:T(8,128)(2,1)} %maximum_select_fusion.1), channel_id=1, source_target_pairs={{0,32},{16,48},{32,0},{48,16},{64,96},{80,112},{96,64},{112,80},{1... | collective-permute-start | bytes 6291464 | tf_op jit(solution)/shard_map/ppermute | solution.py:14
  380.4 4.0 copy-start.9
  380.4 4.1 copy-start.5
  384.4 3.0 copy-start.6
  388.2 3.1 copy-start.8
  388.2 3.1 copy-start.12
  388.2 3.1 copy-start.13
  388.2 3.1 copy-start.14
  388.2 3.1 copy-start.15
  388.2 3.2 copy-start.11
  388.7 2.7 copy-start.4
Sparse Core Ops, SparseCore 0:
  9.8 60.3 all-gather.8
  72.6 56.2 all-gather.4
  132.5 115.7 all-gather.6
  251.8 112.5 all-gather.10
where the time goes:
time: 415 us; the launch traced here: 413 us
  waiting for transfers between devices  245 us (59%)
  local copies, waits for them, and re-layouts  97.2 us (23%)
  matrix products  34.9 us (8%)
  other arithmetic  19.8 us (5%)
  between operations  13.7 us (3%)
    all_gather x1, waiting for transfers between devices, shards(): lax.all_gather(long_values, ('row', 'col'), axis=0, tiled=True)  104 us
    all_gather x1, waiting for transfers between devices, shards(): lax.all_gather(long_keys, ('row', 'col'), axis=0, tiled=True)  55.6 us
    reshape x12, local copies, waits for them, and re-layouts, select_rows(): source_data.reshape(row_count, dilation, head_count, feature_width // hea...  47.6 us
    all_gather x1, waiting for transfers between devices, shards(): lax.all_gather(values, 'col', axis=0, tiled=True)  46.8 us
    all_gather x1, waiting for transfers between devices, shards(): lax.all_gather(keys, 'col', axis=0, tiled=True)  37.2 us
    dot_general x5, matrix products, attend(): jnp.einsum('hqk,khd->hqd', weights.astype(jnp.bfloat16), value_heads, pre...  19 us
    dot_general x5, matrix products, attend(): jnp.einsum('qhd,khd->hqk', query_rows, key_heads, preferred_element_type=...  12.1 us
    gather x6, local copies, waits for them, and re-layouts, select_rows(): jnp.take_along_axis(shaped, offsets.reshape(1, 1, head_count, 1), axis=1)  9.63 us
  transfers between devices with their start and end apart: 8, of which 4 were waited for; matrix products, arithmetic and copies ran while one was open for 30% of the time, Pallas kernels for 0%

commit v1 on v0

v1 whole, which is shorter than its diff:
```python
import functools

import jax
import jax.numpy as jnp
from jax import lax
from jax.experimental import pallas as pl
from jax.experimental.pallas import tpu as pltpu
from jax.sharding import PartitionSpec as P

R_MID = 4
R_LONG = 16
HEADS = 16
HD = 64
LANES = 128
BLOCK = 128
SEG = 2048
HALF = BLOCK // 2
PACKED = BLOCK + HALF
NOTE = 16
ROWS = 16
MID_ROWS = 4
N_MID = SEG // R_MID
N_LONG = SEG // R_LONG
NEGATIVE = -1e30
SCALE = 0.125 * 1.4426950408889634
VMEM_LIMIT = 20 * 1024 * 1024
VMEM_MOST = 60 * 1024 * 1024

VM = pl.BlockSpec(memory_space=pltpu.VMEM)
HB = pl.BlockSpec(memory_space=pl.ANY)
DMA = pltpu.SemaphoreType.DMA


def call(
    kernel, out_shape, in_specs, scratch=(), flops=0, moved=0, exps=0, out_specs=None, aliases=None, limit=VMEM_LIMIT
):
    return pl.pallas_call(
        kernel,
        out_shape=out_shape,
        in_specs=in_specs,
        out_specs=jax.tree.map(lambda _: VM, out_shape) if out_specs is None else out_specs,
        scratch_shapes=list(scratch),
        input_output_aliases=aliases or {},
        compiler_params=pltpu.CompilerParams(vmem_limit_bytes=limit),
        cost_estimate=pl.CostEstimate(flops=flops, bytes_accessed=moved, transcendentals=exps),
    )


def shape(*dims, dtype=jnp.bfloat16):
    return jax.ShapeDtypeStruct(dims, dtype)


def low_lanes(rows):
    return lax.broadcasted_iota(jnp.int32, (rows, LANES), 1) < HD


def fetch(pairs, sems):
    copies = [pltpu.make_async_copy(src, dst, sems.at[i]) for i, (src, dst) in enumerate(pairs)]
    for copy in copies:
        copy.start()
    return copies


def pack_kernel(
    mid_hbm, long_hbm, q_hbm, k_hbm, v_hbm, out_hbm,
    mid_ref, long_ref, q_ref, k_ref, v_ref, out_ref, at_sems, in_sems, out_sems,
):
    notes = fetch([(mid_hbm, mid_ref), (long_hbm, long_ref)], at_sems)
    chunks = in_sems.shape[0]
    heads = HEADS // chunks
    loads, stores = [], []
    for i in range(chunks):
        cols = pl.ds(i * heads * HD, heads * HD)
        pairs = [(src.at[:, cols], dst.at[:, cols]) for src, dst in ((k_hbm, k_ref), (v_hbm, v_ref), (q_hbm, q_ref))]
        loads.append(fetch(pairs, in_sems.at[i]))
    for copy in notes:
        copy.wait()
    for i in range(chunks):
        for copy in loads[i]:
            copy.wait()
        for head in range(i * heads, i * heads + heads):
            cols = pl.ds(head // 2 * LANES, LANES)
            lanes = slice(head % 2 * HD, head % 2 * HD + HD)
            q = q_ref[:, cols][:, lanes]
            out_ref[head, :BLOCK] = jnp.concatenate([k_ref[:, cols][:, lanes], v_ref[:, cols][:, lanes]], axis=1)
            out_ref[head, BLOCK:PACKED] = jnp.concatenate([q[:HALF], q[HALF:]], axis=1)
            note = jnp.where(low_lanes(NOTE), mid_ref[head].astype(jnp.float32), long_ref[head].astype(jnp.float32))
            out_ref[head, PACKED:] = note.astype(jnp.bfloat16)
        done = pl.ds(i * heads, heads)
        stores.append(pltpu.make_async_copy(out_ref.at[done], out_hbm.at[done], out_sems.at[i]))
        stores[-1].start()
    for copy in stores:
        copy.wait()


def select_kernel(got_ref, kvm_ref, far_ref, qm_ref, ql_ref, at_ref, wide):
    for src in range(HEADS):
        wide[0, pl.ds(src * BLOCK, BLOCK), :] = got_ref[src, :BLOCK].astype(jnp.float32)
        packed = got_ref[src, BLOCK:PACKED].astype(jnp.float32)
        wide[1, pl.ds(src * BLOCK, HALF), :] = packed
        wide[1, pl.ds(src * BLOCK + HALF, HALF), :] = pltpu.roll(packed, HD, 1)
    at_ref[...] = got_ref[0, PACKED:].astype(jnp.float32)
    o_mid, o_long = own_offsets(at_ref)
    kvm_ref[...] = wide[0, pl.ds(o_mid, N_MID, stride=R_MID), :].astype(jnp.bfloat16)
    far = wide[0, pl.ds(o_long, N_LONG, stride=R_LONG), :].astype(jnp.bfloat16)
    for z in range(ROWS // 2):
        far_ref[z] = far
    q = wide[1, pl.ds(o_mid, N_MID, stride=R_MID), :]
    qm_ref[...] = jnp.where(low_lanes(N_MID), q, 0.0).astype(jnp.bfloat16)
    q = wide[1, pl.ds(o_long, N_LONG, stride=R_LONG), :]
    ql_ref[...] = jnp.where(low_lanes(N_LONG), q, 0.0).astype(jnp.bfloat16)


def own_offsets(at_ref):
    lane = lax.broadcasted_iota(jnp.int32, at_ref.shape, 1)
    at = at_ref[...].astype(jnp.int32)
    return [jnp.max(jnp.where(lane == where, at, 0)) for where in (0, LANES - 1)]


def scores_of(q, kv):
    return lax.dot_general(q, kv, (((1,), (1,)), ((), ())), preferred_element_type=jnp.float32)


def with_ones(kv):
    return jnp.where(low_lanes(kv.shape[0]), jnp.ones_like(kv), kv)


def soft(s, kv1):
    top = jnp.max(s, axis=1, keepdims=True)
    w = jnp.exp2((s - top) * SCALE).astype(jnp.bfloat16)
    return top, jnp.dot(w, kv1, preferred_element_type=jnp.float32)


def state_of(top, acc):
    lane = lax.broadcasted_iota(jnp.int32, acc.shape, 1)
    return jnp.where((lane >= HD // 2) & (lane < HD), top, acc)


def merge(state, rows, new_top, new_acc):
    old = state[rows, :]
    old_top = old[:, HD // 2 : HD // 2 + 1]
    best = jnp.maximum(old_top, new_top)
    acc = old * jnp.exp2((old_top - best) * SCALE) + new_acc * jnp.exp2((new_top - best) * SCALE)
    state[rows, :] = state_of(best, acc)


def causal(rows, cols, first):
    at = lax.broadcasted_iota(jnp.int32, (rows, cols), 0) + first
    return lax.broadcasted_iota(jnp.int32, (rows, cols), 1) <= at


def short_kernel(at_ref, got_ref, kvm, far_ref, qm_ref, ql_ref, state, kv_buf, one_buf):
    for src in range(HEADS):
        rows = pl.ds(src * BLOCK, BLOCK)
        kv = got_ref[src, :BLOCK]
        kv_buf[rows, :] = kv
        one_buf[rows, :] = with_ones(kv)
    step = 2 * BLOCK
    visible = causal(step, step, 0)
    low = low_lanes(HALF)
    zero = jnp.zeros((HALF, LANES), jnp.bfloat16)
    for i in range(SEG // step):
        parts = []
        for src in (2 * i, 2 * i + 1):
            packed = got_ref[src, BLOCK:PACKED]
            parts.append(jnp.where(low, packed, zero))
            parts.append(jnp.where(low, jnp.concatenate([packed[:, HD:], packed[:, :HD]], axis=1), zero))
        q = jnp.concatenate(parts, axis=0)
        rows = pl.ds(i * step, step)
        n = (i + 1) * step
        s = scores_of(q, kv_buf[rows, :])
        s = jnp.where(visible, s, NEGATIVE)
        if i:
            s = jnp.concatenate([scores_of(q, kv_buf[pl.ds(0, i * step), :]), s], axis=1)
        state[rows, :] = state_of(*soft(s, one_buf[pl.ds(0, n), :]))
    o_mid, o_long = own_offsets(at_ref)
    for i in range(N_MID // step):
        n = (i + 1) * step
        s = scores_of(qm_ref[pl.ds(i * step, step), :], kvm[:n])
        top, acc = soft(jnp.where(causal(step, n, i * step), s, NEGATIVE), with_ones(kvm[:n]))
        merge(state, pl.ds(o_mid + i * step * R_MID, step, stride=R_MID), top, acc)
    far = far_ref[0]
    s = scores_of(ql_ref[...], far)
    top, acc = soft(jnp.where(causal(N_LONG, N_LONG, 0), s, NEGATIVE), with_ones(far))
    merge(state, pl.ds(o_long, N_LONG, stride=R_LONG), top, acc)


def last_kernel(at_ref, state_in, qm, m1, m2, m3, ql, same, other, w_hbm, out_ref, state, w_ref, w_sem):
    load = pltpu.make_async_copy(w_hbm, w_ref, w_sem)
    load.start()
    o_mid, o_long = own_offsets(at_ref)
    row = lax.axis_index("row")
    pos = lax.rem(row, MID_ROWS)
    step = 256
    for i in range(N_MID // step):
        q = qm[pl.ds(i * step, step), :]
        pieces, ones = [], []
        for d, ref in ((1, m1), (2, m2), (3, m3)):
            before = jnp.bitwise_xor(pos, d) < pos
            pieces.append(scores_of(q, ref[...]) + jnp.where(before, 0.0, NEGATIVE))
            ones.append(with_ones(ref[...]))
        top, new = soft(jnp.concatenate(pieces, axis=1), jnp.concatenate(ones, axis=0))
        merge(state, pl.ds(o_mid + i * step * R_MID, step, stride=R_MID), top, new)
    q = ql[...]
    pieces, ones = [], []
    core = lax.rem(row, 2)
    half = (ROWS // 2) * N_LONG
    for ref, its_core in ((same, core), (other, 1 - core)):
        every = ref[...].reshape(half, LANES)
        s = scores_of(q, every)
        before = lax.broadcasted_iota(jnp.int32, s.shape, 1) < ((row + 1 - its_core) // 2) * N_LONG
        pieces.append(jnp.where(before, s, NEGATIVE))
        ones.append(with_ones(every))
    top, new = soft(jnp.concatenate(pieces, axis=1), jnp.concatenate(ones, axis=0))
    merge(state, pl.ds(o_long, N_LONG, stride=R_LONG), top, new)
    low = low_lanes(HALF)
    for src in range(HEADS):
        done = []
        for half in range(2):
            a = state[pl.ds(src * BLOCK + half * HALF, HALF), :]
            done.append(a / a[:, :1])
        out_ref[src] = jnp.where(low, pltpu.roll(done[0], HD, 1), done[1]).astype(jnp.bfloat16)
    load.wait()


def project_kernel(got_ref, w_ref, out_hbm, combined, tiles, sems):
    count, _, tile = tiles.shape
    for pair in range(HEADS // 2):
        a, b = got_ref[2 * pair], got_ref[2 * pair + 1]
        cols = pl.ds(pair * LANES, LANES)
        combined[:HALF, cols] = jnp.concatenate([a[:, :HD], b[:, :HD]], axis=1)
        combined[HALF:, cols] = jnp.concatenate([a[:, HD:], b[:, HD:]], axis=1)
    rows = combined[...]
    copies = []
    for i in range(count):
        cols = pl.ds(i * tile, tile)
        tiles[i] = jnp.dot(rows, w_ref[:, cols], preferred_element_type=jnp.float32).astype(jnp.bfloat16)
        copies.append(pltpu.make_async_copy(tiles.at[i], out_hbm.at[:, cols], sems.at[i]))
        copies[-1].start()
    for copy in copies:
        copy.wait()


def xor_rows(x, d):
    return lax.ppermute(x, "row", [(i, i ^ d) for i in range(ROWS)])


CORES = [[2 * z + c for z in range(ROWS // 2)] for c in range(2)]
bar = lax.optimization_barrier


def shards(queries, keys, values, mid_offsets, long_offsets, out_weight):
    f32, s32, bf16 = jnp.float32, jnp.int32, jnp.bfloat16
    width = queries.shape[1]
    depth, wide_out = out_weight.shape
    chunks = 4
    sent = call(
        pack_kernel,
        shape(HEADS, PACKED + NOTE, LANES),
        [HB] * 5,
        scratch=[pltpu.SMEM((HEADS,), s32)] * 2
        + [pltpu.VMEM((BLOCK, width), bf16)] * 3
        + [pltpu.VMEM((HEADS, PACKED + NOTE, LANES), bf16), DMA((2,)), DMA((chunks, 3)), DMA((chunks,))],
        moved=1 << 20,
        out_specs=HB,
        limit=VMEM_MOST,
    )(mid_offsets, long_offsets, queries, keys, values)
    got = lax.all_to_all(sent, "col", 0, 0)
    kv_mid, far, q_mid, q_long, at = call(
        select_kernel,
        (
            shape(N_MID, LANES),
            shape(ROWS // 2, N_LONG, LANES),
            shape(N_MID, LANES),
            shape(N_LONG, LANES),
            shape(NOTE, LANES, dtype=f32),
        ),
        [VM],
        scratch=[pltpu.VMEM((2, SEG, LANES), f32)],
        moved=1 << 20,
    )(got)
    m1 = xor_rows(kv_mid, 1)
    m2 = xor_rows(kv_mid, 2)
    same = lax.all_to_all(far, "row", 0, 0, axis_index_groups=CORES)
    state = call(
        short_kernel,
        shape(SEG, LANES, dtype=f32),
        [VM] * 6,
        scratch=[pltpu.VMEM((SEG, LANES), bf16)] * 2,
        flops=4 * SEG * SEG * LANES,
        moved=3 << 20,
        exps=SEG * SEG // 2,
    )(at, got, kv_mid, far, q_mid, q_long)
    same, m2, state = bar((same, m2, state))
    m3 = xor_rows(m2, 1)
    other = xor_rows(same, 1)
    back, _, weight = call(
        last_kernel,
        (shape(HEADS, HALF, LANES), shape(SEG, LANES, dtype=f32), shape(depth, wide_out)),
        [VM] * 9 + [HB],
        scratch=[DMA],
        flops=4 * N_MID * SEG * LANES,
        moved=4 << 20,
        exps=N_MID * SEG,
        aliases={1: 1},
    )(at, state, q_mid, m1, m2, m3, q_long, same, other, out_weight)
    tile = 512
    count = wide_out // tile
    return call(
        project_kernel,
        shape(BLOCK, wide_out),
        [VM, VM],
        scratch=[
            pltpu.VMEM((BLOCK, depth), jnp.bfloat16),
            pltpu.VMEM((count, BLOCK, tile), jnp.bfloat16),
            DMA((count,)),
        ],
        flops=2 * BLOCK * depth * wide_out,
        moved=2 * depth * wide_out,
        out_specs=HB,
    )(lax.all_to_all(back, "col", 0, 0), weight)


def solution(mesh):
    split = P(("row", "col"), None)
    return jax.shard_map(
        shards,
        mesh=mesh,
        in_specs=(split, split, split, P(), P(), P()),
        out_specs=split,
        check_vma=False,
    )
```

time: 415 us -> 66.3 us (0.16)
  waiting for transfers between devices: 245 us -> 2.75 us
  local copies, waits for them, and re-layouts: 97.2 us -> 2.19 us
  matrix products: 34.9 us -> 0 us
  blocking collectives: 0 us -> 32.2 us
  other arithmetic: 19.8 us -> 0 us
  Pallas kernels: 0 us -> 13.9 us
  between operations: 13.7 us -> 0.03 us
  starting transfers between devices: 2.44 us -> 14.8 us
    all_gather x4 -> x0, waiting for transfers between devices: 243 us -> none  [the longest x1 104 us: shards(): lax.all_gather(long_values, ('row', 'col'), axis=0, tiled=True)]
    reshape x14 -> x0, local copies, waits for them, and re-layouts: 49.1 us -> none  [the longest x12 47.6 us: select_rows(): source_data.reshape(row_count, dilation, head_count, feature_width // hea...]
    dot_general x11 -> x0, matrix products: 34.9 us -> none  [the longest x5 19 us: attend(): jnp.einsum('hqk,khd->hqd', weights.astype(jnp.bfloat16), value_heads, pre...]
    all_to_all x0 -> x2, blocking collectives: none -> 32.2 us  [the longest x1 21.5 us: shards(): got = lax.all_to_all(sent, 'col', 0, 0)]
    all_gather x4 -> x0, local copies, waits for them, and re-layouts: 26.1 us -> none  [the longest x1 6.57 us: shards(): lax.all_gather(keys, 'col', axis=0, tiled=True)]
    pallas_call x0 -> x5, Pallas kernels: none -> 13.9 us  [the longest x1 6.35 us: shards(): call(short_kernel, shape(SEG, LANES, dtype=f32), [VM] * 6, scratch=[pltpu...]
    gather x6 -> x0, local copies, waits for them, and re-layouts: 9.63 us -> none  [select_rows(): jnp.take_along_axis(shaped, offsets.reshape(1, 1, head_count, 1), axis=1)]
    all_to_all x0 -> x1, starting transfers between devices: none -> 8.19 us  [shards(): same = lax.all_to_all(far, 'row', 0, 0, axis_index_groups=CORES)]
  transfers between devices with their start and end apart: 8 -> 5, of which waited for: 4 -> 4; matrix products, arithmetic and copies ran while one was open for 30% -> 0% of each run, Pallas kernels for 0% -> 10%
where the time goes in v1:
time: 66.3 us; the launch traced here: 65.8 us
  blocking collectives  32.2 us (49%)
  starting transfers between devices  14.8 us (22%)
  Pallas kernels  13.9 us (21%)
  waiting for transfers between devices  2.75 us (4%)
  local copies, waits for them, and re-layouts  2.19 us (3%)
    all_to_all x1, blocking collectives, shards(): got = lax.all_to_all(sent, 'col', 0, 0)  21.5 us
    all_to_all x1, blocking collectives, shards(): lax.all_to_all(back, 'col', 0, 0)  10.8 us
    all_to_all x1, starting transfers between devices, shards(): same = lax.all_to_all(far, 'row', 0, 0, axis_index_groups=CORES)  8.19 us
    ppermute x4, starting transfers between devices, xor_rows(): return lax.ppermute(x, 'row', [(i, i ^ d) for i in range(ROWS)])  6.57 us
    pallas_call x1, Pallas kernels, shards(): call(short_kernel, shape(SEG, LANES, dtype=f32), [VM] * 6, scratch=[pltpu...  6.35 us
    pallas_call x1, Pallas kernels, shards(): call(last_kernel, (shape(HEADS, HALF, LANES), shape(SEG, LANES, dtype=f32...  2.75 us
    pallas_call x1, Pallas kernels, shards(): call(pack_kernel, shape(HEADS, PACKED + NOTE, LANES), [HB] * 5, scratch=[...  2.23 us
    unnamed x2, local copies, waits for them, and re-layouts  2.19 us
  transfers between devices with their start and end apart: 5, of which 4 were waited for; matrix products, arithmetic and copies ran while one was open for 0% of the time, Pallas kernels for 10%

profile of v1, /device:TPU:1, one launch (start us, length us, event | category | flops | bytes accessed | tf_op | source)
XLA Modules:
  0.0 65.8 jit_solution(2874037860512560471)
XLA Ops:
  0.0 2.2 %shard_map.64 = bf16[16,208,128]{2,1,0:T(8,128)(2,1)} custom-call(s32[16]{0:T(128)} %mid_hbm.1, s32[16]{0:T(128)} %long_hbm.1, bf16[128,1024]{1,0:T(8,128)(2,1)} %q_hbm.1, bf16[128,1024]{1,0:T(8,128)(2,1)} %k_hbm.1, bf16[128,1024]{1,0:T(8,128)(2,1)} %v_hbm.1), custom_call_target="tpu_custom_call" | custom-call | bytes 1048576 | tf_op jit(solution)/shard_map/pallas_call | solution.py:257
  2.2 21.5 %all_to_all.15.got_ref = bf16[16,208,128]{2,1,0:T(8,128)(2,1)S(1)} all-to-all(bf16[16,208,128]{2,1,0:T(8,128)(2,1)} %shard_map.64), channel_id=1, replica_groups=mesh['row'=16,'col'=16] {'col'}, dimensions={0} | all-to-all | bytes 1703936 | tf_op jit(solution)/shard_map/all_to_all | solution.py:268
  23.7 1.1 %shard_map.65 = (bf16[512,128]{1,0:T(8,128)(2,1)S(1)}, bf16[8,128,128]{2,1,0:T(8,128)(2,1)}, bf16[512,128]{1,0:T(8,128)(2,1)S(1)}, bf16[128,128]{1,0:T(8,128)(2,1)S(1)}, f32[16,128]{1,0:T(8,128)S(1)}) custom-call(bf16[16,208,128]{2,1,0:T(8,128)(2,1)S(1)} %all_to_all.15.got_ref), custom_call_target="tpu_custom_call" | custom-call | bytes 1048576 | tf_op jit(solution)/shard_map/pallas_call | solution.py:269
  24.8 8.2 %all-to-all-start.1 = ((bf16[8,128,128]{2,1,0:T(8,128)(2,1)}), bf16[8,128,128]{2,1,0:T(8,128)(2,1)S(1)}, u32[]{:S(2)}, u32[]{:S(2)}) async-start(bf16[8,128,128]{2,1,0:T(8,128)(2,1)} %get-tuple-element.16.far_ref), calls=%async_computation.1 | async-start | bytes 524288 | tf_op jit(solution)/shard_map/all_to_all | solution.py:284
  33.0 1.5 %collective-permute-start = (bf16[512,128]{1,0:T(8,128)(2,1)S(1)}, bf16[512,128]{1,0:T(8,128)(2,1)S(1)}, u32[]{:S(2)}, u32[]{:S(2)}) collective-permute-start(bf16[512,128]{1,0:T(8,128)(2,1)S(1)} %get-tuple-element.17.kvm), channel_id=1, source_target_pairs={{0,32},{16,48},{32,0},{48,16},{64,96},{80,112},{96,64},{112,80},{1... | collective-permute-start | bytes 393224 | tf_op jit(solution)/shard_map/ppermute | solution.py:245
  34.4 6.3 %shard_map.66.state_in = f32[2048,128]{1,0:T(8,128)S(1)} custom-call(f32[16,128]{1,0:T(8,128)S(1)} %get-tuple-element.15.at_ref, bf16[16,208,128]{2,1,0:T(8,128)(2,1)S(1)} %all_to_all.15.got_ref, bf16[512,128]{1,0:T(8,128)(2,1)S(1)} %get-tuple-element.17.kvm, bf16[8,128,128]{2,1,0:T(8,128)(2,1)} %get-tuple-element.16.far_ref, ...), custom_call_target="tpu_custom_call" | custom-call | flops 2147483648 | bytes 3145728 | tf_op jit(solution)/shard_map/pallas_call | solution.py:285
  40.8 0.9 %collective-permute-done.m2 = bf16[512,128]{1,0:T(8,128)(2,1)S(1)} collective-permute-done((bf16[512,128]{1,0:T(8,128)(2,1)S(1)}, bf16[512,128]{1,0:T(8,128)(2,1)S(1)}, u32[]{:S(2)}, u32[]{:S(2)}) %collective-permute-start) | collective-permute-done | bytes 131104 | tf_op jit(solution)/shard_map/ppermute | solution.py:245
  41.7 0.9 %all-to-all-done.1.same = bf16[8,128,128]{2,1,0:T(8,128)(2,1)S(1)} async-done(((bf16[8,128,128]{2,1,0:T(8,128)(2,1)}), bf16[8,128,128]{2,1,0:T(8,128)(2,1)S(1)}, u32[]{:S(2)}, u32[]{:S(2)}) %all-to-all-start.1) | async-done | bytes 262176 | tf_op jit(solution)/shard_map/all_to_all | solution.py:284
  42.5 4.6 %collective-permute-start.3 = (bf16[8,128,128]{2,1,0:T(8,128)(2,1)S(1)}, bf16[8,128,128]{2,1,0:T(8,128)(2,1)S(1)}, u32[]{:S(2)}, u32[]{:S(2)}) collective-permute-start(bf16[8,128,128]{2,1,0:T(8,128)(2,1)S(1)} %all-to-all-done.1.same), channel_id=1, source_target_pairs={{0,16},{16,0},{32,48},{48,32},{64,80},{80,64},{96,112},{112,96},{1... | collective-permute-start | bytes 786440 | tf_op jit(solution)/shard_map/ppermute | solution.py:245
  47.1 0.0 collective-permute-start.1
  47.1 0.5 collective-permute-start.2
  47.6 0.8 %collective-permute-done.1.m1 = bf16[512,128]{1,0:T(8,128)(2,1)S(1)} collective-permute-done((bf16[512,128]{1,0:T(8,128)(2,1)S(1)}, bf16[512,128]{1,0:T(8,128)(2,1)S(1)}, u32[]{:S(2)}, u32[]{:S(2)}) %collective-permute-start.1) | collective-permute-done | bytes 131104 | tf_op jit(solution)/shard_map/ppermute | solution.py:245
  48.5 0.2 collective-permute-done.2.m3
  48.7 0.0 collective-permute-done.3.other
  48.7 0.0 copy-start
  48.7 2.2 %copy-done = bf16[1024,2048]{1,0:T(8,128)(2,1)S(1)} copy-done((bf16[1024,2048]{1,0:T(8,128)(2,1)S(1)}, bf16[1024,2048]{1,0:T(8,128)(2,1)}, u32[]{:S(2)}) %copy-start) | copy-done | bytes 4194328
  50.9 2.8 %shard_map.67 = (bf16[16,64,128]{2,1,0:T(8,128)(2,1)S(1)}, f32[2048,128]{1,0:T(8,128)S(1)}, bf16[1024,2048]{1,0:T(8,128)(2,1)S(1)}) custom-call(f32[16,128]{1,0:T(8,128)S(1)} %get-tuple-element.15.at_ref, f32[2048,128]{1,0:T(8,128)S(1)} %shard_map.66.state_in, bf16[512,128]{1,0:T(8,128)(2,1)S(1)} %get-tuple-element.18.qm_ref.qm, ...), custom_call_target="tpu_custom_call", output_to_operand_aliasing={{1}: (1, {})} | custom-call | flops 536870912 | bytes 4194304 | tf_op jit(solution)/shard_map/pallas_call | solution.py:297
  53.6 10.8 %all_to_all.16.got_ref = bf16[16,64,128]{2,1,0:T(8,128)(2,1)S(1)} all-to-all(bf16[16,64,128]{2,1,0:T(8,128)(2,1)S(1)} %get-tuple-element.23), channel_id=1, replica_groups=mesh['row'=16,'col'=16] {'col'}, dimensions={0} | all-to-all | bytes 524288 | tf_op jit(solution)/shard_map/all_to_all | solution.py:321
  64.4 1.5 %shard_map.68 = bf16[128,2048]{1,0:T(8,128)(2,1)} custom-call(bf16[16,64,128]{2,1,0:T(8,128)(2,1)S(1)} %all_to_all.16.got_ref, bf16[1024,2048]{1,0:T(8,128)(2,1)S(1)} %get-tuple-element.24.w_ref), custom_call_target="tpu_custom_call" | custom-call | flops 536870912 | bytes 4194304 | tf_op jit(solution)/shard_map/pallas_call | solution.py:309
Async XLA Ops:
  24.8 17.7 %all-to-all-start.1 = ((bf16[8,128,128]{2,1,0:T(8,128)(2,1)}), bf16[8,128,128]{2,1,0:T(8,128)(2,1)S(1)}, u32[]{:S(2)}, u32[]{:S(2)}) async-start(bf16[8,128,128]{2,1,0:T(8,128)(2,1)} %get-tuple-element.16.far_ref), calls=%async_computation.1 | async-start | bytes 524288 | tf_op jit(solution)/shard_map/all_to_all | solution.py:284
  33.0 8.7 %collective-permute-start = (bf16[512,128]{1,0:T(8,128)(2,1)S(1)}, bf16[512,128]{1,0:T(8,128)(2,1)S(1)}, u32[]{:S(2)}, u32[]{:S(2)}) collective-permute-start(bf16[512,128]{1,0:T(8,128)(2,1)S(1)} %get-tuple-element.17.kvm), channel_id=1, source_target_pairs={{0,32},{16,48},{32,0},{48,16},{64,96},{80,112},{96,64},{112,80},{1... | collective-permute-start | bytes 393224 | tf_op jit(solution)/shard_map/ppermute | solution.py:245
  42.5 6.1 %collective-permute-start.3 = (bf16[8,128,128]{2,1,0:T(8,128)(2,1)S(1)}, bf16[8,128,128]{2,1,0:T(8,128)(2,1)S(1)}, u32[]{:S(2)}, u32[]{:S(2)}) collective-permute-start(bf16[8,128,128]{2,1,0:T(8,128)(2,1)S(1)} %all-to-all-done.1.same), channel_id=1, source_target_pairs={{0,16},{16,0},{32,48},{48,32},{64,80},{80,64},{96,112},{112,96},{1... | collective-permute-start | bytes 786440 | tf_op jit(solution)/shard_map/ppermute | solution.py:245
  47.1 1.3 %collective-permute-start.1 = (bf16[512,128]{1,0:T(8,128)(2,1)S(1)}, bf16[512,128]{1,0:T(8,128)(2,1)S(1)}, u32[]{:S(2)}, u32[]{:S(2)}) collective-permute-start(bf16[512,128]{1,0:T(8,128)(2,1)S(1)} %get-tuple-element.17.kvm), channel_id=1, source_target_pairs={{0,16},{16,0},{32,48},{48,32},{64,80},{80,64},{96,112},{112,96},{1... | collective-permute-start | bytes 393224 | tf_op jit(solution)/shard_map/ppermute | solution.py:245
  47.1 1.5 %collective-permute-start.2 = (bf16[512,128]{1,0:T(8,128)(2,1)S(1)}, bf16[512,128]{1,0:T(8,128)(2,1)S(1)}, u32[]{:S(2)}, u32[]{:S(2)}) collective-permute-start(bf16[512,128]{1,0:T(8,128)(2,1)S(1)} %collective-permute-done.m2), channel_id=1, source_target_pairs={{0,16},{16,0},{32,48},{48,32},{64,80},{80,64},{96,112},{112,96},{1... | collective-permute-start | bytes 393224 | tf_op jit(solution)/shard_map/ppermute | solution.py:245
  48.7 2.2 %copy-start = (bf16[1024,2048]{1,0:T(8,128)(2,1)S(1)}, bf16[1024,2048]{1,0:T(8,128)(2,1)}, u32[]{:S(2)}) copy-start(bf16[1024,2048]{1,0:T(8,128)(2,1)} %w_hbm.1) | copy-start | bytes 12582916

commit v2 on v1

--- a/solution.py
+++ b/solution.py
@@ -24,6 +24,7 @@
 NEGATIVE = -1e30
 SCALE = 0.125 * 1.4426950408889634
 VMEM_LIMIT = 20 * 1024 * 1024
+VMEM_LAST = 46 * 1024 * 1024
 VMEM_MOST = 60 * 1024 * 1024
 
 VM = pl.BlockSpec(memory_space=pltpu.VMEM)
@@ -185,34 +186,41 @@
     merge(state, pl.ds(o_long, N_LONG, stride=R_LONG), top, acc)
 
 
-def last_kernel(at_ref, state_in, qm, m1, m2, m3, ql, same, other, w_hbm, out_ref, state, w_ref, w_sem):
+def mid_part(state, qm, o_mid, pos, parts):
+    step = 256
+    ones = jnp.concatenate([with_ones(ref[...]) for _, ref in parts], axis=0)
+    for i in range(N_MID // step):
+        q = qm[pl.ds(i * step, step), :]
+        pieces = []
+        for d, ref in parts:
+            before = jnp.bitwise_xor(pos, d) < pos
+            pieces.append(scores_of(q, ref[...]) + jnp.where(before, 0.0, NEGATIVE))
+        top, new = soft(jnp.concatenate(pieces, axis=1), ones)
+        merge(state, pl.ds(o_mid + i * step * R_MID, step, stride=R_MID), top, new)
+
+
+def long_part(state, ql, o_long, row, its_core, ref):
+    every = ref[...].reshape(ROWS // 2 * N_LONG, LANES)
+    s = scores_of(ql[...], every)
+    before = lax.broadcasted_iota(jnp.int32, s.shape, 1) < ((row + 1 - its_core) // 2) * N_LONG
+    top, new = soft(jnp.where(before, s, NEGATIVE), with_ones(every))
+    merge(state, pl.ds(o_long, N_LONG, stride=R_LONG), top, new)
+
+
+def near_kernel(at_ref, state_in, qm, m1, m2, ql, same, state):
+    o_mid, o_long = own_offsets(at_ref)
+    row = lax.axis_index("row")
+    mid_part(state, qm, o_mid, lax.rem(row, MID_ROWS), ((1, m1), (2, m2)))
+    long_part(state, ql, o_long, row, lax.rem(row, 2), same)
+
+
+def last_kernel(at_ref, state_in, qm, m3, ql, other, w_hbm, out_ref, state, w_ref, w_sem):
     load = pltpu.make_async_copy(w_hbm, w_ref, w_sem)
     load.start()
     o_mid, o_long = own_offsets(at_ref)
     row = lax.axis_index("row")
-    pos = lax.rem(row, MID_ROWS)
-    step = 256
-    for i in range(N_MID // step):
-        q = qm[pl.ds(i * step, step), :]
-        pieces, ones = [], []
-        for d, ref in ((1, m1), (2, m2), (3, m3)):
-            before = jnp.bitwise_xor(pos, d) < pos
-            pieces.append(scores_of(q, ref[...]) + jnp.where(before, 0.0, NEGATIVE))
-            ones.append(with_ones(ref[...]))
-        top, new = soft(jnp.concatenate(pieces, axis=1), jnp.concatenate(ones, axis=0))
-        merge(state, pl.ds(o_mid + i * step * R_MID, step, stride=R_MID), top, new)
-    q = ql[...]
-    pieces, ones = [], []
-    core = lax.rem(row, 2)
-    half = (ROWS // 2) * N_LONG
-    for ref, its_core in ((same, core), (other, 1 - core)):
-        every = ref[...].reshape(half, LANES)
-        s = scores_of(q, every)
-        before = lax.broadcasted_iota(jnp.int32, s.shape, 1) < ((row + 1 - its_core) // 2) * N_LONG
-        pieces.append(jnp.where(before, s, NEGATIVE))
-        ones.append(with_ones(every))
-    top, new = soft(jnp.concatenate(pieces, axis=1), jnp.concatenate(ones, axis=0))
-    merge(state, pl.ds(o_long, N_LONG, stride=R_LONG), top, new)
+    mid_part(state, qm, o_mid, lax.rem(row, MID_ROWS), ((3, m3),))
+    long_part(state, ql, o_long, row, 1 - lax.rem(row, 2), other)
     low = low_lanes(HALF)
     for src in range(HEADS):
         done = []
@@ -291,19 +299,29 @@
         moved=3 << 20,
         exps=SEG * SEG // 2,
     )(at, got, kv_mid, far, q_mid, q_long)
-    same, m2, state = bar((same, m2, state))
+    same, m1, m2, state = bar((same, m1, m2, state))
     m3 = xor_rows(m2, 1)
     other = xor_rows(same, 1)
+    state = call(
+        near_kernel,
+        shape(SEG, LANES, dtype=f32),
+        [VM] * 7,
+        flops=4 * N_MID * SEG * LANES,
+        moved=2 << 20,
+        exps=N_MID * SEG,
+        aliases={1: 0},
+    )(at, state, q_mid, m1, m2, q_long, same)
     back, _, weight = call(
         last_kernel,
         (shape(HEADS, HALF, LANES), shape(SEG, LANES, dtype=f32), shape(depth, wide_out)),
-        [VM] * 9 + [HB],
+        [VM] * 6 + [HB],
         scratch=[DMA],
         flops=4 * N_MID * SEG * LANES,
         moved=4 << 20,
         exps=N_MID * SEG,
         aliases={1: 1},
-    )(at, state, q_mid, m1, m2, m3, q_long, same, other, out_weight)
+        limit=VMEM_LAST,
+    )(at, state, q_mid, m3, q_long, other, out_weight)
     tile = 512
     count = wide_out // tile
     return call(

time: 66.3 us -> 63.5 us (0.958)
  waiting for transfers between devices: 2.75 us -> 0.01 us
  local copies, waits for them, and re-layouts: 2.19 us -> 0 us
  starting transfers between devices: 14.8 us -> 15.9 us
  Pallas kernels: 13.9 us -> 14.9 us
    unnamed x2 -> x0, local copies, waits for them, and re-layouts: 2.19 us -> none
    ppermute x4, waiting for transfers between devices: 1.9 us -> 0.01 us  [xor_rows(): return lax.ppermute(x, 'row', [(i, i ^ d) for i in range(ROWS)])]
    pallas_call x0 -> x1, Pallas kernels: none -> 1.52 us  [shards(): call(near_kernel, shape(SEG, LANES, dtype=f32), [VM] * 7, flops=4 * N_MID...]
    ppermute x4, starting transfers between devices: 6.57 us -> 7.74 us  [xor_rows(): return lax.ppermute(x, 'row', [(i, i ^ d) for i in range(ROWS)])]
    all_to_all x1, waiting for transfers between devices: 0.85 us -> 0.01 us  [shards(): same = lax.all_to_all(far, 'row', 0, 0, axis_index_groups=CORES)]
  transfers between devices with their start and end apart: 5 -> 5, of which waited for: 4 -> 0; matrix products, arithmetic and copies ran while one was open for 0% -> 0% of each run, Pallas kernels for 10% -> 12%
where the time goes in v2:
time: 63.5 us; the launch traced here: 63.1 us
  blocking collectives  32.2 us (51%)
  starting transfers between devices  15.9 us (25%)
  Pallas kernels  14.9 us (23%)
    all_to_all x1, blocking collectives, shards(): got = lax.all_to_all(sent, 'col', 0, 0)  21.5 us
    all_to_all x1, blocking collectives, shards(): lax.all_to_all(back, 'col', 0, 0)  10.7 us
    all_to_all x1, starting transfers between devices, shards(): same = lax.all_to_all(far, 'row', 0, 0, axis_index_groups=CORES)  8.19 us
    ppermute x4, starting transfers between devices, xor_rows(): return lax.ppermute(x, 'row', [(i, i ^ d) for i in range(ROWS)])  7.74 us
    pallas_call x1, Pallas kernels, shards(): call(short_kernel, shape(SEG, LANES, dtype=f32), [VM] * 6, scratch=[pltpu...  6.36 us
    pallas_call x1, Pallas kernels, shards(): call(pack_kernel, shape(HEADS, PACKED + NOTE, LANES), [HB] * 5, scratch=[...  2.24 us
    pallas_call x1, Pallas kernels, shards(): call(last_kernel, (shape(HEADS, HALF, LANES), shape(SEG, LANES, dtype=f32...  2.21 us
    pallas_call x1, Pallas kernels, shards(): call(near_kernel, shape(SEG, LANES, dtype=f32), [VM] * 7, flops=4 * N_MID...  1.52 us
  transfers between devices with their start and end apart: 5, of which 0 were waited for; matrix products, arithmetic and copies ran while one was open for 0% of the time, Pallas kernels for 12%

profile of v2, /device:TPU:1, one launch (start us, length us, event | category | flops | bytes accessed | tf_op | source)
XLA Modules:
  0.0 63.1 jit_solution(2623786829812516915)
XLA Ops:
  0.0 2.2 %shard_map.64 = bf16[16,208,128]{2,1,0:T(8,128)(2,1)} custom-call(s32[16]{0:T(128)} %mid_hbm.1, s32[16]{0:T(128)} %long_hbm.1, bf16[128,1024]{1,0:T(8,128)(2,1)} %q_hbm.1, bf16[128,1024]{1,0:T(8,128)(2,1)} %k_hbm.1, bf16[128,1024]{1,0:T(8,128)(2,1)} %v_hbm.1), custom_call_target="tpu_custom_call" | custom-call | bytes 1048576 | tf_op jit(solution)/shard_map/pallas_call | solution.py:265
  2.2 21.5 %all_to_all.15.got_ref = bf16[16,208,128]{2,1,0:T(8,128)(2,1)S(1)} all-to-all(bf16[16,208,128]{2,1,0:T(8,128)(2,1)} %shard_map.64), channel_id=1, replica_groups=mesh['row'=16,'col'=16] {'col'}, dimensions={0} | all-to-all | bytes 1703936 | tf_op jit(solution)/shard_map/all_to_all | solution.py:276
  23.7 1.1 %shard_map.65 = (bf16[512,128]{1,0:T(8,128)(2,1)S(1)}, bf16[8,128,128]{2,1,0:T(8,128)(2,1)}, bf16[512,128]{1,0:T(8,128)(2,1)S(1)}, bf16[128,128]{1,0:T(8,128)(2,1)S(1)}, f32[16,128]{1,0:T(8,128)S(1)}) custom-call(bf16[16,208,128]{2,1,0:T(8,128)(2,1)S(1)} %all_to_all.15.got_ref), custom_call_target="tpu_custom_call" | custom-call | bytes 1048576 | tf_op jit(solution)/shard_map/pallas_call | solution.py:277
  24.8 8.2 %all-to-all-start.1 = ((bf16[8,128,128]{2,1,0:T(8,128)(2,1)}), bf16[8,128,128]{2,1,0:T(8,128)(2,1)S(1)}, u32[]{:S(2)}, u32[]{:S(2)}) async-start(bf16[8,128,128]{2,1,0:T(8,128)(2,1)} %get-tuple-element.17.far_ref), calls=%async_computation.1 | async-start | bytes 524288 | tf_op jit(solution)/shard_map/all_to_all | solution.py:292
  33.0 1.5 %collective-permute-start.1 = (bf16[512,128]{1,0:T(8,128)(2,1)S(1)}, bf16[512,128]{1,0:T(8,128)(2,1)S(1)}, u32[]{:S(2)}, u32[]{:S(2)}) collective-permute-start(bf16[512,128]{1,0:T(8,128)(2,1)S(1)} %get-tuple-element.18.kvm), channel_id=1, source_target_pairs={{0,32},{16,48},{32,0},{48,16},{64,96},{80,112},{96,64},{112,80},{1... | collective-permute-start | bytes 393224 | tf_op jit(solution)/shard_map/ppermute | solution.py:253
  34.4 2.7 %collective-permute-start = (bf16[512,128]{1,0:T(8,128)(2,1)S(1)}, bf16[512,128]{1,0:T(8,128)(2,1)S(1)}, u32[]{:S(2)}, u32[]{:S(2)}) collective-permute-start(bf16[512,128]{1,0:T(8,128)(2,1)S(1)} %get-tuple-element.18.kvm), channel_id=1, source_target_pairs={{0,16},{16,0},{32,48},{48,32},{64,80},{80,64},{96,112},{112,96},{1... | collective-permute-start | bytes 393224 | tf_op jit(solution)/shard_map/ppermute | solution.py:253
  37.1 6.4 %shard_map.66.state_in = f32[2048,128]{1,0:T(8,128)S(1)} custom-call(f32[16,128]{1,0:T(8,128)S(1)} %get-tuple-element.16.at_ref, bf16[16,208,128]{2,1,0:T(8,128)(2,1)S(1)} %all_to_all.15.got_ref, bf16[512,128]{1,0:T(8,128)(2,1)S(1)} %get-tuple-element.18.kvm, bf16[8,128,128]{2,1,0:T(8,128)(2,1)} %get-tuple-element.17.far_ref, ...), custom_call_target="tpu_custom_call" | custom-call | flops 2147483648 | bytes 3145728 | tf_op jit(solution)/shard_map/pallas_call | solution.py:293
  43.5 0.0 collective-permute-done.1.m2
  43.5 0.0 collective-permute-done.m1
  43.5 0.0 all-to-all-done.1.same
  43.5 3.6 %collective-permute-start.3 = (bf16[8,128,128]{2,1,0:T(8,128)(2,1)S(1)}, bf16[8,128,128]{2,1,0:T(8,128)(2,1)S(1)}, u32[]{:S(2)}, u32[]{:S(2)}) collective-permute-start(bf16[8,128,128]{2,1,0:T(8,128)(2,1)S(1)} %all-to-all-done.1.same), channel_id=1, source_target_pairs={{0,16},{16,0},{32,48},{48,32},{64,80},{80,64},{96,112},{112,96},{1... | collective-permute-start | bytes 786440 | tf_op jit(solution)/shard_map/ppermute | solution.py:253
  47.1 0.0 collective-permute-start.2
  47.1 1.5 %shard_map.67.state_in = f32[2048,128]{1,0:T(8,128)S(1)} custom-call(f32[16,128]{1,0:T(8,128)S(1)} %get-tuple-element.16.at_ref, f32[2048,128]{1,0:T(8,128)S(1)} %shard_map.66.state_in, bf16[512,128]{1,0:T(8,128)(2,1)S(1)} %get-tuple-element.19.qm_ref.qm, bf16[512,128]{1,0:T(8,128)(2,1)S(1)} %collective-permute-done.m1, ...), custom_call_target="tpu_custom_call", output_to_operand_aliasing={{}: (1, {})} | custom-call | flops 536870912 | bytes 2097152 | tf_op jit(solution)/shard_map/pallas_call | solution.py:305
  48.7 0.0 collective-permute-done.2.m3
  48.7 0.0 collective-permute-done.3.other
  48.7 2.2 %shard_map.68 = (bf16[16,64,128]{2,1,0:T(8,128)(2,1)S(1)}, f32[2048,128]{1,0:T(8,128)S(1)}, bf16[1024,2048]{1,0:T(8,128)(2,1)S(1)}) custom-call(f32[16,128]{1,0:T(8,128)S(1)} %get-tuple-element.16.at_ref, f32[2048,128]{1,0:T(8,128)S(1)} %shard_map.67.state_in, bf16[512,128]{1,0:T(8,128)(2,1)S(1)} %get-tuple-element.19.qm_ref.qm, ...), custom_call_target="tpu_custom_call", output_to_operand_aliasing={{1}: (1, {})} | custom-call | flops 536870912 | bytes 4194304 | tf_op jit(solution)/shard_map/pallas_call | solution.py:314
  50.9 10.7 %all_to_all.16.got_ref = bf16[16,64,128]{2,1,0:T(8,128)(2,1)S(1)} all-to-all(bf16[16,64,128]{2,1,0:T(8,128)(2,1)S(1)} %get-tuple-element.25), channel_id=1, replica_groups=mesh['row'=16,'col'=16] {'col'}, dimensions={0} | all-to-all | bytes 524288 | tf_op jit(solution)/shard_map/all_to_all | solution.py:339
  61.6 1.5 %shard_map.69 = bf16[128,2048]{1,0:T(8,128)(2,1)} custom-call(bf16[16,64,128]{2,1,0:T(8,128)(2,1)S(1)} %all_to_all.16.got_ref, bf16[1024,2048]{1,0:T(8,128)(2,1)S(1)} %get-tuple-element.26.w_ref), custom_call_target="tpu_custom_call" | custom-call | flops 536870912 | bytes 4194304 | tf_op jit(solution)/shard_map/pallas_call | solution.py:327
Async XLA Ops:
  24.8 18.7 %all-to-all-start.1 = ((bf16[8,128,128]{2,1,0:T(8,128)(2,1)}), bf16[8,128,128]{2,1,0:T(8,128)(2,1)S(1)}, u32[]{:S(2)}, u32[]{:S(2)}) async-start(bf16[8,128,128]{2,1,0:T(8,128)(2,1)} %get-tuple-element.17.far_ref), calls=%async_computation.1 | async-start | bytes 524288 | tf_op jit(solution)/shard_map/all_to_all | solution.py:292
  33.0 10.5 %collective-permute-start.1 = (bf16[512,128]{1,0:T(8,128)(2,1)S(1)}, bf16[512,128]{1,0:T(8,128)(2,1)S(1)}, u32[]{:S(2)}, u32[]{:S(2)}) collective-permute-start(bf16[512,128]{1,0:T(8,128)(2,1)S(1)} %get-tuple-element.18.kvm), channel_id=1, source_target_pairs={{0,32},{16,48},{32,0},{48,16},{64,96},{80,112},{96,64},{112,80},{1... | collective-permute-start | bytes 393224 | tf_op jit(solution)/shard_map/ppermute | solution.py:253
  34.4 9.1 %collective-permute-start = (bf16[512,128]{1,0:T(8,128)(2,1)S(1)}, bf16[512,128]{1,0:T(8,128)(2,1)S(1)}, u32[]{:S(2)}, u32[]{:S(2)}) collective-permute-start(bf16[512,128]{1,0:T(8,128)(2,1)S(1)} %get-tuple-element.18.kvm), channel_id=1, source_target_pairs={{0,16},{16,0},{32,48},{48,32},{64,80},{80,64},{96,112},{112,96},{1... | collective-permute-start | bytes 393224 | tf_op jit(solution)/shard_map/ppermute | solution.py:253
  43.5 5.1 %collective-permute-start.3 = (bf16[8,128,128]{2,1,0:T(8,128)(2,1)S(1)}, bf16[8,128,128]{2,1,0:T(8,128)(2,1)S(1)}, u32[]{:S(2)}, u32[]{:S(2)}) collective-permute-start(bf16[8,128,128]{2,1,0:T(8,128)(2,1)S(1)} %all-to-all-done.1.same), channel_id=1, source_target_pairs={{0,16},{16,0},{32,48},{48,32},{64,80},{80,64},{96,112},{112,96},{1... | collective-permute-start | bytes 786440 | tf_op jit(solution)/shard_map/ppermute | solution.py:253
  47.1 1.5 %collective-permute-start.2 = (bf16[512,128]{1,0:T(8,128)(2,1)S(1)}, bf16[512,128]{1,0:T(8,128)(2,1)S(1)}, u32[]{:S(2)}, u32[]{:S(2)}) collective-permute-start(bf16[512,128]{1,0:T(8,128)(2,1)S(1)} %collective-permute-done.1.m2), channel_id=1, source_target_pairs={{0,16},{16,0},{32,48},{48,32},{64,80},{80,64},{96,112},{112,96},{1... | collective-permute-start | bytes 393224 | tf_op jit(solution)/shard_map/ppermute | solution.py:253

commit v3 on v2

--- a/solution.py
+++ b/solution.py
@@ -24,7 +24,8 @@
 NEGATIVE = -1e30
 SCALE = 0.125 * 1.4426950408889634
 VMEM_LIMIT = 20 * 1024 * 1024
-VMEM_LAST = 46 * 1024 * 1024
+VMEM_LAST = 47 * 1024 * 1024
+VMEM_NEAR = 49 * 1024 * 1024
 VMEM_MOST = 60 * 1024 * 1024
 
 VM = pl.BlockSpec(memory_space=pltpu.VMEM)
@@ -94,22 +95,16 @@
         copy.wait()
 
 
-def select_kernel(got_ref, kvm_ref, far_ref, qm_ref, ql_ref, at_ref, wide):
-    for src in range(HEADS):
-        wide[0, pl.ds(src * BLOCK, BLOCK), :] = got_ref[src, :BLOCK].astype(jnp.float32)
-        packed = got_ref[src, BLOCK:PACKED].astype(jnp.float32)
-        wide[1, pl.ds(src * BLOCK, HALF), :] = packed
-        wide[1, pl.ds(src * BLOCK + HALF, HALF), :] = pltpu.roll(packed, HD, 1)
+def select_kernel(got_ref, kvm_ref, own_ref, at_ref, far_ref, wide):
     at_ref[...] = got_ref[0, PACKED:].astype(jnp.float32)
     o_mid, o_long = own_offsets(at_ref)
-    kvm_ref[...] = wide[0, pl.ds(o_mid, N_MID, stride=R_MID), :].astype(jnp.bfloat16)
-    far = wide[0, pl.ds(o_long, N_LONG, stride=R_LONG), :].astype(jnp.bfloat16)
+    for src in range(HEADS):
+        wide[pl.ds(src * BLOCK, BLOCK), :] = got_ref[src, :BLOCK].astype(jnp.float32)
+    far = wide[pl.ds(o_long, N_LONG, stride=R_LONG), :].astype(jnp.bfloat16)
+    own_ref[...] = far
     for z in range(ROWS // 2):
         far_ref[z] = far
-    q = wide[1, pl.ds(o_mid, N_MID, stride=R_MID), :]
-    qm_ref[...] = jnp.where(low_lanes(N_MID), q, 0.0).astype(jnp.bfloat16)
-    q = wide[1, pl.ds(o_long, N_LONG, stride=R_LONG), :]
-    ql_ref[...] = jnp.where(low_lanes(N_LONG), q, 0.0).astype(jnp.bfloat16)
+    kvm_ref[...] = wide[pl.ds(o_mid, N_MID, stride=R_MID), :].astype(jnp.bfloat16)
 
 
 def own_offsets(at_ref):
@@ -150,7 +145,7 @@
     return lax.broadcasted_iota(jnp.int32, (rows, cols), 1) <= at
 
 
-def short_kernel(at_ref, got_ref, kvm, far_ref, qm_ref, ql_ref, state, kv_buf, one_buf):
+def short_kernel(at_ref, got_ref, kvm, own_ref, state, qm_ref, ql_ref, kv_buf, one_buf, wide):
     for src in range(HEADS):
         rows = pl.ds(src * BLOCK, BLOCK)
         kv = got_ref[src, :BLOCK]
@@ -168,6 +163,7 @@
             parts.append(jnp.where(low, jnp.concatenate([packed[:, HD:], packed[:, :HD]], axis=1), zero))
         q = jnp.concatenate(parts, axis=0)
         rows = pl.ds(i * step, step)
+        wide[rows, :] = q.astype(jnp.float32)
         n = (i + 1) * step
         s = scores_of(q, kv_buf[rows, :])
         s = jnp.where(visible, s, NEGATIVE)
@@ -175,12 +171,14 @@
             s = jnp.concatenate([scores_of(q, kv_buf[pl.ds(0, i * step), :]), s], axis=1)
         state[rows, :] = state_of(*soft(s, one_buf[pl.ds(0, n), :]))
     o_mid, o_long = own_offsets(at_ref)
+    qm_ref[...] = wide[pl.ds(o_mid, N_MID, stride=R_MID), :].astype(jnp.bfloat16)
+    ql_ref[...] = wide[pl.ds(o_long, N_LONG, stride=R_LONG), :].astype(jnp.bfloat16)
     for i in range(N_MID // step):
         n = (i + 1) * step
         s = scores_of(qm_ref[pl.ds(i * step, step), :], kvm[:n])
         top, acc = soft(jnp.where(causal(step, n, i * step), s, NEGATIVE), with_ones(kvm[:n]))
         merge(state, pl.ds(o_mid + i * step * R_MID, step, stride=R_MID), top, acc)
-    far = far_ref[0]
+    far = own_ref[...]
     s = scores_of(ql_ref[...], far)
     top, acc = soft(jnp.where(causal(N_LONG, N_LONG, 0), s, NEGATIVE), with_ones(far))
     merge(state, pl.ds(o_long, N_LONG, stride=R_LONG), top, acc)
@@ -207,19 +205,32 @@
     merge(state, pl.ds(o_long, N_LONG, stride=R_LONG), top, new)
 
 
-def near_kernel(at_ref, state_in, qm, m1, m2, ql, same, state):
-    o_mid, o_long = own_offsets(at_ref)
-    row = lax.axis_index("row")
-    mid_part(state, qm, o_mid, lax.rem(row, MID_ROWS), ((1, m1), (2, m2)))
-    long_part(state, ql, o_long, row, lax.rem(row, 2), same)
-
-
-def last_kernel(at_ref, state_in, qm, m3, ql, other, w_hbm, out_ref, state, w_ref, w_sem):
-    load = pltpu.make_async_copy(w_hbm, w_ref, w_sem)
-    load.start()
+def load_rows(src, first, dst, sems):
+    count = sems.shape[0]
+    part = dst.shape[0] // count
+    pairs = [(src.at[pl.ds(first + i * part, part)], dst.at[pl.ds(i * part, part)]) for i in range(count)]
+    return fetch(pairs, sems)
+
+
+def near_kernel(at_ref, state_in, qm, m1, m2, w_hbm, state, w_ref, w_sems):
+    loads = load_rows(w_hbm, 0, w_ref, w_sems)
+    o_mid, _ = own_offsets(at_ref)
+    mid_part(state, qm, o_mid, lax.rem(lax.axis_index("row"), MID_ROWS), ((1, m1), (2, m2)))
+    for load in loads:
+        load.wait()
+
+
+def same_kernel(at_ref, state_in, qm, m3, ql, same, state):
     o_mid, o_long = own_offsets(at_ref)
     row = lax.axis_index("row")
     mid_part(state, qm, o_mid, lax.rem(row, MID_ROWS), ((3, m3),))
+    long_part(state, ql, o_long, row, lax.rem(row, 2), same)
+
+
+def last_kernel(at_ref, state_in, ql, other, w_hbm, out_ref, state, w_ref, w_sems):
+    loads = load_rows(w_hbm, w_hbm.shape[0] - w_ref.shape[0], w_ref, w_sems)
+    _, o_long = own_offsets(at_ref)
+    row = lax.axis_index("row")
     long_part(state, ql, o_long, row, 1 - lax.rem(row, 2), other)
     low = low_lanes(HALF)
     for src in range(HEADS):
@@ -228,21 +239,25 @@
             a = state[pl.ds(src * BLOCK + half * HALF, HALF), :]
             done.append(a / a[:, :1])
         out_ref[src] = jnp.where(low, pltpu.roll(done[0], HD, 1), done[1]).astype(jnp.bfloat16)
-    load.wait()
-
-
-def project_kernel(got_ref, w_ref, out_hbm, combined, tiles, sems):
+    for load in loads:
+        load.wait()
+
+
+def project_kernel(got_ref, w0_ref, w1_ref, out_hbm, combined, tiles, sems):
     count, _, tile = tiles.shape
     for pair in range(HEADS // 2):
         a, b = got_ref[2 * pair], got_ref[2 * pair + 1]
         cols = pl.ds(pair * LANES, LANES)
         combined[:HALF, cols] = jnp.concatenate([a[:, :HD], b[:, :HD]], axis=1)
         combined[HALF:, cols] = jnp.concatenate([a[:, HD:], b[:, HD:]], axis=1)
-    rows = combined[...]
+    cut = w0_ref.shape[0]
+    first, second = combined[:, :cut], combined[:, cut:]
     copies = []
     for i in range(count):
         cols = pl.ds(i * tile, tile)
-        tiles[i] = jnp.dot(rows, w_ref[:, cols], preferred_element_type=jnp.float32).astype(jnp.bfloat16)
+        total = jnp.dot(first, w0_ref[:, cols], preferred_element_type=jnp.float32)
+        total += jnp.dot(second, w1_ref[:, cols], preferred_element_type=jnp.float32)
+        tiles[i] = total.astype(jnp.bfloat16)
         copies.append(pltpu.make_async_copy(tiles.at[i], out_hbm.at[:, cols], sems.at[i]))
         copies[-1].start()
     for copy in copies:
@@ -274,69 +289,81 @@
         limit=VMEM_MOST,
     )(mid_offsets, long_offsets, queries, keys, values)
     got = lax.all_to_all(sent, "col", 0, 0)
-    kv_mid, far, q_mid, q_long, at = call(
+    kv_mid, own, at, far = call(
         select_kernel,
         (
             shape(N_MID, LANES),
-            shape(ROWS // 2, N_LONG, LANES),
-            shape(N_MID, LANES),
             shape(N_LONG, LANES),
             shape(NOTE, LANES, dtype=f32),
+            shape(ROWS // 2, N_LONG, LANES),
         ),
         [VM],
-        scratch=[pltpu.VMEM((2, SEG, LANES), f32)],
+        scratch=[pltpu.VMEM((SEG, LANES), f32)],
         moved=1 << 20,
     )(got)
     m1 = xor_rows(kv_mid, 1)
     m2 = xor_rows(kv_mid, 2)
     same = lax.all_to_all(far, "row", 0, 0, axis_index_groups=CORES)
-    state = call(
+    state, q_mid, q_long = call(
         short_kernel,
-        shape(SEG, LANES, dtype=f32),
-        [VM] * 6,
-        scratch=[pltpu.VMEM((SEG, LANES), bf16)] * 2,
+        (shape(SEG, LANES, dtype=f32), shape(N_MID, LANES), shape(N_LONG, LANES)),
+        [VM] * 4,
+        scratch=[pltpu.VMEM((SEG, LANES), bf16)] * 2 + [pltpu.VMEM((SEG, LANES), f32)],
         flops=4 * SEG * SEG * LANES,
         moved=3 << 20,
         exps=SEG * SEG // 2,
-    )(at, got, kv_mid, far, q_mid, q_long)
-    same, m1, m2, state = bar((same, m1, m2, state))
+    )(at, got, kv_mid, own)
+    m1, m2, state = bar((m1, m2, state))
     m3 = xor_rows(m2, 1)
-    other = xor_rows(same, 1)
-    state = call(
+    early = depth * 3 // 8
+    state, weight0 = call(
         near_kernel,
-        shape(SEG, LANES, dtype=f32),
-        [VM] * 7,
+        (shape(SEG, LANES, dtype=f32), shape(early, wide_out)),
+        [VM] * 5 + [HB],
+        scratch=[DMA((1,))],
         flops=4 * N_MID * SEG * LANES,
         moved=2 << 20,
         exps=N_MID * SEG,
         aliases={1: 0},
-    )(at, state, q_mid, m1, m2, q_long, same)
+        limit=VMEM_NEAR,
+    )(at, state, q_mid, m1, m2, out_weight)
+    same, m3, state = bar((same, m3, state))
+    other = xor_rows(same, 1)
+    state = call(
+        same_kernel,
+        shape(SEG, LANES, dtype=f32),
+        [VM] * 6,
+        flops=4 * N_MID * SEG * LANES,
+        moved=2 << 20,
+        exps=N_MID * SEG,
+        aliases={1: 0},
+    )(at, state, q_mid, m3, q_long, same)
+    tile = 512
+    count = wide_out // tile
     back, _, weight = call(
         last_kernel,
-        (shape(HEADS, HALF, LANES), shape(SEG, LANES, dtype=f32), shape(depth, wide_out)),
-        [VM] * 6 + [HB],
-        scratch=[DMA],
-        flops=4 * N_MID * SEG * LANES,
+        (shape(HEADS, HALF, LANES), shape(SEG, LANES, dtype=f32), shape(depth - early, wide_out)),
+        [VM] * 4 + [HB],
+        scratch=[DMA((1,))],
+        flops=4 * N_LONG * SEG * LANES,
         moved=4 << 20,
-        exps=N_MID * SEG,
+        exps=N_LONG * SEG,
         aliases={1: 1},
         limit=VMEM_LAST,
-    )(at, state, q_mid, m3, q_long, other, out_weight)
-    tile = 512
-    count = wide_out // tile
+    )(at, state, q_long, other, out_weight)
     return call(
         project_kernel,
         shape(BLOCK, wide_out),
-        [VM, VM],
+        [VM, VM, VM],
         scratch=[
-            pltpu.VMEM((BLOCK, depth), jnp.bfloat16),
-            pltpu.VMEM((count, BLOCK, tile), jnp.bfloat16),
+            pltpu.VMEM((BLOCK, depth), bf16),
+            pltpu.VMEM((count, BLOCK, tile), bf16),
             DMA((count,)),
         ],
         flops=2 * BLOCK * depth * wide_out,
         moved=2 * depth * wide_out,
         out_specs=HB,
-    )(lax.all_to_all(back, "col", 0, 0), weight)
+    )(lax.all_to_all(back, "col", 0, 0), weight0, weight)
 
 
 def solution(mesh):

time: 63.5 us -> 62.9 us (level)
    pallas_call x4 -> x5, Pallas kernels: 10.4 us -> 10.6 us  [the longest x1 5.37 us: shards(): call(short_kernel, (shape(SEG, LANES, dtype=f32), shape(N_MID, LANES), sh...]
  transfers between devices with their start and end apart: 5 -> 5, of which waited for: 0 -> 0; matrix products, arithmetic and copies ran while one was open for 0% -> 0% of each run, Pallas kernels for 12% -> 13%
where the time goes in v3:
time: 62.9 us; the launch traced here: 62.4 us
  blocking collectives  32.3 us (51%)
  starting transfers between devices  15.5 us (25%)
  Pallas kernels  14.6 us (23%)
    all_to_all x1, blocking collectives, shards(): got = lax.all_to_all(sent, 'col', 0, 0)  21.5 us
    all_to_all x1, blocking collectives, shards(): lax.all_to_all(back, 'col', 0, 0)  10.8 us
    all_to_all x1, starting transfers between devices, shards(): same = lax.all_to_all(far, 'row', 0, 0, axis_index_groups=CORES)  8.19 us
    ppermute x4, starting transfers between devices, xor_rows(): return lax.ppermute(x, 'row', [(i, i ^ d) for i in range(ROWS)])  7.28 us
    pallas_call x1, Pallas kernels, shards(): call(short_kernel, (shape(SEG, LANES, dtype=f32), shape(N_MID, LANES), sh...  5.37 us
    pallas_call x1, Pallas kernels, shards(): call(pack_kernel, shape(HEADS, PACKED + NOTE, LANES), [HB] * 5, scratch=[...  2.25 us
    pallas_call x1, Pallas kernels, shards(): call(last_kernel, (shape(HEADS, HALF, LANES), shape(SEG, LANES, dtype=f32...  1.77 us
    pallas_call x1, Pallas kernels, shards(): call(project_kernel, shape(BLOCK, wide_out), [VM, VM, VM], scratch=[pltpu...  1.59 us
  transfers between devices with their start and end apart: 5, of which 0 were waited for; matrix products, arithmetic and copies ran while one was open for 0% of the time, Pallas kernels for 13%

profile of v3, /device:TPU:1, one launch (start us, length us, event | category | flops | bytes accessed | tf_op | source)
XLA Modules:
  0.0 62.4 jit_solution(16214055822902213973)
XLA Ops:
  0.0 2.2 %shard_map.64 = bf16[16,208,128]{2,1,0:T(8,128)(2,1)} custom-call(s32[16]{0:T(128)} %mid_hbm.1, s32[16]{0:T(128)} %long_hbm.1, bf16[128,1024]{1,0:T(8,128)(2,1)} %q_hbm.1, bf16[128,1024]{1,0:T(8,128)(2,1)} %k_hbm.1, bf16[128,1024]{1,0:T(8,128)(2,1)} %v_hbm.1), custom_call_target="tpu_custom_call" | custom-call | bytes 1048576 | tf_op jit(solution)/shard_map/pallas_call | solution.py:280
  2.3 21.5 %all_to_all.15.got_ref = bf16[16,208,128]{2,1,0:T(8,128)(2,1)S(1)} all-to-all(bf16[16,208,128]{2,1,0:T(8,128)(2,1)} %shard_map.64), channel_id=1, replica_groups=mesh['row'=16,'col'=16] {'col'}, dimensions={0} | all-to-all | bytes 1703936 | tf_op jit(solution)/shard_map/all_to_all | solution.py:291
  23.7 1.0 %shard_map.65 = (bf16[512,128]{1,0:T(8,128)(2,1)S(1)}, bf16[128,128]{1,0:T(8,128)(2,1)S(1)}, f32[16,128]{1,0:T(8,128)S(1)}, bf16[8,128,128]{2,1,0:T(8,128)(2,1)}) custom-call(bf16[16,208,128]{2,1,0:T(8,128)(2,1)S(1)} %all_to_all.15.got_ref), custom_call_target="tpu_custom_call" | custom-call | bytes 1048576 | tf_op jit(solution)/shard_map/pallas_call | solution.py:292
  24.7 8.2 %all-to-all-start.1 = ((bf16[8,128,128]{2,1,0:T(8,128)(2,1)}), bf16[8,128,128]{2,1,0:T(8,128)(2,1)S(1)}, u32[]{:S(2)}, u32[]{:S(2)}) async-start(bf16[8,128,128]{2,1,0:T(8,128)(2,1)} %get-tuple-element.23), calls=%async_computation.1 | async-start | bytes 524288 | tf_op jit(solution)/shard_map/all_to_all | solution.py:306
  32.9 1.5 %collective-permute-start.1 = (bf16[512,128]{1,0:T(8,128)(2,1)S(1)}, bf16[512,128]{1,0:T(8,128)(2,1)S(1)}, u32[]{:S(2)}, u32[]{:S(2)}) collective-permute-start(bf16[512,128]{1,0:T(8,128)(2,1)S(1)} %get-tuple-element.24.kvm), channel_id=1, source_target_pairs={{0,32},{16,48},{32,0},{48,16},{64,96},{80,112},{96,64},{112,80},{1... | collective-permute-start | bytes 393224 | tf_op jit(solution)/shard_map/ppermute | solution.py:268
  34.4 2.7 %collective-permute-start = (bf16[512,128]{1,0:T(8,128)(2,1)S(1)}, bf16[512,128]{1,0:T(8,128)(2,1)S(1)}, u32[]{:S(2)}, u32[]{:S(2)}) collective-permute-start(bf16[512,128]{1,0:T(8,128)(2,1)S(1)} %get-tuple-element.24.kvm), channel_id=1, source_target_pairs={{0,16},{16,0},{32,48},{48,32},{64,80},{80,64},{96,112},{112,96},{1... | collective-permute-start | bytes 393224 | tf_op jit(solution)/shard_map/ppermute | solution.py:268
  37.0 5.4 %shard_map.66 = (f32[2048,128]{1,0:T(8,128)S(1)}, bf16[512,128]{1,0:T(8,128)(2,1)S(1)}, bf16[128,128]{1,0:T(8,128)(2,1)S(1)}) custom-call(f32[16,128]{1,0:T(8,128)S(1)} %get-tuple-element.22.at_ref, bf16[16,208,128]{2,1,0:T(8,128)(2,1)S(1)} %all_to_all.15.got_ref, bf16[512,128]{1,0:T(8,128)(2,1)S(1)} %get-tuple-element.24.kvm, ...), custom_call_target="tpu_custom_call" | custom-call | flops 2147483648 | bytes 3145728 | tf_op jit(solution)/shard_map/pallas_call | solution.py:307
  42.4 0.0 collective-permute-done.1.m2
  42.4 0.0 collective-permute-done.m1
  42.4 2.2 %collective-permute-start.2 = (bf16[512,128]{1,0:T(8,128)(2,1)S(1)}, bf16[512,128]{1,0:T(8,128)(2,1)S(1)}, u32[]{:S(2)}, u32[]{:S(2)}) collective-permute-start(bf16[512,128]{1,0:T(8,128)(2,1)S(1)} %collective-permute-done.1.m2), channel_id=1, source_target_pairs={{0,16},{16,0},{32,48},{48,32},{64,80},{80,64},{96,112},{112,96},{1... | collective-permute-start | bytes 393224 | tf_op jit(solution)/shard_map/ppermute | solution.py:268
  44.6 1.4 %shard_map.67 = (f32[2048,128]{1,0:T(8,128)S(1)}, bf16[384,2048]{1,0:T(8,128)(2,1)S(1)}) custom-call(f32[16,128]{1,0:T(8,128)S(1)} %get-tuple-element.22.at_ref, f32[2048,128]{1,0:T(8,128)S(1)} %get-tuple-element.28.state_in, bf16[512,128]{1,0:T(8,128)(2,1)S(1)} %get-tuple-element.29.qm, ...), custom_call_target="tpu_custom_call", output_to_operand_aliasing={{0}: (1, {})} | custom-call | flops 536870912 | bytes 2097152 | tf_op jit(solution)/shard_map/pallas_call | solution.py:319
  46.1 0.0 collective-permute-done.2.m3
  46.1 0.0 all-to-all-done.1.same
  46.1 0.9 %collective-permute-start.3 = (bf16[8,128,128]{2,1,0:T(8,128)(2,1)S(1)}, bf16[8,128,128]{2,1,0:T(8,128)(2,1)S(1)}, u32[]{:S(2)}, u32[]{:S(2)}) collective-permute-start(bf16[8,128,128]{2,1,0:T(8,128)(2,1)S(1)} %all-to-all-done.1.same), channel_id=1, source_target_pairs={{0,16},{16,0},{32,48},{48,32},{64,80},{80,64},{96,112},{112,96},{1... | collective-permute-start | bytes 786440 | tf_op jit(solution)/shard_map/ppermute | solution.py:268
  47.0 1.2 %shard_map.68.state_in = f32[2048,128]{1,0:T(8,128)S(1)} custom-call(f32[16,128]{1,0:T(8,128)S(1)} %get-tuple-element.22.at_ref, f32[2048,128]{1,0:T(8,128)S(1)} %get-tuple-element.32.state_in, bf16[512,128]{1,0:T(8,128)(2,1)S(1)} %get-tuple-element.29.qm, bf16[512,128]{1,0:T(8,128)(2,1)S(1)} %collective-permute-done.2.m3, ...), custom_call_target="tpu_custom_call", output_to_operand_aliasing={{}: (1, {})} | custom-call | flops 536870912 | bytes 2097152 | tf_op jit(solution)/shard_map/pallas_call | solution.py:332
  48.2 0.0 collective-permute-done.3.other
  48.2 1.8 %shard_map.69 = (bf16[16,64,128]{2,1,0:T(8,128)(2,1)S(1)}, f32[2048,128]{1,0:T(8,128)S(1)}, bf16[640,2048]{1,0:T(8,128)(2,1)S(1)}) custom-call(f32[16,128]{1,0:T(8,128)S(1)} %get-tuple-element.22.at_ref, f32[2048,128]{1,0:T(8,128)S(1)} %shard_map.68.state_in, bf16[128,128]{1,0:T(8,128)(2,1)S(1)} %get-tuple-element.34.ql, ...), custom_call_target="tpu_custom_call", output_to_operand_aliasing={{1}: (1, {})} | custom-call | flops 134217728 | bytes 4194304 | tf_op jit(solution)/shard_map/pallas_call | solution.py:343
  50.0 10.8 %all_to_all.16.got_ref = bf16[16,64,128]{2,1,0:T(8,128)(2,1)S(1)} all-to-all(bf16[16,64,128]{2,1,0:T(8,128)(2,1)S(1)} %get-tuple-element.36), channel_id=1, replica_groups=mesh['row'=16,'col'=16] {'col'}, dimensions={0} | all-to-all | bytes 524288 | tf_op jit(solution)/shard_map/all_to_all | solution.py:366
  60.9 1.6 %shard_map.70 = bf16[128,2048]{1,0:T(8,128)(2,1)} custom-call(bf16[16,64,128]{2,1,0:T(8,128)(2,1)S(1)} %all_to_all.16.got_ref, bf16[384,2048]{1,0:T(8,128)(2,1)S(1)} %get-tuple-element.37.w0_ref, bf16[640,2048]{1,0:T(8,128)(2,1)S(1)} %get-tuple-element.38.w1_ref), custom_call_target="tpu_custom_call" | custom-call | flops 536870912 | bytes 4194304 | tf_op jit(solution)/shard_map/pallas_call | solution.py:354
Async XLA Ops:
  24.7 21.4 %all-to-all-start.1 = ((bf16[8,128,128]{2,1,0:T(8,128)(2,1)}), bf16[8,128,128]{2,1,0:T(8,128)(2,1)S(1)}, u32[]{:S(2)}, u32[]{:S(2)}) async-start(bf16[8,128,128]{2,1,0:T(8,128)(2,1)} %get-tuple-element.23), calls=%async_computation.1 | async-start | bytes 524288 | tf_op jit(solution)/shard_map/all_to_all | solution.py:306
  32.9 9.5 %collective-permute-start.1 = (bf16[512,128]{1,0:T(8,128)(2,1)S(1)}, bf16[512,128]{1,0:T(8,128)(2,1)S(1)}, u32[]{:S(2)}, u32[]{:S(2)}) collective-permute-start(bf16[512,128]{1,0:T(8,128)(2,1)S(1)} %get-tuple-element.24.kvm), channel_id=1, source_target_pairs={{0,32},{16,48},{32,0},{48,16},{64,96},{80,112},{96,64},{112,80},{1... | collective-permute-start | bytes 393224 | tf_op jit(solution)/shard_map/ppermute | solution.py:268
  34.4 8.1 %collective-permute-start = (bf16[512,128]{1,0:T(8,128)(2,1)S(1)}, bf16[512,128]{1,0:T(8,128)(2,1)S(1)}, u32[]{:S(2)}, u32[]{:S(2)}) collective-permute-start(bf16[512,128]{1,0:T(8,128)(2,1)S(1)} %get-tuple-element.24.kvm), channel_id=1, source_target_pairs={{0,16},{16,0},{32,48},{48,32},{64,80},{80,64},{96,112},{112,96},{1... | collective-permute-start | bytes 393224 | tf_op jit(solution)/shard_map/ppermute | solution.py:268
  42.4 3.6 %collective-permute-start.2 = (bf16[512,128]{1,0:T(8,128)(2,1)S(1)}, bf16[512,128]{1,0:T(8,128)(2,1)S(1)}, u32[]{:S(2)}, u32[]{:S(2)}) collective-permute-start(bf16[512,128]{1,0:T(8,128)(2,1)S(1)} %collective-permute-done.1.m2), channel_id=1, source_target_pairs={{0,16},{16,0},{32,48},{48,32},{64,80},{80,64},{96,112},{112,96},{1... | collective-permute-start | bytes 393224 | tf_op jit(solution)/shard_map/ppermute | solution.py:268
  46.1 2.2 %collective-permute-start.3 = (bf16[8,128,128]{2,1,0:T(8,128)(2,1)S(1)}, bf16[8,128,128]{2,1,0:T(8,128)(2,1)S(1)}, u32[]{:S(2)}, u32[]{:S(2)}) collective-permute-start(bf16[8,128,128]{2,1,0:T(8,128)(2,1)S(1)} %all-to-all-done.1.same), channel_id=1, source_target_pairs={{0,16},{16,0},{32,48},{48,32},{64,80},{80,64},{96,112},{112,96},{1... | collective-permute-start | bytes 786440 | tf_op jit(solution)/shard_map/ppermute | solution.py:268

commit v4 on v3

--- a/solution.py
+++ b/solution.py
@@ -19,6 +19,9 @@
 NOTE = 16
 ROWS = 16
 MID_ROWS = 4
+ZS = ROWS // 2
+Z_FIRST = 5
+COL_FIRST = 15
 N_MID = SEG // R_MID
 N_LONG = SEG // R_LONG
 NEGATIVE = -1e30
@@ -61,6 +64,10 @@
     for copy in copies:
         copy.start()
     return copies
+
+
+def slot(col):
+    return (col - COL_FIRST) % HEADS
 
 
 def pack_kernel(
@@ -84,13 +91,17 @@
             cols = pl.ds(head // 2 * LANES, LANES)
             lanes = slice(head % 2 * HD, head % 2 * HD + HD)
             q = q_ref[:, cols][:, lanes]
-            out_ref[head, :BLOCK] = jnp.concatenate([k_ref[:, cols][:, lanes], v_ref[:, cols][:, lanes]], axis=1)
-            out_ref[head, BLOCK:PACKED] = jnp.concatenate([q[:HALF], q[HALF:]], axis=1)
+            out_ref[slot(head), :BLOCK] = jnp.concatenate([k_ref[:, cols][:, lanes], v_ref[:, cols][:, lanes]], axis=1)
+            out_ref[slot(head), BLOCK:PACKED] = jnp.concatenate([q[:HALF], q[HALF:]], axis=1)
             note = jnp.where(low_lanes(NOTE), mid_ref[head].astype(jnp.float32), long_ref[head].astype(jnp.float32))
-            out_ref[head, PACKED:] = note.astype(jnp.bfloat16)
-        done = pl.ds(i * heads, heads)
-        stores.append(pltpu.make_async_copy(out_ref.at[done], out_hbm.at[done], out_sems.at[i]))
-        stores[-1].start()
+            out_ref[slot(head), PACKED:] = note.astype(jnp.bfloat16)
+        slots = sorted(slot(head) for head in range(i * heads, i * heads + heads))
+        runs = [[at for at in slots if at <= slots[0] + heads], [at for at in slots if at > slots[0] + heads]]
+        for run in runs:
+            if run:
+                done = pl.ds(run[0], len(run))
+                stores.append(pltpu.make_async_copy(out_ref.at[done], out_hbm.at[done], out_sems.at[len(stores)]))
+                stores[-1].start()
     for copy in stores:
         copy.wait()
 
@@ -99,7 +110,7 @@
     at_ref[...] = got_ref[0, PACKED:].astype(jnp.float32)
     o_mid, o_long = own_offsets(at_ref)
     for src in range(HEADS):
-        wide[pl.ds(src * BLOCK, BLOCK), :] = got_ref[src, :BLOCK].astype(jnp.float32)
+        wide[pl.ds(src * BLOCK, BLOCK), :] = got_ref[slot(src), :BLOCK].astype(jnp.float32)
     far = wide[pl.ds(o_long, N_LONG, stride=R_LONG), :].astype(jnp.bfloat16)
     own_ref[...] = far
     for z in range(ROWS // 2):
@@ -148,7 +159,7 @@
 def short_kernel(at_ref, got_ref, kvm, own_ref, state, qm_ref, ql_ref, kv_buf, one_buf, wide):
     for src in range(HEADS):
         rows = pl.ds(src * BLOCK, BLOCK)
-        kv = got_ref[src, :BLOCK]
+        kv = got_ref[slot(src), :BLOCK]
         kv_buf[rows, :] = kv
         one_buf[rows, :] = with_ones(kv)
     step = 2 * BLOCK
@@ -158,7 +169,7 @@
     for i in range(SEG // step):
         parts = []
         for src in (2 * i, 2 * i + 1):
-            packed = got_ref[src, BLOCK:PACKED]
+            packed = got_ref[slot(src), BLOCK:PACKED]
             parts.append(jnp.where(low, packed, zero))
             parts.append(jnp.where(low, jnp.concatenate([packed[:, HD:], packed[:, :HD]], axis=1), zero))
         q = jnp.concatenate(parts, axis=0)
@@ -198,9 +209,10 @@
 
 
 def long_part(state, ql, o_long, row, its_core, ref):
-    every = ref[...].reshape(ROWS // 2 * N_LONG, LANES)
+    every = ref[...].reshape(ZS * N_LONG, LANES)
     s = scores_of(ql[...], every)
-    before = lax.broadcasted_iota(jnp.int32, s.shape, 1) < ((row + 1 - its_core) // 2) * N_LONG
+    z = (lax.broadcasted_iota(jnp.int32, s.shape, 1) // N_LONG + Z_FIRST) % ZS
+    before = 2 * z + its_core < row
     top, new = soft(jnp.where(before, s, NEGATIVE), with_ones(every))
     merge(state, pl.ds(o_long, N_LONG, stride=R_LONG), top, new)
 
@@ -268,7 +280,8 @@
     return lax.ppermute(x, "row", [(i, i ^ d) for i in range(ROWS)])
 
 
-CORES = [[2 * z + c for z in range(ROWS // 2)] for c in range(2)]
+CORES = [[2 * ((p + Z_FIRST) % ZS) + c for p in range(ZS)] for c in range(2)]
+COLS = [[(p + COL_FIRST) % HEADS for p in range(HEADS)]]
 bar = lax.optimization_barrier
 
 
@@ -283,12 +296,12 @@
         [HB] * 5,
         scratch=[pltpu.SMEM((HEADS,), s32)] * 2
         + [pltpu.VMEM((BLOCK, width), bf16)] * 3
-        + [pltpu.VMEM((HEADS, PACKED + NOTE, LANES), bf16), DMA((2,)), DMA((chunks, 3)), DMA((chunks,))],
+        + [pltpu.VMEM((HEADS, PACKED + NOTE, LANES), bf16), DMA((2,)), DMA((chunks, 3)), DMA((chunks + 1,))],
         moved=1 << 20,
         out_specs=HB,
         limit=VMEM_MOST,
     )(mid_offsets, long_offsets, queries, keys, values)
-    got = lax.all_to_all(sent, "col", 0, 0)
+    got = lax.all_to_all(sent, "col", 0, 0, axis_index_groups=COLS)
     kv_mid, own, at, far = call(
         select_kernel,
         (

time: 62.9 us -> 64 us (1.017)
  waiting for transfers between devices: 0.01 us -> 1.26 us
    all_to_all x1, blocking collectives: 10.8 us -> 12.9 us  [shards(): lax.all_to_all(back, 'col', 0, 0)]
    ppermute x4, starting transfers between devices: 7.28 us -> 5.23 us  [xor_rows(): return lax.ppermute(x, 'row', [(i, i ^ d) for i in range(ROWS)])]
    all_to_all x1, blocking collectives: 21.5 us -> 19.7 us  [shards(): got = lax.all_to_all(sent, 'col', 0, 0, axis_index_groups=COLS)]
    all_to_all x1, starting transfers between devices: 8.19 us -> 9.79 us  [shards(): same = lax.all_to_all(far, 'row', 0, 0, axis_index_groups=CORES)]
    ppermute x4, waiting for transfers between devices: 0.01 us -> 1.26 us  [xor_rows(): return lax.ppermute(x, 'row', [(i, i ^ d) for i in range(ROWS)])]
  transfers between devices with their start and end apart: 5 -> 5, of which waited for: 0 -> 2; matrix products, arithmetic and copies ran while one was open for 0% -> 0% of each run, Pallas kernels for 13% -> 13%
where the time goes in v4:
time: 64 us; the launch traced here: 63.5 us
  blocking collectives  32.6 us (51%)
  starting transfers between devices  15 us (23%)
  Pallas kernels  14.6 us (23%)
  waiting for transfers between devices  1.26 us (2%)
    all_to_all x1, blocking collectives, shards(): got = lax.all_to_all(sent, 'col', 0, 0, axis_index_groups=COLS)  19.7 us
    all_to_all x1, blocking collectives, shards(): lax.all_to_all(back, 'col', 0, 0)  12.9 us
    all_to_all x1, starting transfers between devices, shards(): same = lax.all_to_all(far, 'row', 0, 0, axis_index_groups=CORES)  9.79 us
    pallas_call x1, Pallas kernels, shards(): call(short_kernel, (shape(SEG, LANES, dtype=f32), shape(N_MID, LANES), sh...  5.37 us
    ppermute x4, starting transfers between devices, xor_rows(): return lax.ppermute(x, 'row', [(i, i ^ d) for i in range(ROWS)])  5.23 us
    pallas_call x1, Pallas kernels, shards(): call(pack_kernel, shape(HEADS, PACKED + NOTE, LANES), [HB] * 5, scratch=[...  2.25 us
    pallas_call x1, Pallas kernels, shards(): call(last_kernel, (shape(HEADS, HALF, LANES), shape(SEG, LANES, dtype=f32...  1.76 us
    pallas_call x1, Pallas kernels, shards(): call(project_kernel, shape(BLOCK, wide_out), [VM, VM, VM], scratch=[pltpu...  1.61 us
  transfers between devices with their start and end apart: 5, of which 2 were waited for; matrix products, arithmetic and copies ran while one was open for 0% of the time, Pallas kernels for 13%

profile of v4, /device:TPU:1, one launch (start us, length us, event | category | flops | bytes accessed | tf_op | source)
XLA Modules:
  0.0 63.5 jit_solution(15921422165531120561)
XLA Ops:
  0.0 2.2 %shard_map.64 = bf16[16,208,128]{2,1,0:T(8,128)(2,1)} custom-call(s32[16]{0:T(128)} %mid_hbm.1, s32[16]{0:T(128)} %long_hbm.1, bf16[128,1024]{1,0:T(8,128)(2,1)} %q_hbm.1, bf16[128,1024]{1,0:T(8,128)(2,1)} %k_hbm.1, bf16[128,1024]{1,0:T(8,128)(2,1)} %v_hbm.1), custom_call_target="tpu_custom_call" | custom-call | bytes 1048576 | tf_op jit(solution)/shard_map/pallas_call | solution.py:293
  2.3 19.7 %all_to_all.15.got_ref = bf16[16,208,128]{2,1,0:T(8,128)(2,1)S(1)} all-to-all(bf16[16,208,128]{2,1,0:T(8,128)(2,1)} %shard_map.64), channel_id=1, replica_groups={{15,0,1,2,3,4,5,6,7,8,9,10,11,12,13,14},{31,16,17,18,19,20,21,22,23,24,..., dimensions={0} | all-to-all | bytes 1703936 | tf_op jit(solution)/shard_map/all_to_all | solution.py:304
  21.9 1.0 %shard_map.65 = (bf16[512,128]{1,0:T(8,128)(2,1)S(1)}, bf16[128,128]{1,0:T(8,128)(2,1)S(1)}, f32[16,128]{1,0:T(8,128)S(1)}, bf16[8,128,128]{2,1,0:T(8,128)(2,1)}) custom-call(bf16[16,208,128]{2,1,0:T(8,128)(2,1)S(1)} %all_to_all.15.got_ref), custom_call_target="tpu_custom_call" | custom-call | bytes 1048576 | tf_op jit(solution)/shard_map/pallas_call | solution.py:305
  22.9 9.8 %all-to-all-start.1 = ((bf16[8,128,128]{2,1,0:T(8,128)(2,1)}), bf16[8,128,128]{2,1,0:T(8,128)(2,1)S(1)}, u32[]{:S(2)}, u32[]{:S(2)}) async-start(bf16[8,128,128]{2,1,0:T(8,128)(2,1)} %get-tuple-element.23), calls=%async_computation.1 | async-start | bytes 524288 | tf_op jit(solution)/shard_map/all_to_all | solution.py:319
  32.7 1.2 %collective-permute-start.1 = (bf16[512,128]{1,0:T(8,128)(2,1)S(1)}, bf16[512,128]{1,0:T(8,128)(2,1)S(1)}, u32[]{:S(2)}, u32[]{:S(2)}) collective-permute-start(bf16[512,128]{1,0:T(8,128)(2,1)S(1)} %get-tuple-element.24.kvm), channel_id=1, source_target_pairs={{0,32},{16,48},{32,0},{48,16},{64,96},{80,112},{96,64},{112,80},{1... | collective-permute-start | bytes 393224 | tf_op jit(solution)/shard_map/ppermute | solution.py:280
  33.9 2.3 %collective-permute-start = (bf16[512,128]{1,0:T(8,128)(2,1)S(1)}, bf16[512,128]{1,0:T(8,128)(2,1)S(1)}, u32[]{:S(2)}, u32[]{:S(2)}) collective-permute-start(bf16[512,128]{1,0:T(8,128)(2,1)S(1)} %get-tuple-element.24.kvm), channel_id=1, source_target_pairs={{0,16},{16,0},{32,48},{48,32},{64,80},{80,64},{96,112},{112,96},{1... | collective-permute-start | bytes 393224 | tf_op jit(solution)/shard_map/ppermute | solution.py:280
  36.2 5.4 %shard_map.66 = (f32[2048,128]{1,0:T(8,128)S(1)}, bf16[512,128]{1,0:T(8,128)(2,1)S(1)}, bf16[128,128]{1,0:T(8,128)(2,1)S(1)}) custom-call(f32[16,128]{1,0:T(8,128)S(1)} %get-tuple-element.22.at_ref, bf16[16,208,128]{2,1,0:T(8,128)(2,1)S(1)} %all_to_all.15.got_ref, bf16[512,128]{1,0:T(8,128)(2,1)S(1)} %get-tuple-element.24.kvm, ...), custom_call_target="tpu_custom_call" | custom-call | flops 2147483648 | bytes 3145728 | tf_op jit(solution)/shard_map/pallas_call | solution.py:320
  41.6 0.9 %collective-permute-done.1.m2 = bf16[512,128]{1,0:T(8,128)(2,1)S(1)} collective-permute-done((bf16[512,128]{1,0:T(8,128)(2,1)S(1)}, bf16[512,128]{1,0:T(8,128)(2,1)S(1)}, u32[]{:S(2)}, u32[]{:S(2)}) %collective-permute-start.1) | collective-permute-done | bytes 131104 | tf_op jit(solution)/shard_map/ppermute | solution.py:280
  42.5 0.0 collective-permute-done.m1
  42.6 1.6 %collective-permute-start.2 = (bf16[512,128]{1,0:T(8,128)(2,1)S(1)}, bf16[512,128]{1,0:T(8,128)(2,1)S(1)}, u32[]{:S(2)}, u32[]{:S(2)}) collective-permute-start(bf16[512,128]{1,0:T(8,128)(2,1)S(1)} %collective-permute-done.1.m2), channel_id=1, source_target_pairs={{0,16},{16,0},{32,48},{48,32},{64,80},{80,64},{96,112},{112,96},{1... | collective-permute-start | bytes 393224 | tf_op jit(solution)/shard_map/ppermute | solution.py:280
  44.2 1.4 %shard_map.67 = (f32[2048,128]{1,0:T(8,128)S(1)}, bf16[384,2048]{1,0:T(8,128)(2,1)S(1)}) custom-call(f32[16,128]{1,0:T(8,128)S(1)} %get-tuple-element.22.at_ref, f32[2048,128]{1,0:T(8,128)S(1)} %get-tuple-element.28.state_in, bf16[512,128]{1,0:T(8,128)(2,1)S(1)} %get-tuple-element.29.qm, ...), custom_call_target="tpu_custom_call", output_to_operand_aliasing={{0}: (1, {})} | custom-call | flops 536870912 | bytes 2097152 | tf_op jit(solution)/shard_map/pallas_call | solution.py:332
  45.6 0.0 collective-permute-done.2.m3
  45.6 0.0 all-to-all-done.1.same
  45.6 0.1 collective-permute-start.3
  45.7 1.2 %shard_map.68.state_in = f32[2048,128]{1,0:T(8,128)S(1)} custom-call(f32[16,128]{1,0:T(8,128)S(1)} %get-tuple-element.22.at_ref, f32[2048,128]{1,0:T(8,128)S(1)} %get-tuple-element.32.state_in, bf16[512,128]{1,0:T(8,128)(2,1)S(1)} %get-tuple-element.29.qm, bf16[512,128]{1,0:T(8,128)(2,1)S(1)} %collective-permute-done.2.m3, ...), custom_call_target="tpu_custom_call", output_to_operand_aliasing={{}: (1, {})} | custom-call | flops 536870912 | bytes 2097152 | tf_op jit(solution)/shard_map/pallas_call | solution.py:345
  46.9 0.3 collective-permute-done.3.other
  47.3 1.8 %shard_map.69 = (bf16[16,64,128]{2,1,0:T(8,128)(2,1)S(1)}, f32[2048,128]{1,0:T(8,128)S(1)}, bf16[640,2048]{1,0:T(8,128)(2,1)S(1)}) custom-call(f32[16,128]{1,0:T(8,128)S(1)} %get-tuple-element.22.at_ref, f32[2048,128]{1,0:T(8,128)S(1)} %shard_map.68.state_in, bf16[128,128]{1,0:T(8,128)(2,1)S(1)} %get-tuple-element.34.ql, ...), custom_call_target="tpu_custom_call", output_to_operand_aliasing={{1}: (1, {})} | custom-call | flops 134217728 | bytes 4194304 | tf_op jit(solution)/shard_map/pallas_call | solution.py:356
  49.0 12.9 %all_to_all.16.got_ref = bf16[16,64,128]{2,1,0:T(8,128)(2,1)S(1)} all-to-all(bf16[16,64,128]{2,1,0:T(8,128)(2,1)S(1)} %get-tuple-element.36), channel_id=1, replica_groups=mesh['row'=16,'col'=16] {'col'}, dimensions={0} | all-to-all | bytes 524288 | tf_op jit(solution)/shard_map/all_to_all | solution.py:379
  61.9 1.6 %shard_map.70 = bf16[128,2048]{1,0:T(8,128)(2,1)} custom-call(bf16[16,64,128]{2,1,0:T(8,128)(2,1)S(1)} %all_to_all.16.got_ref, bf16[384,2048]{1,0:T(8,128)(2,1)S(1)} %get-tuple-element.37.w0_ref, bf16[640,2048]{1,0:T(8,128)(2,1)S(1)} %get-tuple-element.38.w1_ref), custom_call_target="tpu_custom_call" | custom-call | flops 536870912 | bytes 4194304 | tf_op jit(solution)/shard_map/pallas_call | solution.py:367
Async XLA Ops:
  22.9 22.7 %all-to-all-start.1 = ((bf16[8,128,128]{2,1,0:T(8,128)(2,1)}), bf16[8,128,128]{2,1,0:T(8,128)(2,1)S(1)}, u32[]{:S(2)}, u32[]{:S(2)}) async-start(bf16[8,128,128]{2,1,0:T(8,128)(2,1)} %get-tuple-element.23), calls=%async_computation.1 | async-start | bytes 524288 | tf_op jit(solution)/shard_map/all_to_all | solution.py:319
  32.7 9.8 %collective-permute-start.1 = (bf16[512,128]{1,0:T(8,128)(2,1)S(1)}, bf16[512,128]{1,0:T(8,128)(2,1)S(1)}, u32[]{:S(2)}, u32[]{:S(2)}) collective-permute-start(bf16[512,128]{1,0:T(8,128)(2,1)S(1)} %get-tuple-element.24.kvm), channel_id=1, source_target_pairs={{0,32},{16,48},{32,0},{48,16},{64,96},{80,112},{96,64},{112,80},{1... | collective-permute-start | bytes 393224 | tf_op jit(solution)/shard_map/ppermute | solution.py:280
  33.9 8.7 %collective-permute-start = (bf16[512,128]{1,0:T(8,128)(2,1)S(1)}, bf16[512,128]{1,0:T(8,128)(2,1)S(1)}, u32[]{:S(2)}, u32[]{:S(2)}) collective-permute-start(bf16[512,128]{1,0:T(8,128)(2,1)S(1)} %get-tuple-element.24.kvm), channel_id=1, source_target_pairs={{0,16},{16,0},{32,48},{48,32},{64,80},{80,64},{96,112},{112,96},{1... | collective-permute-start | bytes 393224 | tf_op jit(solution)/shard_map/ppermute | solution.py:280
  42.6 3.1 %collective-permute-start.2 = (bf16[512,128]{1,0:T(8,128)(2,1)S(1)}, bf16[512,128]{1,0:T(8,128)(2,1)S(1)}, u32[]{:S(2)}, u32[]{:S(2)}) collective-permute-start(bf16[512,128]{1,0:T(8,128)(2,1)S(1)} %collective-permute-done.1.m2), channel_id=1, source_target_pairs={{0,16},{16,0},{32,48},{48,32},{64,80},{80,64},{96,112},{112,96},{1... | collective-permute-start | bytes 393224 | tf_op jit(solution)/shard_map/ppermute | solution.py:280
  45.6 1.6 %collective-permute-start.3 = (bf16[8,128,128]{2,1,0:T(8,128)(2,1)S(1)}, bf16[8,128,128]{2,1,0:T(8,128)(2,1)S(1)}, u32[]{:S(2)}, u32[]{:S(2)}) collective-permute-start(bf16[8,128,128]{2,1,0:T(8,128)(2,1)S(1)} %all-to-all-done.1.same), channel_id=1, source_target_pairs={{0,16},{16,0},{32,48},{48,32},{64,80},{80,64},{96,112},{112,96},{1... | collective-permute-start | bytes 786440 | tf_op jit(solution)/shard_map/ppermute | solution.py:280

commit v5 on v4

--- a/solution.py
+++ b/solution.py
@@ -250,7 +250,7 @@
         for half in range(2):
             a = state[pl.ds(src * BLOCK + half * HALF, HALF), :]
             done.append(a / a[:, :1])
-        out_ref[src] = jnp.where(low, pltpu.roll(done[0], HD, 1), done[1]).astype(jnp.bfloat16)
+        out_ref[slot(src)] = jnp.where(low, pltpu.roll(done[0], HD, 1), done[1]).astype(jnp.bfloat16)
     for load in loads:
         load.wait()
 
@@ -258,7 +258,7 @@
 def project_kernel(got_ref, w0_ref, w1_ref, out_hbm, combined, tiles, sems):
     count, _, tile = tiles.shape
     for pair in range(HEADS // 2):
-        a, b = got_ref[2 * pair], got_ref[2 * pair + 1]
+        a, b = got_ref[slot(2 * pair)], got_ref[slot(2 * pair + 1)]
         cols = pl.ds(pair * LANES, LANES)
         combined[:HALF, cols] = jnp.concatenate([a[:, :HD], b[:, :HD]], axis=1)
         combined[HALF:, cols] = jnp.concatenate([a[:, HD:], b[:, HD:]], axis=1)
@@ -376,7 +376,7 @@
         flops=2 * BLOCK * depth * wide_out,
         moved=2 * depth * wide_out,
         out_specs=HB,
-    )(lax.all_to_all(back, "col", 0, 0), weight0, weight)
+    )(lax.all_to_all(back, "col", 0, 0, axis_index_groups=COLS), weight0, weight)
 
 
 def solution(mesh):

time: 64 us -> 62.1 us (0.970)
  blocking collectives: 32.6 us -> 30.7 us
    all_to_all x1, blocking collectives: 12.9 us -> 11 us  [shards(): lax.all_to_all(back, 'col', 0, 0, axis_index_groups=COLS)]
where the time goes in v5:
time: 62.1 us; the launch traced here: 61.6 us
  blocking collectives  30.7 us (49%)
  starting transfers between devices  15 us (24%)
  Pallas kernels  14.6 us (24%)
  waiting for transfers between devices  1.26 us (2%)
    all_to_all x1, blocking collectives, shards(): got = lax.all_to_all(sent, 'col', 0, 0, axis_index_groups=COLS)  19.7 us
    all_to_all x1, blocking collectives, shards(): lax.all_to_all(back, 'col', 0, 0, axis_index_groups=COLS)  11 us
    all_to_all x1, starting transfers between devices, shards(): same = lax.all_to_all(far, 'row', 0, 0, axis_index_groups=CORES)  9.79 us
    pallas_call x1, Pallas kernels, shards(): call(short_kernel, (shape(SEG, LANES, dtype=f32), shape(N_MID, LANES), sh...  5.37 us
    ppermute x4, starting transfers between devices, xor_rows(): return lax.ppermute(x, 'row', [(i, i ^ d) for i in range(ROWS)])  5.23 us
    pallas_call x1, Pallas kernels, shards(): call(pack_kernel, shape(HEADS, PACKED + NOTE, LANES), [HB] * 5, scratch=[...  2.25 us
    pallas_call x1, Pallas kernels, shards(): call(last_kernel, (shape(HEADS, HALF, LANES), shape(SEG, LANES, dtype=f32...  1.76 us
    pallas_call x1, Pallas kernels, shards(): call(project_kernel, shape(BLOCK, wide_out), [VM, VM, VM], scratch=[pltpu...  1.6 us
  transfers between devices with their start and end apart: 5, of which 2 were waited for; matrix products, arithmetic and copies ran while one was open for 0% of the time, Pallas kernels for 13%

profile of v5, /device:TPU:1, one launch (start us, length us, event | category | flops | bytes accessed | tf_op | source)
XLA Modules:
  0.0 61.6 jit_solution(5455373991234993750)
XLA Ops:
  0.0 2.2 %shard_map.64 = bf16[16,208,128]{2,1,0:T(8,128)(2,1)} custom-call(s32[16]{0:T(128)} %mid_hbm.1, s32[16]{0:T(128)} %long_hbm.1, bf16[128,1024]{1,0:T(8,128)(2,1)} %q_hbm.1, bf16[128,1024]{1,0:T(8,128)(2,1)} %k_hbm.1, bf16[128,1024]{1,0:T(8,128)(2,1)} %v_hbm.1), custom_call_target="tpu_custom_call" | custom-call | bytes 1048576 | tf_op jit(solution)/shard_map/pallas_call | solution.py:293
  2.3 19.7 %all_to_all.15.got_ref = bf16[16,208,128]{2,1,0:T(8,128)(2,1)S(1)} all-to-all(bf16[16,208,128]{2,1,0:T(8,128)(2,1)} %shard_map.64), channel_id=1, replica_groups={{15,0,1,2,3,4,5,6,7,8,9,10,11,12,13,14},{31,16,17,18,19,20,21,22,23,24,..., dimensions={0} | all-to-all | bytes 1703936 | tf_op jit(solution)/shard_map/all_to_all | solution.py:304
  21.9 1.0 %shard_map.65 = (bf16[512,128]{1,0:T(8,128)(2,1)S(1)}, bf16[128,128]{1,0:T(8,128)(2,1)S(1)}, f32[16,128]{1,0:T(8,128)S(1)}, bf16[8,128,128]{2,1,0:T(8,128)(2,1)}) custom-call(bf16[16,208,128]{2,1,0:T(8,128)(2,1)S(1)} %all_to_all.15.got_ref), custom_call_target="tpu_custom_call" | custom-call | bytes 1048576 | tf_op jit(solution)/shard_map/pallas_call | solution.py:305
  22.9 9.8 %all-to-all-start.1 = ((bf16[8,128,128]{2,1,0:T(8,128)(2,1)}), bf16[8,128,128]{2,1,0:T(8,128)(2,1)S(1)}, u32[]{:S(2)}, u32[]{:S(2)}) async-start(bf16[8,128,128]{2,1,0:T(8,128)(2,1)} %get-tuple-element.23), calls=%async_computation.1 | async-start | bytes 524288 | tf_op jit(solution)/shard_map/all_to_all | solution.py:319
  32.7 1.2 %collective-permute-start.1 = (bf16[512,128]{1,0:T(8,128)(2,1)S(1)}, bf16[512,128]{1,0:T(8,128)(2,1)S(1)}, u32[]{:S(2)}, u32[]{:S(2)}) collective-permute-start(bf16[512,128]{1,0:T(8,128)(2,1)S(1)} %get-tuple-element.24.kvm), channel_id=1, source_target_pairs={{0,32},{16,48},{32,0},{48,16},{64,96},{80,112},{96,64},{112,80},{1... | collective-permute-start | bytes 393224 | tf_op jit(solution)/shard_map/ppermute | solution.py:280
  33.9 2.3 %collective-permute-start = (bf16[512,128]{1,0:T(8,128)(2,1)S(1)}, bf16[512,128]{1,0:T(8,128)(2,1)S(1)}, u32[]{:S(2)}, u32[]{:S(2)}) collective-permute-start(bf16[512,128]{1,0:T(8,128)(2,1)S(1)} %get-tuple-element.24.kvm), channel_id=1, source_target_pairs={{0,16},{16,0},{32,48},{48,32},{64,80},{80,64},{96,112},{112,96},{1... | collective-permute-start | bytes 393224 | tf_op jit(solution)/shard_map/ppermute | solution.py:280
  36.2 5.4 %shard_map.66 = (f32[2048,128]{1,0:T(8,128)S(1)}, bf16[512,128]{1,0:T(8,128)(2,1)S(1)}, bf16[128,128]{1,0:T(8,128)(2,1)S(1)}) custom-call(f32[16,128]{1,0:T(8,128)S(1)} %get-tuple-element.22.at_ref, bf16[16,208,128]{2,1,0:T(8,128)(2,1)S(1)} %all_to_all.15.got_ref, bf16[512,128]{1,0:T(8,128)(2,1)S(1)} %get-tuple-element.24.kvm, ...), custom_call_target="tpu_custom_call" | custom-call | flops 2147483648 | bytes 3145728 | tf_op jit(solution)/shard_map/pallas_call | solution.py:320
  41.6 0.9 %collective-permute-done.1.m2 = bf16[512,128]{1,0:T(8,128)(2,1)S(1)} collective-permute-done((bf16[512,128]{1,0:T(8,128)(2,1)S(1)}, bf16[512,128]{1,0:T(8,128)(2,1)S(1)}, u32[]{:S(2)}, u32[]{:S(2)}) %collective-permute-start.1) | collective-permute-done | bytes 131104 | tf_op jit(solution)/shard_map/ppermute | solution.py:280
  42.5 0.0 collective-permute-done.m1
  42.6 1.6 %collective-permute-start.2 = (bf16[512,128]{1,0:T(8,128)(2,1)S(1)}, bf16[512,128]{1,0:T(8,128)(2,1)S(1)}, u32[]{:S(2)}, u32[]{:S(2)}) collective-permute-start(bf16[512,128]{1,0:T(8,128)(2,1)S(1)} %collective-permute-done.1.m2), channel_id=1, source_target_pairs={{0,16},{16,0},{32,48},{48,32},{64,80},{80,64},{96,112},{112,96},{1... | collective-permute-start | bytes 393224 | tf_op jit(solution)/shard_map/ppermute | solution.py:280
  44.2 1.4 %shard_map.67 = (f32[2048,128]{1,0:T(8,128)S(1)}, bf16[384,2048]{1,0:T(8,128)(2,1)S(1)}) custom-call(f32[16,128]{1,0:T(8,128)S(1)} %get-tuple-element.22.at_ref, f32[2048,128]{1,0:T(8,128)S(1)} %get-tuple-element.28.state_in, bf16[512,128]{1,0:T(8,128)(2,1)S(1)} %get-tuple-element.29.qm, ...), custom_call_target="tpu_custom_call", output_to_operand_aliasing={{0}: (1, {})} | custom-call | flops 536870912 | bytes 2097152 | tf_op jit(solution)/shard_map/pallas_call | solution.py:332
  45.6 0.0 collective-permute-done.2.m3
  45.6 0.0 all-to-all-done.1.same
  45.6 0.1 collective-permute-start.3
  45.7 1.2 %shard_map.68.state_in = f32[2048,128]{1,0:T(8,128)S(1)} custom-call(f32[16,128]{1,0:T(8,128)S(1)} %get-tuple-element.22.at_ref, f32[2048,128]{1,0:T(8,128)S(1)} %get-tuple-element.32.state_in, bf16[512,128]{1,0:T(8,128)(2,1)S(1)} %get-tuple-element.29.qm, bf16[512,128]{1,0:T(8,128)(2,1)S(1)} %collective-permute-done.2.m3, ...), custom_call_target="tpu_custom_call", output_to_operand_aliasing={{}: (1, {})} | custom-call | flops 536870912 | bytes 2097152 | tf_op jit(solution)/shard_map/pallas_call | solution.py:345
  46.9 0.3 collective-permute-done.3.other
  47.3 1.8 %shard_map.69 = (bf16[16,64,128]{2,1,0:T(8,128)(2,1)S(1)}, f32[2048,128]{1,0:T(8,128)S(1)}, bf16[640,2048]{1,0:T(8,128)(2,1)S(1)}) custom-call(f32[16,128]{1,0:T(8,128)S(1)} %get-tuple-element.22.at_ref, f32[2048,128]{1,0:T(8,128)S(1)} %shard_map.68.state_in, bf16[128,128]{1,0:T(8,128)(2,1)S(1)} %get-tuple-element.34.ql, ...), custom_call_target="tpu_custom_call", output_to_operand_aliasing={{1}: (1, {})} | custom-call | flops 134217728 | bytes 4194304 | tf_op jit(solution)/shard_map/pallas_call | solution.py:356
  49.0 11.0 %all_to_all.16.got_ref = bf16[16,64,128]{2,1,0:T(8,128)(2,1)S(1)} all-to-all(bf16[16,64,128]{2,1,0:T(8,128)(2,1)S(1)} %get-tuple-element.36), channel_id=1, replica_groups={{15,0,1,2,3,4,5,6,7,8,9,10,11,12,13,14},{31,16,17,18,19,20,21,22,23,24,..., dimensions={0} | all-to-all | bytes 524288 | tf_op jit(solution)/shard_map/all_to_all | solution.py:379
  60.0 1.6 %shard_map.70 = bf16[128,2048]{1,0:T(8,128)(2,1)} custom-call(bf16[16,64,128]{2,1,0:T(8,128)(2,1)S(1)} %all_to_all.16.got_ref, bf16[384,2048]{1,0:T(8,128)(2,1)S(1)} %get-tuple-element.37.w0_ref, bf16[640,2048]{1,0:T(8,128)(2,1)S(1)} %get-tuple-element.38.w1_ref), custom_call_target="tpu_custom_call" | custom-call | flops 536870912 | bytes 4194304 | tf_op jit(solution)/shard_map/pallas_call | solution.py:367
Async XLA Ops:
  22.9 22.7 %all-to-all-start.1 = ((bf16[8,128,128]{2,1,0:T(8,128)(2,1)}), bf16[8,128,128]{2,1,0:T(8,128)(2,1)S(1)}, u32[]{:S(2)}, u32[]{:S(2)}) async-start(bf16[8,128,128]{2,1,0:T(8,128)(2,1)} %get-tuple-element.23), calls=%async_computation.1 | async-start | bytes 524288 | tf_op jit(solution)/shard_map/all_to_all | solution.py:319
  32.7 9.8 %collective-permute-start.1 = (bf16[512,128]{1,0:T(8,128)(2,1)S(1)}, bf16[512,128]{1,0:T(8,128)(2,1)S(1)}, u32[]{:S(2)}, u32[]{:S(2)}) collective-permute-start(bf16[512,128]{1,0:T(8,128)(2,1)S(1)} %get-tuple-element.24.kvm), channel_id=1, source_target_pairs={{0,32},{16,48},{32,0},{48,16},{64,96},{80,112},{96,64},{112,80},{1... | collective-permute-start | bytes 393224 | tf_op jit(solution)/shard_map/ppermute | solution.py:280
  33.9 8.7 %collective-permute-start = (bf16[512,128]{1,0:T(8,128)(2,1)S(1)}, bf16[512,128]{1,0:T(8,128)(2,1)S(1)}, u32[]{:S(2)}, u32[]{:S(2)}) collective-permute-start(bf16[512,128]{1,0:T(8,128)(2,1)S(1)} %get-tuple-element.24.kvm), channel_id=1, source_target_pairs={{0,16},{16,0},{32,48},{48,32},{64,80},{80,64},{96,112},{112,96},{1... | collective-permute-start | bytes 393224 | tf_op jit(solution)/shard_map/ppermute | solution.py:280
  42.6 3.1 %collective-permute-start.2 = (bf16[512,128]{1,0:T(8,128)(2,1)S(1)}, bf16[512,128]{1,0:T(8,128)(2,1)S(1)}, u32[]{:S(2)}, u32[]{:S(2)}) collective-permute-start(bf16[512,128]{1,0:T(8,128)(2,1)S(1)} %collective-permute-done.1.m2), channel_id=1, source_target_pairs={{0,16},{16,0},{32,48},{48,32},{64,80},{80,64},{96,112},{112,96},{1... | collective-permute-start | bytes 393224 | tf_op jit(solution)/shard_map/ppermute | solution.py:280
  45.6 1.6 %collective-permute-start.3 = (bf16[8,128,128]{2,1,0:T(8,128)(2,1)S(1)}, bf16[8,128,128]{2,1,0:T(8,128)(2,1)S(1)}, u32[]{:S(2)}, u32[]{:S(2)}) collective-permute-start(bf16[8,128,128]{2,1,0:T(8,128)(2,1)S(1)} %all-to-all-done.1.same), channel_id=1, source_target_pairs={{0,16},{16,0},{32,48},{48,32},{64,80},{80,64},{96,112},{112,96},{1... | collective-permute-start | bytes 786440 | tf_op jit(solution)/shard_map/ppermute | solution.py:280

commit v6 on v5

--- a/solution.py
+++ b/solution.py
@@ -334,7 +334,7 @@
         (shape(SEG, LANES, dtype=f32), shape(early, wide_out)),
         [VM] * 5 + [HB],
         scratch=[DMA((1,))],
-        flops=4 * N_MID * SEG * LANES,
+        flops=32 * 4 * N_MID * SEG * LANES,
         moved=2 << 20,
         exps=N_MID * SEG,
         aliases={1: 0},

time: 62.1 us -> 59.3 us (0.955)
  starting transfers between devices: 15 us -> 13.6 us
  waiting for transfers between devices: 1.26 us -> 0.01 us
    ppermute x4, waiting for transfers between devices: 1.26 us -> 0.01 us  [xor_rows(): return lax.ppermute(x, 'row', [(i, i ^ d) for i in range(ROWS)])]
    all_to_all x1, starting transfers between devices: 9.79 us -> 8.88 us  [shards(): same = lax.all_to_all(far, 'row', 0, 0, axis_index_groups=CORES)]
  transfers between devices with their start and end apart: 5 -> 5, of which waited for: 2 -> 0; matrix products, arithmetic and copies ran while one was open for 0% -> 0% of each run, Pallas kernels for 13% -> 14%
where the time goes in v6:
time: 59.3 us; the launch traced here: 58.9 us
  blocking collectives  30.7 us (52%)
  Pallas kernels  14.6 us (25%)
  starting transfers between devices  13.6 us (23%)
    all_to_all x1, blocking collectives, shards(): got = lax.all_to_all(sent, 'col', 0, 0, axis_index_groups=COLS)  19.7 us
    all_to_all x1, blocking collectives, shards(): lax.all_to_all(back, 'col', 0, 0, axis_index_groups=COLS)  11 us
    all_to_all x1, starting transfers between devices, shards(): same = lax.all_to_all(far, 'row', 0, 0, axis_index_groups=CORES)  8.88 us
    pallas_call x1, Pallas kernels, shards(): call(short_kernel, (shape(SEG, LANES, dtype=f32), shape(N_MID, LANES), sh...  5.36 us
    ppermute x4, starting transfers between devices, xor_rows(): return lax.ppermute(x, 'row', [(i, i ^ d) for i in range(ROWS)])  4.68 us
    pallas_call x1, Pallas kernels, shards(): call(pack_kernel, shape(HEADS, PACKED + NOTE, LANES), [HB] * 5, scratch=[...  2.25 us
    pallas_call x1, Pallas kernels, shards(): call(last_kernel, (shape(HEADS, HALF, LANES), shape(SEG, LANES, dtype=f32...  1.77 us
    pallas_call x1, Pallas kernels, shards(): call(project_kernel, shape(BLOCK, wide_out), [VM, VM, VM], scratch=[pltpu...  1.6 us
  transfers between devices with their start and end apart: 5, of which 0 were waited for; matrix products, arithmetic and copies ran while one was open for 0% of the time, Pallas kernels for 14%

profile of v6, /device:TPU:1, one launch (start us, length us, event | category | flops | bytes accessed | tf_op | source)
XLA Modules:
  0.0 58.9 jit_solution(4204473864903269872)
XLA Ops:
  0.0 2.2 %shard_map.64 = bf16[16,208,128]{2,1,0:T(8,128)(2,1)} custom-call(s32[16]{0:T(128)} %mid_hbm.1, s32[16]{0:T(128)} %long_hbm.1, bf16[128,1024]{1,0:T(8,128)(2,1)} %q_hbm.1, bf16[128,1024]{1,0:T(8,128)(2,1)} %k_hbm.1, bf16[128,1024]{1,0:T(8,128)(2,1)} %v_hbm.1), custom_call_target="tpu_custom_call" | custom-call | bytes 1048576 | tf_op jit(solution)/shard_map/pallas_call | solution.py:293
  2.3 19.7 %all_to_all.15.got_ref = bf16[16,208,128]{2,1,0:T(8,128)(2,1)S(1)} all-to-all(bf16[16,208,128]{2,1,0:T(8,128)(2,1)} %shard_map.64), channel_id=1, replica_groups={{15,0,1,2,3,4,5,6,7,8,9,10,11,12,13,14},{31,16,17,18,19,20,21,22,23,24,..., dimensions={0} | all-to-all | bytes 1703936 | tf_op jit(solution)/shard_map/all_to_all | solution.py:304
  21.9 1.0 %shard_map.65 = (bf16[512,128]{1,0:T(8,128)(2,1)S(1)}, bf16[128,128]{1,0:T(8,128)(2,1)S(1)}, f32[16,128]{1,0:T(8,128)S(1)}, bf16[8,128,128]{2,1,0:T(8,128)(2,1)}) custom-call(bf16[16,208,128]{2,1,0:T(8,128)(2,1)S(1)} %all_to_all.15.got_ref), custom_call_target="tpu_custom_call" | custom-call | bytes 1048576 | tf_op jit(solution)/shard_map/pallas_call | solution.py:305
  22.9 1.6 %collective-permute-start.1 = (bf16[512,128]{1,0:T(8,128)(2,1)S(1)}, bf16[512,128]{1,0:T(8,128)(2,1)S(1)}, u32[]{:S(2)}, u32[]{:S(2)}) collective-permute-start(bf16[512,128]{1,0:T(8,128)(2,1)S(1)} %get-tuple-element.24.kvm), channel_id=1, source_target_pairs={{0,32},{16,48},{32,0},{48,16},{64,96},{80,112},{96,64},{112,80},{1... | collective-permute-start | bytes 393224 | tf_op jit(solution)/shard_map/ppermute | solution.py:280
  24.6 2.0 %collective-permute-start = (bf16[512,128]{1,0:T(8,128)(2,1)S(1)}, bf16[512,128]{1,0:T(8,128)(2,1)S(1)}, u32[]{:S(2)}, u32[]{:S(2)}) collective-permute-start(bf16[512,128]{1,0:T(8,128)(2,1)S(1)} %get-tuple-element.24.kvm), channel_id=1, source_target_pairs={{0,16},{16,0},{32,48},{48,32},{64,80},{80,64},{96,112},{112,96},{1... | collective-permute-start | bytes 393224 | tf_op jit(solution)/shard_map/ppermute | solution.py:280
  26.6 8.9 %all-to-all-start.1 = ((bf16[8,128,128]{2,1,0:T(8,128)(2,1)}), bf16[8,128,128]{2,1,0:T(8,128)(2,1)S(1)}, u32[]{:S(2)}, u32[]{:S(2)}) async-start(bf16[8,128,128]{2,1,0:T(8,128)(2,1)} %get-tuple-element.23), calls=%async_computation.1 | async-start | bytes 524288 | tf_op jit(solution)/shard_map/all_to_all | solution.py:319
  35.5 5.4 %shard_map.66 = (f32[2048,128]{1,0:T(8,128)S(1)}, bf16[512,128]{1,0:T(8,128)(2,1)S(1)}, bf16[128,128]{1,0:T(8,128)(2,1)S(1)}) custom-call(f32[16,128]{1,0:T(8,128)S(1)} %get-tuple-element.22.at_ref, bf16[16,208,128]{2,1,0:T(8,128)(2,1)S(1)} %all_to_all.15.got_ref, bf16[512,128]{1,0:T(8,128)(2,1)S(1)} %get-tuple-element.24.kvm, ...), custom_call_target="tpu_custom_call" | custom-call | flops 2147483648 | bytes 3145728 | tf_op jit(solution)/shard_map/pallas_call | solution.py:320
  40.9 0.0 collective-permute-done.1.m2
  40.9 0.0 collective-permute-done.m1
  40.9 0.4 collective-permute-start.2
  41.3 1.4 %shard_map.67 = (f32[2048,128]{1,0:T(8,128)S(1)}, bf16[384,2048]{1,0:T(8,128)(2,1)S(1)}) custom-call(f32[16,128]{1,0:T(8,128)S(1)} %get-tuple-element.22.at_ref, f32[2048,128]{1,0:T(8,128)S(1)} %get-tuple-element.28.state_in, bf16[512,128]{1,0:T(8,128)(2,1)S(1)} %get-tuple-element.29.qm, ...), custom_call_target="tpu_custom_call", output_to_operand_aliasing={{0}: (1, {})} | custom-call | flops 17179869184 | bytes 2097152 | tf_op jit(solution)/shard_map/pallas_call | solution.py:332
  42.7 0.0 collective-permute-done.2.m3
  42.7 0.0 all-to-all-done.1.same
  42.7 0.6 %collective-permute-start.3 = (bf16[8,128,128]{2,1,0:T(8,128)(2,1)S(1)}, bf16[8,128,128]{2,1,0:T(8,128)(2,1)S(1)}, u32[]{:S(2)}, u32[]{:S(2)}) collective-permute-start(bf16[8,128,128]{2,1,0:T(8,128)(2,1)S(1)} %all-to-all-done.1.same), channel_id=1, source_target_pairs={{0,16},{16,0},{32,48},{48,32},{64,80},{80,64},{96,112},{112,96},{1... | collective-permute-start | bytes 786440 | tf_op jit(solution)/shard_map/ppermute | solution.py:280
  43.3 1.2 %shard_map.68.state_in = f32[2048,128]{1,0:T(8,128)S(1)} custom-call(f32[16,128]{1,0:T(8,128)S(1)} %get-tuple-element.22.at_ref, f32[2048,128]{1,0:T(8,128)S(1)} %get-tuple-element.32.state_in, bf16[512,128]{1,0:T(8,128)(2,1)S(1)} %get-tuple-element.29.qm, bf16[512,128]{1,0:T(8,128)(2,1)S(1)} %collective-permute-done.2.m3, ...), custom_call_target="tpu_custom_call", output_to_operand_aliasing={{}: (1, {})} | custom-call | flops 536870912 | bytes 2097152 | tf_op jit(solution)/shard_map/pallas_call | solution.py:345
  44.5 0.0 collective-permute-done.3.other
  44.6 1.8 %shard_map.69 = (bf16[16,64,128]{2,1,0:T(8,128)(2,1)S(1)}, f32[2048,128]{1,0:T(8,128)S(1)}, bf16[640,2048]{1,0:T(8,128)(2,1)S(1)}) custom-call(f32[16,128]{1,0:T(8,128)S(1)} %get-tuple-element.22.at_ref, f32[2048,128]{1,0:T(8,128)S(1)} %shard_map.68.state_in, bf16[128,128]{1,0:T(8,128)(2,1)S(1)} %get-tuple-element.34.ql, ...), custom_call_target="tpu_custom_call", output_to_operand_aliasing={{1}: (1, {})} | custom-call | flops 134217728 | bytes 4194304 | tf_op jit(solution)/shard_map/pallas_call | solution.py:356
  46.3 11.0 %all_to_all.16.got_ref = bf16[16,64,128]{2,1,0:T(8,128)(2,1)S(1)} all-to-all(bf16[16,64,128]{2,1,0:T(8,128)(2,1)S(1)} %get-tuple-element.36), channel_id=1, replica_groups={{15,0,1,2,3,4,5,6,7,8,9,10,11,12,13,14},{31,16,17,18,19,20,21,22,23,24,..., dimensions={0} | all-to-all | bytes 524288 | tf_op jit(solution)/shard_map/all_to_all | solution.py:379
  57.3 1.6 %shard_map.70 = bf16[128,2048]{1,0:T(8,128)(2,1)} custom-call(bf16[16,64,128]{2,1,0:T(8,128)(2,1)S(1)} %all_to_all.16.got_ref, bf16[384,2048]{1,0:T(8,128)(2,1)S(1)} %get-tuple-element.37.w0_ref, bf16[640,2048]{1,0:T(8,128)(2,1)S(1)} %get-tuple-element.38.w1_ref), custom_call_target="tpu_custom_call" | custom-call | flops 536870912 | bytes 4194304 | tf_op jit(solution)/shard_map/pallas_call | solution.py:367
Async XLA Ops:
  22.9 17.9 %collective-permute-start.1 = (bf16[512,128]{1,0:T(8,128)(2,1)S(1)}, bf16[512,128]{1,0:T(8,128)(2,1)S(1)}, u32[]{:S(2)}, u32[]{:S(2)}) collective-permute-start(bf16[512,128]{1,0:T(8,128)(2,1)S(1)} %get-tuple-element.24.kvm), channel_id=1, source_target_pairs={{0,32},{16,48},{32,0},{48,16},{64,96},{80,112},{96,64},{112,80},{1... | collective-permute-start | bytes 393224 | tf_op jit(solution)/shard_map/ppermute | solution.py:280
  24.6 16.3 %collective-permute-start = (bf16[512,128]{1,0:T(8,128)(2,1)S(1)}, bf16[512,128]{1,0:T(8,128)(2,1)S(1)}, u32[]{:S(2)}, u32[]{:S(2)}) collective-permute-start(bf16[512,128]{1,0:T(8,128)(2,1)S(1)} %get-tuple-element.24.kvm), channel_id=1, source_target_pairs={{0,16},{16,0},{32,48},{48,32},{64,80},{80,64},{96,112},{112,96},{1... | collective-permute-start | bytes 393224 | tf_op jit(solution)/shard_map/ppermute | solution.py:280
  26.6 16.1 %all-to-all-start.1 = ((bf16[8,128,128]{2,1,0:T(8,128)(2,1)}), bf16[8,128,128]{2,1,0:T(8,128)(2,1)S(1)}, u32[]{:S(2)}, u32[]{:S(2)}) async-start(bf16[8,128,128]{2,1,0:T(8,128)(2,1)} %get-tuple-element.23), calls=%async_computation.1 | async-start | bytes 524288 | tf_op jit(solution)/shard_map/all_to_all | solution.py:319
  40.9 1.8 %collective-permute-start.2 = (bf16[512,128]{1,0:T(8,128)(2,1)S(1)}, bf16[512,128]{1,0:T(8,128)(2,1)S(1)}, u32[]{:S(2)}, u32[]{:S(2)}) collective-permute-start(bf16[512,128]{1,0:T(8,128)(2,1)S(1)} %collective-permute-done.1.m2), channel_id=1, source_target_pairs={{0,16},{16,0},{32,48},{48,32},{64,80},{80,64},{96,112},{112,96},{1... | collective-permute-start | bytes 393224 | tf_op jit(solution)/shard_map/ppermute | solution.py:280
  42.7 1.8 %collective-permute-start.3 = (bf16[8,128,128]{2,1,0:T(8,128)(2,1)S(1)}, bf16[8,128,128]{2,1,0:T(8,128)(2,1)S(1)}, u32[]{:S(2)}, u32[]{:S(2)}) collective-permute-start(bf16[8,128,128]{2,1,0:T(8,128)(2,1)S(1)} %all-to-all-done.1.same), channel_id=1, source_target_pairs={{0,16},{16,0},{32,48},{48,32},{64,80},{80,64},{96,112},{112,96},{1... | collective-permute-start | bytes 786440 | tf_op jit(solution)/shard_map/ppermute | solution.py:280

commit v7 on v6

--- a/solution.py
+++ b/solution.py
@@ -20,7 +20,7 @@
 ROWS = 16
 MID_ROWS = 4
 ZS = ROWS // 2
-Z_FIRST = 5
+Z_FIRST = 6
 COL_FIRST = 15
 N_MID = SEG // R_MID
 N_LONG = SEG // R_LONG

time: 59.3 us -> 59.9 us (1.010)
    ppermute x4, starting transfers between devices: 4.68 us -> 5.7 us  [xor_rows(): return lax.ppermute(x, 'row', [(i, i ^ d) for i in range(ROWS)])]
  transfers between devices with their start and end apart: 5 -> 5, of which waited for: 0 -> 0; matrix products, arithmetic and copies ran while one was open for 0% -> 0% of each run, Pallas kernels for 14% -> 13%
where the time goes in v7:
time: 59.9 us; the launch traced here: 59.5 us
  blocking collectives  30.7 us (51%)
  Pallas kernels  14.6 us (24%)
  starting transfers between devices  14.1 us (24%)
    all_to_all x1, blocking collectives, shards(): got = lax.all_to_all(sent, 'col', 0, 0, axis_index_groups=COLS)  19.7 us
    all_to_all x1, blocking collectives, shards(): lax.all_to_all(back, 'col', 0, 0, axis_index_groups=COLS)  11 us
    all_to_all x1, starting transfers between devices, shards(): same = lax.all_to_all(far, 'row', 0, 0, axis_index_groups=CORES)  8.44 us
    ppermute x4, starting transfers between devices, xor_rows(): return lax.ppermute(x, 'row', [(i, i ^ d) for i in range(ROWS)])  5.7 us
    pallas_call x1, Pallas kernels, shards(): call(short_kernel, (shape(SEG, LANES, dtype=f32), shape(N_MID, LANES), sh...  5.37 us
    pallas_call x1, Pallas kernels, shards(): call(pack_kernel, shape(HEADS, PACKED + NOTE, LANES), [HB] * 5, scratch=[...  2.25 us
    pallas_call x1, Pallas kernels, shards(): call(last_kernel, (shape(HEADS, HALF, LANES), shape(SEG, LANES, dtype=f32...  1.77 us
    pallas_call x1, Pallas kernels, shards(): call(project_kernel, shape(BLOCK, wide_out), [VM, VM, VM], scratch=[pltpu...  1.6 us
  transfers between devices with their start and end apart: 5, of which 0 were waited for; matrix products, arithmetic and copies ran while one was open for 0% of the time, Pallas kernels for 13%

profile of v7, /device:TPU:1, one launch (start us, length us, event | category | flops | bytes accessed | tf_op | source)
XLA Modules:
  0.0 59.5 jit_solution(8533086488384799487)
XLA Ops:
  0.0 2.2 %shard_map.64 = bf16[16,208,128]{2,1,0:T(8,128)(2,1)} custom-call(s32[16]{0:T(128)} %mid_hbm.1, s32[16]{0:T(128)} %long_hbm.1, bf16[128,1024]{1,0:T(8,128)(2,1)} %q_hbm.1, bf16[128,1024]{1,0:T(8,128)(2,1)} %k_hbm.1, bf16[128,1024]{1,0:T(8,128)(2,1)} %v_hbm.1), custom_call_target="tpu_custom_call" | custom-call | bytes 1048576 | tf_op jit(solution)/shard_map/pallas_call | solution.py:293
  2.3 19.7 %all_to_all.15.got_ref = bf16[16,208,128]{2,1,0:T(8,128)(2,1)S(1)} all-to-all(bf16[16,208,128]{2,1,0:T(8,128)(2,1)} %shard_map.64), channel_id=1, replica_groups={{15,0,1,2,3,4,5,6,7,8,9,10,11,12,13,14},{31,16,17,18,19,20,21,22,23,24,..., dimensions={0} | all-to-all | bytes 1703936 | tf_op jit(solution)/shard_map/all_to_all | solution.py:304
  21.9 1.0 %shard_map.65 = (bf16[512,128]{1,0:T(8,128)(2,1)S(1)}, bf16[128,128]{1,0:T(8,128)(2,1)S(1)}, f32[16,128]{1,0:T(8,128)S(1)}, bf16[8,128,128]{2,1,0:T(8,128)(2,1)}) custom-call(bf16[16,208,128]{2,1,0:T(8,128)(2,1)S(1)} %all_to_all.15.got_ref), custom_call_target="tpu_custom_call" | custom-call | bytes 1048576 | tf_op jit(solution)/shard_map/pallas_call | solution.py:305
  22.9 1.6 %collective-permute-start.1 = (bf16[512,128]{1,0:T(8,128)(2,1)S(1)}, bf16[512,128]{1,0:T(8,128)(2,1)S(1)}, u32[]{:S(2)}, u32[]{:S(2)}) collective-permute-start(bf16[512,128]{1,0:T(8,128)(2,1)S(1)} %get-tuple-element.24.kvm), channel_id=1, source_target_pairs={{0,32},{16,48},{32,0},{48,16},{64,96},{80,112},{96,64},{112,80},{1... | collective-permute-start | bytes 393224 | tf_op jit(solution)/shard_map/ppermute | solution.py:280
  24.6 2.0 %collective-permute-start = (bf16[512,128]{1,0:T(8,128)(2,1)S(1)}, bf16[512,128]{1,0:T(8,128)(2,1)S(1)}, u32[]{:S(2)}, u32[]{:S(2)}) collective-permute-start(bf16[512,128]{1,0:T(8,128)(2,1)S(1)} %get-tuple-element.24.kvm), channel_id=1, source_target_pairs={{0,16},{16,0},{32,48},{48,32},{64,80},{80,64},{96,112},{112,96},{1... | collective-permute-start | bytes 393224 | tf_op jit(solution)/shard_map/ppermute | solution.py:280
  26.6 8.4 %all-to-all-start.1 = ((bf16[8,128,128]{2,1,0:T(8,128)(2,1)}), bf16[8,128,128]{2,1,0:T(8,128)(2,1)S(1)}, u32[]{:S(2)}, u32[]{:S(2)}) async-start(bf16[8,128,128]{2,1,0:T(8,128)(2,1)} %get-tuple-element.23), calls=%async_computation.1 | async-start | bytes 524288 | tf_op jit(solution)/shard_map/all_to_all | solution.py:319
  35.0 5.4 %shard_map.66 = (f32[2048,128]{1,0:T(8,128)S(1)}, bf16[512,128]{1,0:T(8,128)(2,1)S(1)}, bf16[128,128]{1,0:T(8,128)(2,1)S(1)}) custom-call(f32[16,128]{1,0:T(8,128)S(1)} %get-tuple-element.22.at_ref, bf16[16,208,128]{2,1,0:T(8,128)(2,1)S(1)} %all_to_all.15.got_ref, bf16[512,128]{1,0:T(8,128)(2,1)S(1)} %get-tuple-element.24.kvm, ...), custom_call_target="tpu_custom_call" | custom-call | flops 2147483648 | bytes 3145728 | tf_op jit(solution)/shard_map/pallas_call | solution.py:320
  40.4 0.0 collective-permute-done.1.m2
  40.4 0.0 collective-permute-done.m1
  40.4 0.4 collective-permute-start.2
  40.8 1.4 %shard_map.67 = (f32[2048,128]{1,0:T(8,128)S(1)}, bf16[384,2048]{1,0:T(8,128)(2,1)S(1)}) custom-call(f32[16,128]{1,0:T(8,128)S(1)} %get-tuple-element.22.at_ref, f32[2048,128]{1,0:T(8,128)S(1)} %get-tuple-element.28.state_in, bf16[512,128]{1,0:T(8,128)(2,1)S(1)} %get-tuple-element.29.qm, ...), custom_call_target="tpu_custom_call", output_to_operand_aliasing={{0}: (1, {})} | custom-call | flops 17179869184 | bytes 2097152 | tf_op jit(solution)/shard_map/pallas_call | solution.py:332
  42.3 0.0 collective-permute-done.2.m3
  42.3 0.0 all-to-all-done.1.same
  42.3 1.6 %collective-permute-start.3 = (bf16[8,128,128]{2,1,0:T(8,128)(2,1)S(1)}, bf16[8,128,128]{2,1,0:T(8,128)(2,1)S(1)}, u32[]{:S(2)}, u32[]{:S(2)}) collective-permute-start(bf16[8,128,128]{2,1,0:T(8,128)(2,1)S(1)} %all-to-all-done.1.same), channel_id=1, source_target_pairs={{0,16},{16,0},{32,48},{48,32},{64,80},{80,64},{96,112},{112,96},{1... | collective-permute-start | bytes 786440 | tf_op jit(solution)/shard_map/ppermute | solution.py:280
  43.9 1.2 %shard_map.68.state_in = f32[2048,128]{1,0:T(8,128)S(1)} custom-call(f32[16,128]{1,0:T(8,128)S(1)} %get-tuple-element.22.at_ref, f32[2048,128]{1,0:T(8,128)S(1)} %get-tuple-element.32.state_in, bf16[512,128]{1,0:T(8,128)(2,1)S(1)} %get-tuple-element.29.qm, bf16[512,128]{1,0:T(8,128)(2,1)S(1)} %collective-permute-done.2.m3, ...), custom_call_target="tpu_custom_call", output_to_operand_aliasing={{}: (1, {})} | custom-call | flops 536870912 | bytes 2097152 | tf_op jit(solution)/shard_map/pallas_call | solution.py:345
  45.1 0.0 collective-permute-done.3.other
  45.1 1.8 %shard_map.69 = (bf16[16,64,128]{2,1,0:T(8,128)(2,1)S(1)}, f32[2048,128]{1,0:T(8,128)S(1)}, bf16[640,2048]{1,0:T(8,128)(2,1)S(1)}) custom-call(f32[16,128]{1,0:T(8,128)S(1)} %get-tuple-element.22.at_ref, f32[2048,128]{1,0:T(8,128)S(1)} %shard_map.68.state_in, bf16[128,128]{1,0:T(8,128)(2,1)S(1)} %get-tuple-element.34.ql, ...), custom_call_target="tpu_custom_call", output_to_operand_aliasing={{1}: (1, {})} | custom-call | flops 134217728 | bytes 4194304 | tf_op jit(solution)/shard_map/pallas_call | solution.py:356
  46.9 11.0 %all_to_all.16.got_ref = bf16[16,64,128]{2,1,0:T(8,128)(2,1)S(1)} all-to-all(bf16[16,64,128]{2,1,0:T(8,128)(2,1)S(1)} %get-tuple-element.36), channel_id=1, replica_groups={{15,0,1,2,3,4,5,6,7,8,9,10,11,12,13,14},{31,16,17,18,19,20,21,22,23,24,..., dimensions={0} | all-to-all | bytes 524288 | tf_op jit(solution)/shard_map/all_to_all | solution.py:379
  57.9 1.6 %shard_map.70 = bf16[128,2048]{1,0:T(8,128)(2,1)} custom-call(bf16[16,64,128]{2,1,0:T(8,128)(2,1)S(1)} %all_to_all.16.got_ref, bf16[384,2048]{1,0:T(8,128)(2,1)S(1)} %get-tuple-element.37.w0_ref, bf16[640,2048]{1,0:T(8,128)(2,1)S(1)} %get-tuple-element.38.w1_ref), custom_call_target="tpu_custom_call" | custom-call | flops 536870912 | bytes 4194304 | tf_op jit(solution)/shard_map/pallas_call | solution.py:367
Async XLA Ops:
  22.9 17.5 %collective-permute-start.1 = (bf16[512,128]{1,0:T(8,128)(2,1)S(1)}, bf16[512,128]{1,0:T(8,128)(2,1)S(1)}, u32[]{:S(2)}, u32[]{:S(2)}) collective-permute-start(bf16[512,128]{1,0:T(8,128)(2,1)S(1)} %get-tuple-element.24.kvm), channel_id=1, source_target_pairs={{0,32},{16,48},{32,0},{48,16},{64,96},{80,112},{96,64},{112,80},{1... | collective-permute-start | bytes 393224 | tf_op jit(solution)/shard_map/ppermute | solution.py:280
  24.6 15.9 %collective-permute-start = (bf16[512,128]{1,0:T(8,128)(2,1)S(1)}, bf16[512,128]{1,0:T(8,128)(2,1)S(1)}, u32[]{:S(2)}, u32[]{:S(2)}) collective-permute-start(bf16[512,128]{1,0:T(8,128)(2,1)S(1)} %get-tuple-element.24.kvm), channel_id=1, source_target_pairs={{0,16},{16,0},{32,48},{48,32},{64,80},{80,64},{96,112},{112,96},{1... | collective-permute-start | bytes 393224 | tf_op jit(solution)/shard_map/ppermute | solution.py:280
  26.6 15.7 %all-to-all-start.1 = ((bf16[8,128,128]{2,1,0:T(8,128)(2,1)}), bf16[8,128,128]{2,1,0:T(8,128)(2,1)S(1)}, u32[]{:S(2)}, u32[]{:S(2)}) async-start(bf16[8,128,128]{2,1,0:T(8,128)(2,1)} %get-tuple-element.23), calls=%async_computation.1 | async-start | bytes 524288 | tf_op jit(solution)/shard_map/all_to_all | solution.py:319
  40.4 1.8 %collective-permute-start.2 = (bf16[512,128]{1,0:T(8,128)(2,1)S(1)}, bf16[512,128]{1,0:T(8,128)(2,1)S(1)}, u32[]{:S(2)}, u32[]{:S(2)}) collective-permute-start(bf16[512,128]{1,0:T(8,128)(2,1)S(1)} %collective-permute-done.1.m2), channel_id=1, source_target_pairs={{0,16},{16,0},{32,48},{48,32},{64,80},{80,64},{96,112},{112,96},{1... | collective-permute-start | bytes 393224 | tf_op jit(solution)/shard_map/ppermute | solution.py:280
  42.3 2.9 %collective-permute-start.3 = (bf16[8,128,128]{2,1,0:T(8,128)(2,1)S(1)}, bf16[8,128,128]{2,1,0:T(8,128)(2,1)S(1)}, u32[]{:S(2)}, u32[]{:S(2)}) collective-permute-start(bf16[8,128,128]{2,1,0:T(8,128)(2,1)S(1)} %all-to-all-done.1.same), channel_id=1, source_target_pairs={{0,16},{16,0},{32,48},{48,32},{64,80},{80,64},{96,112},{112,96},{1... | collective-permute-start | bytes 786440 | tf_op jit(solution)/shard_map/ppermute | solution.py:280

commit v8 on v6

--- a/solution.py
+++ b/solution.py
@@ -29,6 +29,8 @@
 VMEM_LIMIT = 20 * 1024 * 1024
 VMEM_LAST = 47 * 1024 * 1024
 VMEM_NEAR = 49 * 1024 * 1024
+VMEM_PROJECT = 48 * 1024 * 1024
+CUTS = (768, 1792)
 VMEM_MOST = 60 * 1024 * 1024
 
 VM = pl.BlockSpec(memory_space=pltpu.VMEM)
@@ -217,19 +219,17 @@
     merge(state, pl.ds(o_long, N_LONG, stride=R_LONG), top, new)
 
 
-def load_rows(src, first, dst, sems):
-    count = sems.shape[0]
-    part = dst.shape[0] // count
-    pairs = [(src.at[pl.ds(first + i * part, part)], dst.at[pl.ds(i * part, part)]) for i in range(count)]
-    return fetch(pairs, sems)
-
-
-def near_kernel(at_ref, state_in, qm, m1, m2, w_hbm, state, w_ref, w_sems):
-    loads = load_rows(w_hbm, 0, w_ref, w_sems)
+def load_cols(src, first, dst, sem):
+    load = pltpu.make_async_copy(src.at[:, pl.ds(first, dst.shape[1])], dst, sem)
+    load.start()
+    return load
+
+
+def near_kernel(at_ref, state_in, qm, m1, m2, w_hbm, state, w_ref, w_sem):
+    load = load_cols(w_hbm, 0, w_ref, w_sem)
     o_mid, _ = own_offsets(at_ref)
     mid_part(state, qm, o_mid, lax.rem(lax.axis_index("row"), MID_ROWS), ((1, m1), (2, m2)))
-    for load in loads:
-        load.wait()
+    load.wait()
 
 
 def same_kernel(at_ref, state_in, qm, m3, ql, same, state):
@@ -239,8 +239,8 @@
     long_part(state, ql, o_long, row, lax.rem(row, 2), same)
 
 
-def last_kernel(at_ref, state_in, ql, other, w_hbm, out_ref, state, w_ref, w_sems):
-    loads = load_rows(w_hbm, w_hbm.shape[0] - w_ref.shape[0], w_ref, w_sems)
+def last_kernel(at_ref, state_in, ql, other, w_hbm, out_ref, state, w_ref, w_sem):
+    load = load_cols(w_hbm, CUTS[0], w_ref, w_sem)
     _, o_long = own_offsets(at_ref)
     row = lax.axis_index("row")
     long_part(state, ql, o_long, row, 1 - lax.rem(row, 2), other)
@@ -251,26 +251,28 @@
             a = state[pl.ds(src * BLOCK + half * HALF, HALF), :]
             done.append(a / a[:, :1])
         out_ref[slot(src)] = jnp.where(low, pltpu.roll(done[0], HD, 1), done[1]).astype(jnp.bfloat16)
-    for load in loads:
-        load.wait()
-
-
-def project_kernel(got_ref, w0_ref, w1_ref, out_hbm, combined, tiles, sems):
-    count, _, tile = tiles.shape
+    load.wait()
+
+
+def project_kernel(got_ref, w0_ref, w1_ref, w_hbm, out_hbm, combined, rest, out_ref, w_sem, sems):
+    load = load_cols(w_hbm, CUTS[1], rest, w_sem)
     for pair in range(HEADS // 2):
         a, b = got_ref[slot(2 * pair)], got_ref[slot(2 * pair + 1)]
         cols = pl.ds(pair * LANES, LANES)
         combined[:HALF, cols] = jnp.concatenate([a[:, :HD], b[:, :HD]], axis=1)
         combined[HALF:, cols] = jnp.concatenate([a[:, HD:], b[:, HD:]], axis=1)
-    cut = w0_ref.shape[0]
-    first, second = combined[:, :cut], combined[:, cut:]
+    rows = combined[...]
+    tile = w1_ref.shape[1] // 2
+    pieces = [(0, w0_ref, 0, CUTS[0]), (CUTS[0], w1_ref, 0, tile), (CUTS[0] + tile, w1_ref, tile, tile)]
+    pieces.append((CUTS[1], rest, 0, rest.shape[1]))
     copies = []
-    for i in range(count):
-        cols = pl.ds(i * tile, tile)
-        total = jnp.dot(first, w0_ref[:, cols], preferred_element_type=jnp.float32)
-        total += jnp.dot(second, w1_ref[:, cols], preferred_element_type=jnp.float32)
-        tiles[i] = total.astype(jnp.bfloat16)
-        copies.append(pltpu.make_async_copy(tiles.at[i], out_hbm.at[:, cols], sems.at[i]))
+    for first, ref, at, width in pieces:
+        if ref is rest:
+            load.wait()
+        cols = pl.ds(first, width)
+        total = jnp.dot(rows, ref[:, pl.ds(at, width)], preferred_element_type=jnp.float32)
+        out_ref[:, cols] = total.astype(jnp.bfloat16)
+        copies.append(pltpu.make_async_copy(out_ref.at[:, cols], out_hbm.at[:, cols], sems.at[len(copies)]))
         copies[-1].start()
     for copy in copies:
         copy.wait()
@@ -328,12 +330,11 @@
     )(at, got, kv_mid, own)
     m1, m2, state = bar((m1, m2, state))
     m3 = xor_rows(m2, 1)
-    early = depth * 3 // 8
     state, weight0 = call(
         near_kernel,
-        (shape(SEG, LANES, dtype=f32), shape(early, wide_out)),
+        (shape(SEG, LANES, dtype=f32), shape(depth, CUTS[0])),
         [VM] * 5 + [HB],
-        scratch=[DMA((1,))],
+        scratch=[DMA],
         flops=32 * 4 * N_MID * SEG * LANES,
         moved=2 << 20,
         exps=N_MID * SEG,
@@ -351,13 +352,11 @@
         exps=N_MID * SEG,
         aliases={1: 0},
     )(at, state, q_mid, m3, q_long, same)
-    tile = 512
-    count = wide_out // tile
     back, _, weight = call(
         last_kernel,
-        (shape(HEADS, HALF, LANES), shape(SEG, LANES, dtype=f32), shape(depth - early, wide_out)),
+        (shape(HEADS, HALF, LANES), shape(SEG, LANES, dtype=f32), shape(depth, CUTS[1] - CUTS[0])),
         [VM] * 4 + [HB],
-        scratch=[DMA((1,))],
+        scratch=[DMA],
         flops=4 * N_LONG * SEG * LANES,
         moved=4 << 20,
         exps=N_LONG * SEG,
@@ -367,16 +366,19 @@
     return call(
         project_kernel,
         shape(BLOCK, wide_out),
-        [VM, VM, VM],
+        [VM, VM, VM, HB],
         scratch=[
             pltpu.VMEM((BLOCK, depth), bf16),
-            pltpu.VMEM((count, BLOCK, tile), bf16),
-            DMA((count,)),
+            pltpu.VMEM((depth, wide_out - CUTS[1]), bf16),
+            pltpu.VMEM((BLOCK, wide_out), bf16),
+            DMA,
+            DMA((4,)),
         ],
         flops=2 * BLOCK * depth * wide_out,
         moved=2 * depth * wide_out,
         out_specs=HB,
-    )(lax.all_to_all(back, "col", 0, 0, axis_index_groups=COLS), weight0, weight)
+        limit=VMEM_PROJECT,
+    )(lax.all_to_all(back, "col", 0, 0, axis_index_groups=COLS), weight0, weight, out_weight)
 
 
 def solution(mesh):

time: 59.3 us -> 60.7 us (1.024)
  Pallas kernels: 14.6 us -> 16 us
    pallas_call x2, Pallas kernels: 3.02 us -> 4.63 us  [the longest x1 2.68 us: shards(): call(project_kernel, shape(BLOCK, wide_out), [VM, VM, VM, HB], scratch=[p...]
  transfers between devices with their start and end apart: 5 -> 5, of which waited for: 0 -> 1; matrix products, arithmetic and copies ran while one was open for 0% -> 0% of each run, Pallas kernels for 14% -> 14%
where the time goes in v8:
time: 60.7 us; the launch traced here: 60.2 us
  blocking collectives  30.7 us (51%)
  Pallas kernels  16 us (26%)
  starting transfers between devices  13.3 us (22%)
    all_to_all x1, blocking collectives, shards(): got = lax.all_to_all(sent, 'col', 0, 0, axis_index_groups=COLS)  19.7 us
    all_to_all x1, blocking collectives, shards(): lax.all_to_all(back, 'col', 0, 0, axis_index_groups=COLS)  11.1 us
    all_to_all x1, starting transfers between devices, shards(): same = lax.all_to_all(far, 'row', 0, 0, axis_index_groups=CORES)  8.88 us
    pallas_call x1, Pallas kernels, shards(): call(short_kernel, (shape(SEG, LANES, dtype=f32), shape(N_MID, LANES), sh...  5.36 us
    ppermute x4, starting transfers between devices, xor_rows(): return lax.ppermute(x, 'row', [(i, i ^ d) for i in range(ROWS)])  4.37 us
    pallas_call x1, Pallas kernels, shards(): call(project_kernel, shape(BLOCK, wide_out), [VM, VM, VM, HB], scratch=[p...  2.68 us
    pallas_call x1, Pallas kernels, shards(): call(pack_kernel, shape(HEADS, PACKED + NOTE, LANES), [HB] * 5, scratch=[...  2.25 us
    pallas_call x1, Pallas kernels, shards(): call(near_kernel, (shape(SEG, LANES, dtype=f32), shape(depth, CUTS[0])),...  1.95 us
  transfers between devices with their start and end apart: 5, of which 1 were waited for; matrix products, arithmetic and copies ran while one was open for 0% of the time, Pallas kernels for 14%

profile of v8, /device:TPU:1, one launch (start us, length us, event | category | flops | bytes accessed | tf_op | source)
XLA Modules:
  0.0 60.2 jit_solution(16813322950093352208)
XLA Ops:
  0.0 2.2 %shard_map.64 = bf16[16,208,128]{2,1,0:T(8,128)(2,1)} custom-call(s32[16]{0:T(128)} %mid_hbm.1, s32[16]{0:T(128)} %long_hbm.1, bf16[128,1024]{1,0:T(8,128)(2,1)} %q_hbm.1, bf16[128,1024]{1,0:T(8,128)(2,1)} %k_hbm.1, bf16[128,1024]{1,0:T(8,128)(2,1)} %v_hbm.1), custom_call_target="tpu_custom_call" | custom-call | bytes 1048576 | tf_op jit(solution)/shard_map/pallas_call | solution.py:295
  2.3 19.7 %all_to_all.15.got_ref = bf16[16,208,128]{2,1,0:T(8,128)(2,1)S(1)} all-to-all(bf16[16,208,128]{2,1,0:T(8,128)(2,1)} %shard_map.64), channel_id=1, replica_groups={{15,0,1,2,3,4,5,6,7,8,9,10,11,12,13,14},{31,16,17,18,19,20,21,22,23,24,..., dimensions={0} | all-to-all | bytes 1703936 | tf_op jit(solution)/shard_map/all_to_all | solution.py:306
  21.9 1.0 %shard_map.65 = (bf16[512,128]{1,0:T(8,128)(2,1)S(1)}, bf16[128,128]{1,0:T(8,128)(2,1)S(1)}, f32[16,128]{1,0:T(8,128)S(1)}, bf16[8,128,128]{2,1,0:T(8,128)(2,1)}) custom-call(bf16[16,208,128]{2,1,0:T(8,128)(2,1)S(1)} %all_to_all.15.got_ref), custom_call_target="tpu_custom_call" | custom-call | bytes 1048576 | tf_op jit(solution)/shard_map/pallas_call | solution.py:307
  22.9 1.6 %collective-permute-start.1 = (bf16[512,128]{1,0:T(8,128)(2,1)S(1)}, bf16[512,128]{1,0:T(8,128)(2,1)S(1)}, u32[]{:S(2)}, u32[]{:S(2)}) collective-permute-start(bf16[512,128]{1,0:T(8,128)(2,1)S(1)} %get-tuple-element.24.kvm), channel_id=1, source_target_pairs={{0,32},{16,48},{32,0},{48,16},{64,96},{80,112},{96,64},{112,80},{1... | collective-permute-start | bytes 393224 | tf_op jit(solution)/shard_map/ppermute | solution.py:282
  24.6 2.0 %collective-permute-start = (bf16[512,128]{1,0:T(8,128)(2,1)S(1)}, bf16[512,128]{1,0:T(8,128)(2,1)S(1)}, u32[]{:S(2)}, u32[]{:S(2)}) collective-permute-start(bf16[512,128]{1,0:T(8,128)(2,1)S(1)} %get-tuple-element.24.kvm), channel_id=1, source_target_pairs={{0,16},{16,0},{32,48},{48,32},{64,80},{80,64},{96,112},{112,96},{1... | collective-permute-start | bytes 393224 | tf_op jit(solution)/shard_map/ppermute | solution.py:282
  26.6 8.9 %all-to-all-start.1 = ((bf16[8,128,128]{2,1,0:T(8,128)(2,1)}), bf16[8,128,128]{2,1,0:T(8,128)(2,1)S(1)}, u32[]{:S(2)}, u32[]{:S(2)}) async-start(bf16[8,128,128]{2,1,0:T(8,128)(2,1)} %get-tuple-element.23), calls=%async_computation.1 | async-start | bytes 524288 | tf_op jit(solution)/shard_map/all_to_all | solution.py:321
  35.5 5.4 %shard_map.66 = (f32[2048,128]{1,0:T(8,128)S(1)}, bf16[512,128]{1,0:T(8,128)(2,1)S(1)}, bf16[128,128]{1,0:T(8,128)(2,1)S(1)}) custom-call(f32[16,128]{1,0:T(8,128)S(1)} %get-tuple-element.22.at_ref, bf16[16,208,128]{2,1,0:T(8,128)(2,1)S(1)} %all_to_all.15.got_ref, bf16[512,128]{1,0:T(8,128)(2,1)S(1)} %get-tuple-element.24.kvm, ...), custom_call_target="tpu_custom_call" | custom-call | flops 2147483648 | bytes 3145728 | tf_op jit(solution)/shard_map/pallas_call | solution.py:322
  40.9 0.0 collective-permute-done.1.m2
  40.9 0.0 collective-permute-done.m1
  40.9 0.4 collective-permute-start.2
  41.3 1.9 %shard_map.67 = (f32[2048,128]{1,0:T(8,128)S(1)}, bf16[1024,768]{1,0:T(8,128)(2,1)S(1)}) custom-call(f32[16,128]{1,0:T(8,128)S(1)} %get-tuple-element.22.at_ref, f32[2048,128]{1,0:T(8,128)S(1)} %get-tuple-element.28.state_in, bf16[512,128]{1,0:T(8,128)(2,1)S(1)} %get-tuple-element.29.qm, ...), custom_call_target="tpu_custom_call", output_to_operand_aliasing={{0}: (1, {})} | custom-call | flops 17179869184 | bytes 2097152 | tf_op jit(solution)/shard_map/pallas_call | solution.py:333
  43.2 0.0 collective-permute-done.2.m3
  43.2 0.0 all-to-all-done.1.same
  43.2 0.3 collective-permute-start.3
  43.5 1.2 %shard_map.68.state_in = f32[2048,128]{1,0:T(8,128)S(1)} custom-call(f32[16,128]{1,0:T(8,128)S(1)} %get-tuple-element.22.at_ref, f32[2048,128]{1,0:T(8,128)S(1)} %get-tuple-element.32.state_in, bf16[512,128]{1,0:T(8,128)(2,1)S(1)} %get-tuple-element.29.qm, bf16[512,128]{1,0:T(8,128)(2,1)S(1)} %collective-permute-done.2.m3, ...), custom_call_target="tpu_custom_call", output_to_operand_aliasing={{}: (1, {})} | custom-call | flops 536870912 | bytes 2097152 | tf_op jit(solution)/shard_map/pallas_call | solution.py:346
  44.8 0.1 collective-permute-done.3.other
  44.9 1.6 %shard_map.69 = (bf16[16,64,128]{2,1,0:T(8,128)(2,1)S(1)}, f32[2048,128]{1,0:T(8,128)S(1)}, bf16[1024,1024]{1,0:T(8,128)(2,1)S(1)}) custom-call(f32[16,128]{1,0:T(8,128)S(1)} %get-tuple-element.22.at_ref, f32[2048,128]{1,0:T(8,128)S(1)} %shard_map.68.state_in, bf16[128,128]{1,0:T(8,128)(2,1)S(1)} %get-tuple-element.34.ql, ...), custom_call_target="tpu_custom_call", output_to_operand_aliasing={{1}: (1, {})} | custom-call | flops 134217728 | bytes 4194304 | tf_op jit(solution)/shard_map/pallas_call | solution.py:355
  46.5 11.1 %all_to_all.16.got_ref = bf16[16,64,128]{2,1,0:T(8,128)(2,1)S(1)} all-to-all(bf16[16,64,128]{2,1,0:T(8,128)(2,1)S(1)} %get-tuple-element.36), channel_id=1, replica_groups={{15,0,1,2,3,4,5,6,7,8,9,10,11,12,13,14},{31,16,17,18,19,20,21,22,23,24,..., dimensions={0} | all-to-all | bytes 524288 | tf_op jit(solution)/shard_map/all_to_all | solution.py:381
  57.5 2.7 %shard_map.70 = bf16[128,2048]{1,0:T(8,128)(2,1)} custom-call(bf16[16,64,128]{2,1,0:T(8,128)(2,1)S(1)} %all_to_all.16.got_ref, bf16[1024,768]{1,0:T(8,128)(2,1)S(1)} %get-tuple-element.37.w0_ref, bf16[1024,1024]{1,0:T(8,128)(2,1)S(1)} %get-tuple-element.38.w1_ref, bf16[1024,2048]{1,0:T(8,128)(2,1)} %w_hbm.5), custom_call_target="tpu_custom_call" | custom-call | flops 536870912 | bytes 4194304 | tf_op jit(solution)/shard_map/pallas_call | solution.py:366
Async XLA Ops:
  22.9 17.9 %collective-permute-start.1 = (bf16[512,128]{1,0:T(8,128)(2,1)S(1)}, bf16[512,128]{1,0:T(8,128)(2,1)S(1)}, u32[]{:S(2)}, u32[]{:S(2)}) collective-permute-start(bf16[512,128]{1,0:T(8,128)(2,1)S(1)} %get-tuple-element.24.kvm), channel_id=1, source_target_pairs={{0,32},{16,48},{32,0},{48,16},{64,96},{80,112},{96,64},{112,80},{1... | collective-permute-start | bytes 393224 | tf_op jit(solution)/shard_map/ppermute | solution.py:282
  24.6 16.3 %collective-permute-start = (bf16[512,128]{1,0:T(8,128)(2,1)S(1)}, bf16[512,128]{1,0:T(8,128)(2,1)S(1)}, u32[]{:S(2)}, u32[]{:S(2)}) collective-permute-start(bf16[512,128]{1,0:T(8,128)(2,1)S(1)} %get-tuple-element.24.kvm), channel_id=1, source_target_pairs={{0,16},{16,0},{32,48},{48,32},{64,80},{80,64},{96,112},{112,96},{1... | collective-permute-start | bytes 393224 | tf_op jit(solution)/shard_map/ppermute | solution.py:282
  26.6 16.6 %all-to-all-start.1 = ((bf16[8,128,128]{2,1,0:T(8,128)(2,1)}), bf16[8,128,128]{2,1,0:T(8,128)(2,1)S(1)}, u32[]{:S(2)}, u32[]{:S(2)}) async-start(bf16[8,128,128]{2,1,0:T(8,128)(2,1)} %get-tuple-element.23), calls=%async_computation.1 | async-start | bytes 524288 | tf_op jit(solution)/shard_map/all_to_all | solution.py:321
  40.9 2.3 %collective-permute-start.2 = (bf16[512,128]{1,0:T(8,128)(2,1)S(1)}, bf16[512,128]{1,0:T(8,128)(2,1)S(1)}, u32[]{:S(2)}, u32[]{:S(2)}) collective-permute-start(bf16[512,128]{1,0:T(8,128)(2,1)S(1)} %collective-permute-done.1.m2), channel_id=1, source_target_pairs={{0,16},{16,0},{32,48},{48,32},{64,80},{80,64},{96,112},{112,96},{1... | collective-permute-start | bytes 393224 | tf_op jit(solution)/shard_map/ppermute | solution.py:282
  43.2 1.6 %collective-permute-start.3 = (bf16[8,128,128]{2,1,0:T(8,128)(2,1)S(1)}, bf16[8,128,128]{2,1,0:T(8,128)(2,1)S(1)}, u32[]{:S(2)}, u32[]{:S(2)}) collective-permute-start(bf16[8,128,128]{2,1,0:T(8,128)(2,1)S(1)} %all-to-all-done.1.same), channel_id=1, source_target_pairs={{0,16},{16,0},{32,48},{48,32},{64,80},{80,64},{96,112},{112,96},{1... | collective-permute-start | bytes 786440 | tf_op jit(solution)/shard_map/ppermute | solution.py:282

commit v9 on v6

--- a/solution.py
+++ b/solution.py
@@ -162,13 +162,14 @@
         kv = got_ref[slot(src), :BLOCK]
         kv_buf[rows, :] = kv
         one_buf[rows, :] = with_ones(kv)
-    step = 2 * BLOCK
+    blocks = 4
+    step = blocks * BLOCK
     visible = causal(step, step, 0)
     low = low_lanes(HALF)
     zero = jnp.zeros((HALF, LANES), jnp.bfloat16)
     for i in range(SEG // step):
         parts = []
-        for src in (2 * i, 2 * i + 1):
+        for src in range(blocks * i, blocks * i + blocks):
             packed = got_ref[slot(src), BLOCK:PACKED]
             parts.append(jnp.where(low, packed, zero))
             parts.append(jnp.where(low, jnp.concatenate([packed[:, HD:], packed[:, :HD]], axis=1), zero))
@@ -184,6 +185,7 @@
     o_mid, o_long = own_offsets(at_ref)
     qm_ref[...] = wide[pl.ds(o_mid, N_MID, stride=R_MID), :].astype(jnp.bfloat16)
     ql_ref[...] = wide[pl.ds(o_long, N_LONG, stride=R_LONG), :].astype(jnp.bfloat16)
+    step = N_MID
     for i in range(N_MID // step):
         n = (i + 1) * step
         s = scores_of(qm_ref[pl.ds(i * step, step), :], kvm[:n])
@@ -196,7 +198,7 @@
 
 
 def mid_part(state, qm, o_mid, pos, parts):
-    step = 256
+    step = N_MID
     ones = jnp.concatenate([with_ones(ref[...]) for _, ref in parts], axis=0)
     for i in range(N_MID // step):
         q = qm[pl.ds(i * step, step), :]

time: 59.3 us -> 59.2 us (level)
  Pallas kernels: 14.6 us -> 13.7 us
  starting transfers between devices: 13.6 us -> 14.2 us
    ppermute x4, starting transfers between devices: 4.68 us -> 5.35 us  [xor_rows(): return lax.ppermute(x, 'row', [(i, i ^ d) for i in range(ROWS)])]
    pallas_call x1, Pallas kernels: 5.36 us -> 4.7 us  [shards(): call(short_kernel, (shape(SEG, LANES, dtype=f32), shape(N_MID, LANES), sh...]
  transfers between devices with their start and end apart: 5 -> 5, of which waited for: 0 -> 1; matrix products, arithmetic and copies ran while one was open for 0% -> 0% of each run, Pallas kernels for 14% -> 12%
where the time goes in v9:
time: 59.2 us; the launch traced here: 58.8 us
  blocking collectives  30.6 us (52%)
  starting transfers between devices  14.2 us (24%)
  Pallas kernels  13.7 us (23%)
    all_to_all x1, blocking collectives, shards(): got = lax.all_to_all(sent, 'col', 0, 0, axis_index_groups=COLS)  19.7 us
    all_to_all x1, blocking collectives, shards(): lax.all_to_all(back, 'col', 0, 0, axis_index_groups=COLS)  10.9 us
    all_to_all x1, starting transfers between devices, shards(): same = lax.all_to_all(far, 'row', 0, 0, axis_index_groups=CORES)  8.88 us
    ppermute x4, starting transfers between devices, xor_rows(): return lax.ppermute(x, 'row', [(i, i ^ d) for i in range(ROWS)])  5.35 us
    pallas_call x1, Pallas kernels, shards(): call(short_kernel, (shape(SEG, LANES, dtype=f32), shape(N_MID, LANES), sh...  4.7 us
    pallas_call x1, Pallas kernels, shards(): call(pack_kernel, shape(HEADS, PACKED + NOTE, LANES), [HB] * 5, scratch=[...  2.25 us
    pallas_call x1, Pallas kernels, shards(): call(last_kernel, (shape(HEADS, HALF, LANES), shape(SEG, LANES, dtype=f32...  1.76 us
    pallas_call x1, Pallas kernels, shards(): call(project_kernel, shape(BLOCK, wide_out), [VM, VM, VM], scratch=[pltpu...  1.6 us
  transfers between devices with their start and end apart: 5, of which 1 were waited for; matrix products, arithmetic and copies ran while one was open for 0% of the time, Pallas kernels for 12%

profile of v9, /device:TPU:1, one launch (start us, length us, event | category | flops | bytes accessed | tf_op | source)
XLA Modules:
  0.0 58.8 jit_solution(16295577212041010989)
XLA Ops:
  0.0 2.2 %shard_map.64 = bf16[16,208,128]{2,1,0:T(8,128)(2,1)} custom-call(s32[16]{0:T(128)} %mid_hbm.1, s32[16]{0:T(128)} %long_hbm.1, bf16[128,1024]{1,0:T(8,128)(2,1)} %q_hbm.1, bf16[128,1024]{1,0:T(8,128)(2,1)} %k_hbm.1, bf16[128,1024]{1,0:T(8,128)(2,1)} %v_hbm.1), custom_call_target="tpu_custom_call" | custom-call | bytes 1048576 | tf_op jit(solution)/shard_map/pallas_call | solution.py:295
  2.3 19.7 %all_to_all.15.got_ref = bf16[16,208,128]{2,1,0:T(8,128)(2,1)S(1)} all-to-all(bf16[16,208,128]{2,1,0:T(8,128)(2,1)} %shard_map.64), channel_id=1, replica_groups={{15,0,1,2,3,4,5,6,7,8,9,10,11,12,13,14},{31,16,17,18,19,20,21,22,23,24,..., dimensions={0} | all-to-all | bytes 1703936 | tf_op jit(solution)/shard_map/all_to_all | solution.py:306
  21.9 1.0 %shard_map.65 = (bf16[512,128]{1,0:T(8,128)(2,1)S(1)}, bf16[128,128]{1,0:T(8,128)(2,1)S(1)}, f32[16,128]{1,0:T(8,128)S(1)}, bf16[8,128,128]{2,1,0:T(8,128)(2,1)}) custom-call(bf16[16,208,128]{2,1,0:T(8,128)(2,1)S(1)} %all_to_all.15.got_ref), custom_call_target="tpu_custom_call" | custom-call | bytes 1048576 | tf_op jit(solution)/shard_map/pallas_call | solution.py:307
  22.9 1.6 %collective-permute-start.1 = (bf16[512,128]{1,0:T(8,128)(2,1)S(1)}, bf16[512,128]{1,0:T(8,128)(2,1)S(1)}, u32[]{:S(2)}, u32[]{:S(2)}) collective-permute-start(bf16[512,128]{1,0:T(8,128)(2,1)S(1)} %get-tuple-element.24.kvm), channel_id=1, source_target_pairs={{0,32},{16,48},{32,0},{48,16},{64,96},{80,112},{96,64},{112,80},{1... | collective-permute-start | bytes 393224 | tf_op jit(solution)/shard_map/ppermute | solution.py:282
  24.6 2.0 %collective-permute-start = (bf16[512,128]{1,0:T(8,128)(2,1)S(1)}, bf16[512,128]{1,0:T(8,128)(2,1)S(1)}, u32[]{:S(2)}, u32[]{:S(2)}) collective-permute-start(bf16[512,128]{1,0:T(8,128)(2,1)S(1)} %get-tuple-element.24.kvm), channel_id=1, source_target_pairs={{0,16},{16,0},{32,48},{48,32},{64,80},{80,64},{96,112},{112,96},{1... | collective-permute-start | bytes 393224 | tf_op jit(solution)/shard_map/ppermute | solution.py:282
  26.6 8.9 %all-to-all-start.1 = ((bf16[8,128,128]{2,1,0:T(8,128)(2,1)}), bf16[8,128,128]{2,1,0:T(8,128)(2,1)S(1)}, u32[]{:S(2)}, u32[]{:S(2)}) async-start(bf16[8,128,128]{2,1,0:T(8,128)(2,1)} %get-tuple-element.23), calls=%async_computation.1 | async-start | bytes 524288 | tf_op jit(solution)/shard_map/all_to_all | solution.py:321
  35.5 4.7 %shard_map.66 = (f32[2048,128]{1,0:T(8,128)S(1)}, bf16[512,128]{1,0:T(8,128)(2,1)S(1)}, bf16[128,128]{1,0:T(8,128)(2,1)S(1)}) custom-call(f32[16,128]{1,0:T(8,128)S(1)} %get-tuple-element.22.at_ref, bf16[16,208,128]{2,1,0:T(8,128)(2,1)S(1)} %all_to_all.15.got_ref, bf16[512,128]{1,0:T(8,128)(2,1)S(1)} %get-tuple-element.24.kvm, ...), custom_call_target="tpu_custom_call" | custom-call | flops 2147483648 | bytes 3145728 | tf_op jit(solution)/shard_map/pallas_call | solution.py:322
  40.2 0.0 collective-permute-done.1.m2
  40.2 0.0 collective-permute-done.m1
  40.2 0.4 collective-permute-start.2
  40.6 1.4 %shard_map.67 = (f32[2048,128]{1,0:T(8,128)S(1)}, bf16[384,2048]{1,0:T(8,128)(2,1)S(1)}) custom-call(f32[16,128]{1,0:T(8,128)S(1)} %get-tuple-element.22.at_ref, f32[2048,128]{1,0:T(8,128)S(1)} %get-tuple-element.28.state_in, bf16[512,128]{1,0:T(8,128)(2,1)S(1)} %get-tuple-element.29.qm, ...), custom_call_target="tpu_custom_call", output_to_operand_aliasing={{0}: (1, {})} | custom-call | flops 17179869184 | bytes 2097152 | tf_op jit(solution)/shard_map/pallas_call | solution.py:334
  42.0 0.0 collective-permute-done.2.m3
  42.0 0.0 all-to-all-done.1.same
  42.0 1.3 %collective-permute-start.3 = (bf16[8,128,128]{2,1,0:T(8,128)(2,1)S(1)}, bf16[8,128,128]{2,1,0:T(8,128)(2,1)S(1)}, u32[]{:S(2)}, u32[]{:S(2)}) collective-permute-start(bf16[8,128,128]{2,1,0:T(8,128)(2,1)S(1)} %all-to-all-done.1.same), channel_id=1, source_target_pairs={{0,16},{16,0},{32,48},{48,32},{64,80},{80,64},{96,112},{112,96},{1... | collective-permute-start | bytes 786440 | tf_op jit(solution)/shard_map/ppermute | solution.py:282
  43.3 1.0 %shard_map.68.state_in = f32[2048,128]{1,0:T(8,128)S(1)} custom-call(f32[16,128]{1,0:T(8,128)S(1)} %get-tuple-element.22.at_ref, f32[2048,128]{1,0:T(8,128)S(1)} %get-tuple-element.32.state_in, bf16[512,128]{1,0:T(8,128)(2,1)S(1)} %get-tuple-element.29.qm, bf16[512,128]{1,0:T(8,128)(2,1)S(1)} %collective-permute-done.2.m3, ...), custom_call_target="tpu_custom_call", output_to_operand_aliasing={{}: (1, {})} | custom-call | flops 536870912 | bytes 2097152 | tf_op jit(solution)/shard_map/pallas_call | solution.py:347
  44.3 0.2 collective-permute-done.3.other
  44.5 1.8 %shard_map.69 = (bf16[16,64,128]{2,1,0:T(8,128)(2,1)S(1)}, f32[2048,128]{1,0:T(8,128)S(1)}, bf16[640,2048]{1,0:T(8,128)(2,1)S(1)}) custom-call(f32[16,128]{1,0:T(8,128)S(1)} %get-tuple-element.22.at_ref, f32[2048,128]{1,0:T(8,128)S(1)} %shard_map.68.state_in, bf16[128,128]{1,0:T(8,128)(2,1)S(1)} %get-tuple-element.34.ql, ...), custom_call_target="tpu_custom_call", output_to_operand_aliasing={{1}: (1, {})} | custom-call | flops 134217728 | bytes 4194304 | tf_op jit(solution)/shard_map/pallas_call | solution.py:358
  46.3 10.9 %all_to_all.16.got_ref = bf16[16,64,128]{2,1,0:T(8,128)(2,1)S(1)} all-to-all(bf16[16,64,128]{2,1,0:T(8,128)(2,1)S(1)} %get-tuple-element.36), channel_id=1, replica_groups={{15,0,1,2,3,4,5,6,7,8,9,10,11,12,13,14},{31,16,17,18,19,20,21,22,23,24,..., dimensions={0} | all-to-all | bytes 524288 | tf_op jit(solution)/shard_map/all_to_all | solution.py:381
  57.2 1.6 %shard_map.70 = bf16[128,2048]{1,0:T(8,128)(2,1)} custom-call(bf16[16,64,128]{2,1,0:T(8,128)(2,1)S(1)} %all_to_all.16.got_ref, bf16[384,2048]{1,0:T(8,128)(2,1)S(1)} %get-tuple-element.37.w0_ref, bf16[640,2048]{1,0:T(8,128)(2,1)S(1)} %get-tuple-element.38.w1_ref), custom_call_target="tpu_custom_call" | custom-call | flops 536870912 | bytes 4194304 | tf_op jit(solution)/shard_map/pallas_call | solution.py:369
Async XLA Ops:
  22.9 17.3 %collective-permute-start.1 = (bf16[512,128]{1,0:T(8,128)(2,1)S(1)}, bf16[512,128]{1,0:T(8,128)(2,1)S(1)}, u32[]{:S(2)}, u32[]{:S(2)}) collective-permute-start(bf16[512,128]{1,0:T(8,128)(2,1)S(1)} %get-tuple-element.24.kvm), channel_id=1, source_target_pairs={{0,32},{16,48},{32,0},{48,16},{64,96},{80,112},{96,64},{112,80},{1... | collective-permute-start | bytes 393224 | tf_op jit(solution)/shard_map/ppermute | solution.py:282
  24.6 15.6 %collective-permute-start = (bf16[512,128]{1,0:T(8,128)(2,1)S(1)}, bf16[512,128]{1,0:T(8,128)(2,1)S(1)}, u32[]{:S(2)}, u32[]{:S(2)}) collective-permute-start(bf16[512,128]{1,0:T(8,128)(2,1)S(1)} %get-tuple-element.24.kvm), channel_id=1, source_target_pairs={{0,16},{16,0},{32,48},{48,32},{64,80},{80,64},{96,112},{112,96},{1... | collective-permute-start | bytes 393224 | tf_op jit(solution)/shard_map/ppermute | solution.py:282
  26.6 15.4 %all-to-all-start.1 = ((bf16[8,128,128]{2,1,0:T(8,128)(2,1)}), bf16[8,128,128]{2,1,0:T(8,128)(2,1)S(1)}, u32[]{:S(2)}, u32[]{:S(2)}) async-start(bf16[8,128,128]{2,1,0:T(8,128)(2,1)} %get-tuple-element.23), calls=%async_computation.1 | async-start | bytes 524288 | tf_op jit(solution)/shard_map/all_to_all | solution.py:321
  40.2 1.8 %collective-permute-start.2 = (bf16[512,128]{1,0:T(8,128)(2,1)S(1)}, bf16[512,128]{1,0:T(8,128)(2,1)S(1)}, u32[]{:S(2)}, u32[]{:S(2)}) collective-permute-start(bf16[512,128]{1,0:T(8,128)(2,1)S(1)} %collective-permute-done.1.m2), channel_id=1, source_target_pairs={{0,16},{16,0},{32,48},{48,32},{64,80},{80,64},{96,112},{112,96},{1... | collective-permute-start | bytes 393224 | tf_op jit(solution)/shard_map/ppermute | solution.py:282
  42.0 2.5 %collective-permute-start.3 = (bf16[8,128,128]{2,1,0:T(8,128)(2,1)S(1)}, bf16[8,128,128]{2,1,0:T(8,128)(2,1)S(1)}, u32[]{:S(2)}, u32[]{:S(2)}) collective-permute-start(bf16[8,128,128]{2,1,0:T(8,128)(2,1)S(1)} %all-to-all-done.1.same), channel_id=1, source_target_pairs={{0,16},{16,0},{32,48},{48,32},{64,80},{80,64},{96,112},{112,96},{1... | collective-permute-start | bytes 786440 | tf_op jit(solution)/shard_map/ppermute | solution.py:282

commit v10 on v9

--- a/solution.py
+++ b/solution.py
@@ -21,7 +21,7 @@
 MID_ROWS = 4
 ZS = ROWS // 2
 Z_FIRST = 5
-COL_FIRST = 15
+COL_FIRST = 14
 N_MID = SEG // R_MID
 N_LONG = SEG // R_LONG
 NEGATIVE = -1e30

time: 59.2 us -> 59.2 us (level)
  blocking collectives: 30.6 us -> 29.8 us
    all_to_all x1, blocking collectives: 19.7 us -> 19 us  [shards(): got = lax.all_to_all(sent, 'col', 0, 0, axis_index_groups=COLS)]
where the time goes in v10:
time: 59.2 us; the launch traced here: 58.3 us
  blocking collectives  29.8 us (50%)
  starting transfers between devices  14.6 us (25%)
  Pallas kernels  13.7 us (23%)
    all_to_all x1, blocking collectives, shards(): got = lax.all_to_all(sent, 'col', 0, 0, axis_index_groups=COLS)  19 us
    all_to_all x1, blocking collectives, shards(): lax.all_to_all(back, 'col', 0, 0, axis_index_groups=COLS)  10.8 us
    all_to_all x1, starting transfers between devices, shards(): same = lax.all_to_all(far, 'row', 0, 0, axis_index_groups=CORES)  8.88 us
    ppermute x4, starting transfers between devices, xor_rows(): return lax.ppermute(x, 'row', [(i, i ^ d) for i in range(ROWS)])  5.76 us
    pallas_call x1, Pallas kernels, shards(): call(short_kernel, (shape(SEG, LANES, dtype=f32), shape(N_MID, LANES), sh...  4.69 us
    pallas_call x1, Pallas kernels, shards(): call(pack_kernel, shape(HEADS, PACKED + NOTE, LANES), [HB] * 5, scratch=[...  2.26 us
    pallas_call x1, Pallas kernels, shards(): call(last_kernel, (shape(HEADS, HALF, LANES), shape(SEG, LANES, dtype=f32...  1.76 us
    pallas_call x1, Pallas kernels, shards(): call(project_kernel, shape(BLOCK, wide_out), [VM, VM, VM], scratch=[pltpu...  1.6 us
  transfers between devices with their start and end apart: 5, of which 1 were waited for; matrix products, arithmetic and copies ran while one was open for 0% of the time, Pallas kernels for 12%

profile of v10, /device:TPU:1, one launch (start us, length us, event | category | flops | bytes accessed | tf_op | source)
XLA Modules:
  0.0 58.3 jit_solution(835536475810723352)
XLA Ops:
  0.0 2.3 %shard_map.64 = bf16[16,208,128]{2,1,0:T(8,128)(2,1)} custom-call(s32[16]{0:T(128)} %mid_hbm.1, s32[16]{0:T(128)} %long_hbm.1, bf16[128,1024]{1,0:T(8,128)(2,1)} %q_hbm.1, bf16[128,1024]{1,0:T(8,128)(2,1)} %k_hbm.1, bf16[128,1024]{1,0:T(8,128)(2,1)} %v_hbm.1), custom_call_target="tpu_custom_call" | custom-call | bytes 1048576 | tf_op jit(solution)/shard_map/pallas_call | solution.py:295
  2.3 19.0 %all_to_all.15.got_ref = bf16[16,208,128]{2,1,0:T(8,128)(2,1)S(1)} all-to-all(bf16[16,208,128]{2,1,0:T(8,128)(2,1)} %shard_map.64), channel_id=1, replica_groups={{14,15,0,1,2,3,4,5,6,7,8,9,10,11,12,13},{30,31,16,17,18,19,20,21,22,23,..., dimensions={0} | all-to-all | bytes 1703936 | tf_op jit(solution)/shard_map/all_to_all | solution.py:306
  21.2 1.0 %shard_map.65 = (bf16[512,128]{1,0:T(8,128)(2,1)S(1)}, bf16[128,128]{1,0:T(8,128)(2,1)S(1)}, f32[16,128]{1,0:T(8,128)S(1)}, bf16[8,128,128]{2,1,0:T(8,128)(2,1)}) custom-call(bf16[16,208,128]{2,1,0:T(8,128)(2,1)S(1)} %all_to_all.15.got_ref), custom_call_target="tpu_custom_call" | custom-call | bytes 1048576 | tf_op jit(solution)/shard_map/pallas_call | solution.py:307
  22.2 1.6 %collective-permute-start.1 = (bf16[512,128]{1,0:T(8,128)(2,1)S(1)}, bf16[512,128]{1,0:T(8,128)(2,1)S(1)}, u32[]{:S(2)}, u32[]{:S(2)}) collective-permute-start(bf16[512,128]{1,0:T(8,128)(2,1)S(1)} %get-tuple-element.24.kvm), channel_id=1, source_target_pairs={{0,32},{16,48},{32,0},{48,16},{64,96},{80,112},{96,64},{112,80},{1... | collective-permute-start | bytes 393224 | tf_op jit(solution)/shard_map/ppermute | solution.py:282
  23.9 2.4 %collective-permute-start = (bf16[512,128]{1,0:T(8,128)(2,1)S(1)}, bf16[512,128]{1,0:T(8,128)(2,1)S(1)}, u32[]{:S(2)}, u32[]{:S(2)}) collective-permute-start(bf16[512,128]{1,0:T(8,128)(2,1)S(1)} %get-tuple-element.24.kvm), channel_id=1, source_target_pairs={{0,16},{16,0},{32,48},{48,32},{64,80},{80,64},{96,112},{112,96},{1... | collective-permute-start | bytes 393224 | tf_op jit(solution)/shard_map/ppermute | solution.py:282
  26.3 8.9 %all-to-all-start.1 = ((bf16[8,128,128]{2,1,0:T(8,128)(2,1)}), bf16[8,128,128]{2,1,0:T(8,128)(2,1)S(1)}, u32[]{:S(2)}, u32[]{:S(2)}) async-start(bf16[8,128,128]{2,1,0:T(8,128)(2,1)} %get-tuple-element.23), calls=%async_computation.1 | async-start | bytes 524288 | tf_op jit(solution)/shard_map/all_to_all | solution.py:321
  35.2 4.7 %shard_map.66 = (f32[2048,128]{1,0:T(8,128)S(1)}, bf16[512,128]{1,0:T(8,128)(2,1)S(1)}, bf16[128,128]{1,0:T(8,128)(2,1)S(1)}) custom-call(f32[16,128]{1,0:T(8,128)S(1)} %get-tuple-element.22.at_ref, bf16[16,208,128]{2,1,0:T(8,128)(2,1)S(1)} %all_to_all.15.got_ref, bf16[512,128]{1,0:T(8,128)(2,1)S(1)} %get-tuple-element.24.kvm, ...), custom_call_target="tpu_custom_call" | custom-call | flops 2147483648 | bytes 3145728 | tf_op jit(solution)/shard_map/pallas_call | solution.py:322
  39.9 0.0 collective-permute-done.1.m2
  39.9 0.0 collective-permute-done.m1
  39.9 0.4 collective-permute-start.2
  40.3 1.4 %shard_map.67 = (f32[2048,128]{1,0:T(8,128)S(1)}, bf16[384,2048]{1,0:T(8,128)(2,1)S(1)}) custom-call(f32[16,128]{1,0:T(8,128)S(1)} %get-tuple-element.22.at_ref, f32[2048,128]{1,0:T(8,128)S(1)} %get-tuple-element.28.state_in, bf16[512,128]{1,0:T(8,128)(2,1)S(1)} %get-tuple-element.29.qm, ...), custom_call_target="tpu_custom_call", output_to_operand_aliasing={{0}: (1, {})} | custom-call | flops 17179869184 | bytes 2097152 | tf_op jit(solution)/shard_map/pallas_call | solution.py:334
  41.7 0.0 collective-permute-done.2.m3
  41.7 0.0 all-to-all-done.1.same
  41.7 1.3 %collective-permute-start.3 = (bf16[8,128,128]{2,1,0:T(8,128)(2,1)S(1)}, bf16[8,128,128]{2,1,0:T(8,128)(2,1)S(1)}, u32[]{:S(2)}, u32[]{:S(2)}) collective-permute-start(bf16[8,128,128]{2,1,0:T(8,128)(2,1)S(1)} %all-to-all-done.1.same), channel_id=1, source_target_pairs={{0,16},{16,0},{32,48},{48,32},{64,80},{80,64},{96,112},{112,96},{1... | collective-permute-start | bytes 786440 | tf_op jit(solution)/shard_map/ppermute | solution.py:282
  43.0 1.0 %shard_map.68.state_in = f32[2048,128]{1,0:T(8,128)S(1)} custom-call(f32[16,128]{1,0:T(8,128)S(1)} %get-tuple-element.22.at_ref, f32[2048,128]{1,0:T(8,128)S(1)} %get-tuple-element.32.state_in, bf16[512,128]{1,0:T(8,128)(2,1)S(1)} %get-tuple-element.29.qm, bf16[512,128]{1,0:T(8,128)(2,1)S(1)} %collective-permute-done.2.m3, ...), custom_call_target="tpu_custom_call", output_to_operand_aliasing={{}: (1, {})} | custom-call | flops 536870912 | bytes 2097152 | tf_op jit(solution)/shard_map/pallas_call | solution.py:347
  44.0 0.2 collective-permute-done.3.other
  44.2 1.8 %shard_map.69 = (bf16[16,64,128]{2,1,0:T(8,128)(2,1)S(1)}, f32[2048,128]{1,0:T(8,128)S(1)}, bf16[640,2048]{1,0:T(8,128)(2,1)S(1)}) custom-call(f32[16,128]{1,0:T(8,128)S(1)} %get-tuple-element.22.at_ref, f32[2048,128]{1,0:T(8,128)S(1)} %shard_map.68.state_in, bf16[128,128]{1,0:T(8,128)(2,1)S(1)} %get-tuple-element.34.ql, ...), custom_call_target="tpu_custom_call", output_to_operand_aliasing={{1}: (1, {})} | custom-call | flops 134217728 | bytes 4194304 | tf_op jit(solution)/shard_map/pallas_call | solution.py:358
  46.0 10.8 %all_to_all.16.got_ref = bf16[16,64,128]{2,1,0:T(8,128)(2,1)S(1)} all-to-all(bf16[16,64,128]{2,1,0:T(8,128)(2,1)S(1)} %get-tuple-element.36), channel_id=1, replica_groups={{14,15,0,1,2,3,4,5,6,7,8,9,10,11,12,13},{30,31,16,17,18,19,20,21,22,23,..., dimensions={0} | all-to-all | bytes 524288 | tf_op jit(solution)/shard_map/all_to_all | solution.py:381
  56.8 1.6 %shard_map.70 = bf16[128,2048]{1,0:T(8,128)(2,1)} custom-call(bf16[16,64,128]{2,1,0:T(8,128)(2,1)S(1)} %all_to_all.16.got_ref, bf16[384,2048]{1,0:T(8,128)(2,1)S(1)} %get-tuple-element.37.w0_ref, bf16[640,2048]{1,0:T(8,128)(2,1)S(1)} %get-tuple-element.38.w1_ref), custom_call_target="tpu_custom_call" | custom-call | flops 536870912 | bytes 4194304 | tf_op jit(solution)/shard_map/pallas_call | solution.py:369
Async XLA Ops:
  22.2 17.7 %collective-permute-start.1 = (bf16[512,128]{1,0:T(8,128)(2,1)S(1)}, bf16[512,128]{1,0:T(8,128)(2,1)S(1)}, u32[]{:S(2)}, u32[]{:S(2)}) collective-permute-start(bf16[512,128]{1,0:T(8,128)(2,1)S(1)} %get-tuple-element.24.kvm), channel_id=1, source_target_pairs={{0,32},{16,48},{32,0},{48,16},{64,96},{80,112},{96,64},{112,80},{1... | collective-permute-start | bytes 393224 | tf_op jit(solution)/shard_map/ppermute | solution.py:282
  23.9 16.0 %collective-permute-start = (bf16[512,128]{1,0:T(8,128)(2,1)S(1)}, bf16[512,128]{1,0:T(8,128)(2,1)S(1)}, u32[]{:S(2)}, u32[]{:S(2)}) collective-permute-start(bf16[512,128]{1,0:T(8,128)(2,1)S(1)} %get-tuple-element.24.kvm), channel_id=1, source_target_pairs={{0,16},{16,0},{32,48},{48,32},{64,80},{80,64},{96,112},{112,96},{1... | collective-permute-start | bytes 393224 | tf_op jit(solution)/shard_map/ppermute | solution.py:282
  26.3 15.4 %all-to-all-start.1 = ((bf16[8,128,128]{2,1,0:T(8,128)(2,1)}), bf16[8,128,128]{2,1,0:T(8,128)(2,1)S(1)}, u32[]{:S(2)}, u32[]{:S(2)}) async-start(bf16[8,128,128]{2,1,0:T(8,128)(2,1)} %get-tuple-element.23), calls=%async_computation.1 | async-start | bytes 524288 | tf_op jit(solution)/shard_map/all_to_all | solution.py:321
  39.9 1.8 %collective-permute-start.2 = (bf16[512,128]{1,0:T(8,128)(2,1)S(1)}, bf16[512,128]{1,0:T(8,128)(2,1)S(1)}, u32[]{:S(2)}, u32[]{:S(2)}) collective-permute-start(bf16[512,128]{1,0:T(8,128)(2,1)S(1)} %collective-permute-done.1.m2), channel_id=1, source_target_pairs={{0,16},{16,0},{32,48},{48,32},{64,80},{80,64},{96,112},{112,96},{1... | collective-permute-start | bytes 393224 | tf_op jit(solution)/shard_map/ppermute | solution.py:282
  41.7 2.5 %collective-permute-start.3 = (bf16[8,128,128]{2,1,0:T(8,128)(2,1)S(1)}, bf16[8,128,128]{2,1,0:T(8,128)(2,1)S(1)}, u32[]{:S(2)}, u32[]{:S(2)}) collective-permute-start(bf16[8,128,128]{2,1,0:T(8,128)(2,1)S(1)} %all-to-all-done.1.same), channel_id=1, source_target_pairs={{0,16},{16,0},{32,48},{48,32},{64,80},{80,64},{96,112},{112,96},{1... | collective-permute-start | bytes 786440 | tf_op jit(solution)/shard_map/ppermute | solution.py:282
